TPU v7x, 32 devices: a whole 2x2x4 slice. The times are simulated.
32 devices in a mesh: space: 8 (over z, y), dp: 4 (over x, core).
Axes of the slice: x: 2, y: 2, z: 4, core: 2. Of those that a mesh axis runs over, the one named last changes fastest.
Arguments:
- activations: bfloat16 [4, 64, 16, 16, 256], P('dp', 'space'), may hold values from -6 to 6
- cotangent: bfloat16 [4, 64, 16, 16, 256], P('dp', 'space'), may hold values from -6 to 6
- tile_count: int32 [8], P('space'), may hold values from 1 to 8, as said below
- neighbours: int32 [64, 8], P('space'), may hold values from -1 to 63, as said below
- conv_kernel: float32 [7, 7, 256], replicated, may hold values from -0.875 to 0.875
- conv_bias: float32 [256], replicated, may hold values from -3 to 3
- norm_gain: float32 [256], replicated, may hold values from 0.1 to 1.9
- norm_bias: float32 [256], replicated, may hold values from -3 to 3
- proj_in: bfloat16 [256, 1024], replicated, may hold values from -0.375 to 0.375
- bias_in: float32 [1024], replicated, may hold values from -3 to 3
- proj_out: bfloat16 [1024, 256], replicated, may hold values from -0.1875 to 0.1875
- bias_out: float32 [256], replicated, may hold values from -3 to 3
- layer_scale: float32 [256], replicated, may hold values from 0.3 to 3
Outputs:
- out_tiles: bfloat16 [4, 64, 16, 16, 256], P('dp', 'space')
- grad_tiles: bfloat16 [4, 64, 16, 16, 256], P('dp', 'space')
- grad_conv_kernel: float32 [7, 7, 256], replicated
- grad_conv_bias: float32 [256], replicated
- grad_norm_gain: float32 [256], replicated
- grad_norm_bias: float32 [256], replicated
- grad_proj_in: float32 [256, 1024], replicated
- grad_bias_in: float32 [1024], replicated
- grad_proj_out: float32 [1024, 256], replicated
- grad_bias_out: float32 [256], replicated
- grad_layer_scale: float32 [256], replicated
Inputs may be any that keep to these rules, and one draw needn't show every extreme that they name: `tile_count`: each tile column has 1 to 8 ocean tiles; its live slots come first in its block, and the last tile column is all ocean. Tile rows do not wrap, tile columns wrap around. N and S neighbours are slots of the same column, W, NW, SW of the column to the left and E, NE, SE of the column to the right; a neighbour that is land or beyond the band, and every entry of a slot that is not live, is -1. Named slots are live.
All inputs are finite; a program needn't handle non-finite values.
Results may differ from a plain program's by a relative error of at most 0.0085.
Values may be sent and summed in bfloat16 or wider, within the bound.
No kernel may reach another device: no remote copies, remote signals or barrier semaphores. Data moves between devices by JAX's collectives and lax.ppermute only.
A program may use at most 64 MiB of HBM per device.

v0:
```python
import math

import jax
import jax.numpy as jnp
from jax import lax
from jax.sharding import PartitionSpec as P

ROOT_TWO_PI = 0.7978845608
CUBIC_TERM = 0.044715
EPSILON = 1e-06


def shifted(block, axis, distance):
    devices = range(lax.axis_size(axis))
    route = [((i - distance) % len(devices), i) for i in devices]
    return lax.ppermute(block, axis, route)


def gelu_pair(pre_act):
    tangent = jnp.tanh(ROOT_TWO_PI * (pre_act + CUBIC_TERM * pre_act * pre_act * pre_act))
    activated = 0.5 * pre_act * (1.0 + tangent)
    slope_vals = 0.5 * (1.0 + tangent) + 0.5 * pre_act * (1.0 - tangent * tangent) * ROOT_TWO_PI * (
        1.0 + 3.0 * CUBIC_TERM * pre_act * pre_act
    )
    return (activated, slope_vals)


def assemble(
    center, north_rows, south_rows, west_cols, east_cols, corner_nw, corner_ne, corner_sw, corner_se
):
    top_band = jnp.concatenate([corner_nw, north_rows, corner_ne], axis=-2)
    mid_band = jnp.concatenate([west_cols, center, east_cols], axis=-2)
    low_band = jnp.concatenate([corner_sw, south_rows, corner_se], axis=-2)
    return jnp.concatenate([top_band, mid_band, low_band], axis=-3)


def tile_pieces(own_tiles, west_data, east_data, ids_row, slot_count, center):
    present = ids_row >= 0
    local_ids = jnp.where(present, ids_row % slot_count, 0)
    tile_edge = own_tiles.shape[1]

    def masked_piece(piece, which):
        return jnp.where(present[which], piece, jnp.zeros_like(piece))

    return assemble(
        center,
        masked_piece(own_tiles[local_ids[0], tile_edge - 3 :], 0),
        masked_piece(own_tiles[local_ids[1], :3], 1),
        masked_piece(west_data[local_ids[2]], 2),
        masked_piece(east_data[local_ids[3]], 3),
        masked_piece(west_data[local_ids[4], tile_edge - 3 :], 4),
        masked_piece(east_data[local_ids[5], tile_edge - 3 :], 5),
        masked_piece(west_data[local_ids[6], :3], 6),
        masked_piece(east_data[local_ids[7], :3], 7),
    )


def depthwise(padded, kernel, col_start, col_stop):
    tile_edge = padded.shape[-3] - 6
    conv_sum = jnp.zeros(
        padded.shape[:-3] + (tile_edge, col_stop - col_start, padded.shape[-1]), jnp.float32
    )
    for row_tap in range(7):
        for col_tap in range(7):
            window = padded[
                ..., row_tap : row_tap + tile_edge, col_start + col_tap : col_stop + col_tap, :
            ]
            conv_sum = conv_sum + window.astype(jnp.float32) * kernel[row_tap, col_tap]
    return conv_sum


def transposed(padded, kernel):
    tile_edge = padded.shape[-3] - 6
    conv_sum = jnp.zeros(padded.shape[:-3] + (tile_edge, tile_edge, padded.shape[-1]), jnp.float32)
    for row_tap in range(7):
        for col_tap in range(7):
            window = padded[
                ..., 6 - row_tap : 6 - row_tap + tile_edge, 6 - col_tap : 6 - col_tap + tile_edge, :
            ]
            conv_sum = conv_sum + window.astype(jnp.float32) * kernel[row_tap, col_tap]
    return conv_sum


def kernel_grad(padded, grad_vals):
    tile_edge = padded.shape[-3] - 6
    axes_all = tuple(range(grad_vals.ndim - 1))
    tap_list = []
    for row_tap in range(7):
        for col_tap in range(7):
            window = padded[..., row_tap : row_tap + tile_edge, col_tap : col_tap + tile_edge, :]
            tap_list.append(jnp.sum(window.astype(jnp.float32) * grad_vals, axis=axes_all))
    return jnp.stack(tap_list).reshape(7, 7, -1)


def on_device(
    activations,
    cotangent,
    tile_count,
    neighbours,
    conv_kernel,
    conv_bias,
    norm_gain,
    norm_bias,
    proj_in,
    bias_in,
    proj_out,
    bias_out,
    layer_scale,
):
    my_tiles = activations[0]
    grads_out = cotangent[0]
    slot_count = my_tiles.shape[0]
    tile_edge = my_tiles.shape[1]
    channels = my_tiles.shape[3]
    hidden_width = proj_in.shape[1]
    live_count = tile_count[0]
    from_east = shifted(my_tiles[:, :, :3], "space", -1)
    from_west = shifted(my_tiles[:, :, tile_edge - 3 :], "space", 1)

    def zero_vec(length):
        return jnp.zeros((length,), jnp.float32)

    start_sums = (
        jnp.zeros((channels, hidden_width), jnp.float32),
        zero_vec(hidden_width),
        jnp.zeros((hidden_width, channels), jnp.float32),
        zero_vec(channels),
        zero_vec(channels),
        zero_vec(channels),
        zero_vec(channels),
        zero_vec(channels),
    )

    def forward_back(slot_pos, state_now):
        out_buf, conv_buf, grad_sums = state_now
        padded = tile_pieces(
            my_tiles, from_west, from_east, neighbours[slot_pos], slot_count, my_tiles[slot_pos]
        )
        conv_sum = depthwise(padded, conv_kernel, 0, tile_edge)
        conv_out = (conv_sum + conv_bias).reshape(-1, channels)
        centred = conv_out - jnp.mean(conv_out, axis=1, keepdims=True)
        inv_std = lax.rsqrt(jnp.mean(centred * centred, axis=1, keepdims=True) + EPSILON)
        normed = centred * inv_std
        unit_bf = (normed * norm_gain + norm_bias).astype(jnp.bfloat16)
        pre_act = jnp.dot(unit_bf, proj_in, preferred_element_type=jnp.float32) + bias_in
        activated, slope_vals = gelu_pair(pre_act)
        act_bf = activated.astype(jnp.bfloat16)
        branch = jnp.dot(act_bf, proj_out, preferred_element_type=jnp.float32) + bias_out
        x_rows = my_tiles[slot_pos].reshape(-1, channels).astype(jnp.float32)
        out_rows = (x_rows + layer_scale * branch).astype(jnp.bfloat16)
        dy_rows = grads_out[slot_pos].reshape(-1, channels).astype(jnp.float32)
        grad_branch = (dy_rows * layer_scale).astype(jnp.bfloat16)
        grad_wout = jnp.dot(act_bf.T, grad_branch, preferred_element_type=jnp.float32)
        grad_act = jnp.dot(grad_branch, proj_out.T, preferred_element_type=jnp.float32)
        grad_pre = (grad_act * slope_vals).astype(jnp.bfloat16)
        grad_win = jnp.dot(unit_bf.T, grad_pre, preferred_element_type=jnp.float32)
        grad_unit = jnp.dot(grad_pre, proj_in.T, preferred_element_type=jnp.float32)
        scaled = grad_unit * norm_gain
        grad_conv = inv_std * (
            scaled
            - jnp.mean(scaled, axis=1, keepdims=True)
            - normed * jnp.mean(scaled * normed, axis=1, keepdims=True)
        )
        grad_conv_bf = grad_conv.astype(jnp.bfloat16)
        new_sums = (
            grad_sums[0] + grad_win,
            grad_sums[1] + jnp.sum(grad_pre.astype(jnp.float32), axis=0),
            grad_sums[2] + grad_wout,
            grad_sums[3] + jnp.sum(grad_branch.astype(jnp.float32), axis=0),
            grad_sums[4] + jnp.sum(dy_rows * branch, axis=0),
            grad_sums[5] + jnp.sum(grad_unit * normed, axis=0),
            grad_sums[6] + jnp.sum(grad_unit, axis=0),
            grad_sums[7] + jnp.sum(grad_conv_bf.astype(jnp.float32), axis=0),
        )
        out_buf = lax.dynamic_update_index_in_dim(
            out_buf, out_rows.reshape(tile_edge, tile_edge, channels), slot_pos, 0
        )
        conv_buf = lax.dynamic_update_index_in_dim(
            conv_buf, grad_conv_bf.reshape(tile_edge, tile_edge, channels), slot_pos, 0
        )
        return (out_buf, conv_buf, new_sums)

    out_buf, conv_buf, dense_local = lax.fori_loop(
        0,
        live_count,
        forward_back,
        (jnp.zeros_like(my_tiles), jnp.zeros_like(my_tiles), start_sums),
    )
    grad_from_east = shifted(conv_buf[:, :, :3], "space", -1)
    grad_from_west = shifted(conv_buf[:, :, tile_edge - 3 :], "space", 1)

    def backward_input(slot_pos, state_now):
        grad_buf, kernel_sum = state_now
        ids_row = neighbours[slot_pos]
        grad_pad = tile_pieces(
            conv_buf, grad_from_west, grad_from_east, ids_row, slot_count, conv_buf[slot_pos]
        )
        act_pad = tile_pieces(
            my_tiles, from_west, from_east, ids_row, slot_count, my_tiles[slot_pos]
        )
        spread = transposed(grad_pad, conv_kernel)
        grad_tile = (grads_out[slot_pos].astype(jnp.float32) + spread).astype(jnp.bfloat16)
        kernel_sum = kernel_sum + kernel_grad(act_pad, conv_buf[slot_pos].astype(jnp.float32))
        grad_buf = lax.dynamic_update_index_in_dim(grad_buf, grad_tile, slot_pos, 0)
        return (grad_buf, kernel_sum)

    grad_buf, kernel_local = lax.fori_loop(
        0,
        live_count,
        backward_input,
        (jnp.zeros_like(my_tiles), jnp.zeros((7, 7, channels), jnp.float32)),
    )
    everything = lax.psum(
        (
            dense_local[0],
            dense_local[1],
            dense_local[2],
            dense_local[3],
            dense_local[4],
            dense_local[5],
            dense_local[6],
            dense_local[7],
            kernel_local,
        ),
        ("space", "dp"),
    )
    dense_total = everything[:8]
    kernel_total = everything[8]
    factor = 1.0 / math.sqrt(
        lax.axis_size("dp") * lax.axis_size("space") * slot_count * tile_edge * tile_edge
    )
    return (
        out_buf[None],
        grad_buf[None],
        kernel_total * factor,
        dense_total[7] * factor,
        dense_total[5] * factor,
        dense_total[6] * factor,
        dense_total[0] * factor,
        dense_total[1] * factor,
        dense_total[2] * factor,
        dense_total[3] * factor,
        dense_total[4] * factor,
    )


def solution(mesh):
    placed = (
        P("dp", "space", None, None, None),
        P("dp", "space", None, None, None),
        P("space"),
        P("space", None),
        P(),
        P(),
        P(),
        P(),
        P(),
        P(),
        P(),
        P(),
        P(),
    )
    return jax.shard_map(
        on_device,
        mesh=mesh,
        in_specs=placed,
        out_specs=(
            P("dp", "space", None, None, None),
            P("dp", "space", None, None, None),
            P(),
            P(),
            P(),
            P(),
            P(),
            P(),
            P(),
            P(),
            P(),
        ),
        check_vma=False,
    )
```

profile of v0, /device:TPU:0, one launch (start us, length us, event | category | flops | bytes accessed | tf_op | source)
XLA Modules:
  0.0 724.5 jit_solution(8779040167023094780)
XLA Ops:
  8.7 3.0 collective-permute-start
  11.7 3.1 collective-permute-start.1
  14.8 8.1 %collective-permute-done = bf16[8,16,3,256]{3,2,1,0:T(4,128)(2,1)S(1)} collective-permute-done((bf16[8,16,3,256]{3,2,1,0:T(4,128)(2,1)S(1)}, bf16[8,16,3,256]{3,2,1,0:T(4,128)(2,1)S(1)}, u32[]{:S(2)}, u32[]{:S(2)}) %collective-permute-start) | collective-permute-done | bytes 196640 | tf_op jit(solution)/shard_map/ppermute | solution.py:16
  28.8 243.3 %while.44 = (s32[]{:T(128)}, bf16[8,16,16,256]{3,2,1,0:T(8,128)(2,1)}, bf16[8,16,16,256]{3,2,1,0:T(8,128)(2,1)}, f32[256,1024]{1,0:T(8,128)S(1)}, f32[1024]{0:T(...) while((s32[]{:T(128)}, ...), condition=%wide.region_11.12_spmd, body=%wide.region_0.11_spmd.sunk | while | flops 832574848 | bytes 25334828 | solution.py:183
  39.6 2.5 select_bitcast_fusion.33
  80.1 2.5 select_bitcast_fusion.33
  120.5 2.5 select_bitcast_fusion.33
  160.9 2.5 select_bitcast_fusion.33
  201.4 2.5 select_bitcast_fusion.33
  241.8 2.5 select_bitcast_fusion.33
  274.6 84.0 %collective-permute-start.3 = (bf16[8,16,3,256]{3,2,1,0:T(4,128)(2,1)S(1)}, bf16[8,16,3,256]{3,2,1,0:T(4,128)(2,1)}, u32[]{:S(2)}, u32[]{:S(2)}) collective-permute-start(bf16[8,16,3,256]{3,2,1,0:T(4,128)(2,1)S(1)} %get-tuple-element.848), channel_id=1, source_target_pairs={{4,0},{8,4},{12,8},{16,12},{20,16},{24,20},{28,24},{0,28},{5,1},{9... | collective-permute-start | bytes 589832 | tf_op jit(solution)/shard_map/ppermute | solution.py:16
  358.6 5.3 collective-permute-done.2
  364.4 225.2 %while.45 = (s32[]{:T(128)}, bf16[8,16,16,256]{3,2,1,0:T(8,128)(2,1)S(1)}, f32[7,7,256]{2,1,0:T(8,128)S(1)}, s32[]{:T(128)}, bf16[8,16,16,256]{3,2,1,0:T(8,128)(...) while((s32[]{:T(128)}, ...), condition=%wide.region_62.63_spmd, body=%wide.region_12.62_spmd.sunk | while | flops 27273356 | bytes 14937817 | solution.py:207
  375.7 2.6 select_bitcast_fusion.39
  393.2 3.3 select_bitcast_fusion.35
  398.8 3.0 bitcast_dynamic-update-slice_fusion.2
  413.2 2.6 select_bitcast_fusion.39
  430.6 3.3 select_bitcast_fusion.35
  436.2 3.0 bitcast_dynamic-update-slice_fusion.2
  450.6 2.6 select_bitcast_fusion.39
  468.1 3.3 select_bitcast_fusion.35
  473.6 3.0 bitcast_dynamic-update-slice_fusion.2
  488.0 2.6 select_bitcast_fusion.39
  505.5 3.3 select_bitcast_fusion.35
  511.1 3.0 bitcast_dynamic-update-slice_fusion.2
  525.5 2.6 select_bitcast_fusion.39
  542.9 3.3 select_bitcast_fusion.35
  548.5 3.0 bitcast_dynamic-update-slice_fusion.2
  562.9 2.6 select_bitcast_fusion.39
  580.3 3.3 select_bitcast_fusion.35
  585.9 3.0 bitcast_dynamic-update-slice_fusion.2
  590.3 121.0 %all-reduce = (f32[7,7,256]{2,1,0:T(8,128)S(1)}, f32[256]{0:T(256)S(1)}, f32[256]{0:T(256)S(1)}, f32[256]{0:T(256)S(1)}, f32[1024]{0:T(1024)S(1)}, /*index=5*/f32[256]{0:T(256)S(1)}, f32[256]{0:T(256)S(1)}) all-reduce(f32[7,7,256]{2,1,0:T(8,128)S(1)} %get-tuple-element.510, ...), channel_id=1, replica_groups=mesh['space'=8,'dp'=4] {'space','dp'}, use_global_device_ids=true, to_apply=%region_63.64 | all-reduce | flops 14848 | bytes 118784 | tf_op jit(solution)/shard_map/psum | solution.py:213
  (497 shorter events, 220.1 us)
Async XLA Ops:
  7.2 707.0 %all-reduce.4.cloned.1.call-start = ((), (), s32[]{:S(2)}) async-start(), calls=%async_computation | async-start | bytes 4194304 | tf_op jit(solution)/shard_map/psum | solution.py:213
  8.7 14.2 %collective-permute-start = (bf16[8,16,3,256]{3,2,1,0:T(4,128)(2,1)S(1)}, bf16[8,16,3,256]{3,2,1,0:T(4,128)(2,1)S(1)}, u32[]{:S(2)}, u32[]{:S(2)}) collective-permute-start(bf16[8,16,3,256]{3,2,1,0:T(4,128)(2,1)S(1)} %get-tuple-element.851), channel_id=1, source_target_pairs={{28,0},{0,4},{4,8},{8,12},{12,16},{16,20},{20,24},{24,28},{29,1},{... | collective-permute-start | bytes 589832 | tf_op jit(solution)/shard_map/ppermute | solution.py:16
  11.7 13.4 %collective-permute-start.1 = (bf16[8,16,3,256]{3,2,1,0:T(4,128)(2,1)S(1)}, bf16[8,16,3,256]{3,2,1,0:T(4,128)(2,1)S(1)}, u32[]{:S(2)}, u32[]{:S(2)}) collective-permute-start(bf16[8,16,3,256]{3,2,1,0:T(4,128)(2,1)S(1)} %get-tuple-element.850), channel_id=1, source_target_pairs={{4,0},{8,4},{12,8},{16,12},{20,16},{24,20},{28,24},{0,28},{5,1},{9... | collective-permute-start | bytes 589832 | tf_op jit(solution)/shard_map/ppermute | solution.py:16
  27.3 1.3 copy-start.2
  27.3 1.3 copy-start.3
  27.4 1.2 copy-start.6
  28.0 0.7 copy-start.7
  57.7 0.7 copy-start.15
  58.5 1.3 copy-start.17
  58.8 1.0 copy-start.18
  98.1 0.7 copy-start.15
  98.9 1.3 copy-start.17
  99.3 1.0 copy-start.18
  138.5 0.7 copy-start.15
  139.4 1.3 copy-start.17
  139.7 1.0 copy-start.18
  179.0 0.7 copy-start.15
  179.8 1.3 copy-start.17
  180.1 1.0 copy-start.18
  219.4 0.7 copy-start.15
  220.3 1.3 copy-start.17
  220.6 1.0 copy-start.18
  260.7 1.3 copy-start.17
  261.0 1.0 copy-start.18
  272.0 86.6 %copy-start = (f32[1024,256]{1,0:T(8,128)}, f32[1024,256]{1,0:T(8,128)S(1)}, u32[]{:S(2)}) copy-start(f32[1024,256]{1,0:T(8,128)S(1)} %get-tuple-element.516) | copy-start | bytes 3145732
  272.1 86.5 %copy-start.1 = (f32[256,1024]{1,0:T(8,128)}, f32[256,1024]{1,0:T(8,128)S(1)}, u32[]{:S(2)}) copy-start(f32[256,1024]{1,0:T(8,128)S(1)} %get-tuple-element.514) | copy-start | bytes 3145732
  274.3 89.7 %collective-permute-start.2 = (bf16[8,16,3,256]{3,2,1,0:T(4,128)(2,1)S(1)}, bf16[8,16,3,256]{3,2,1,0:T(4,128)(2,1)S(1)}, u32[]{:S(2)}, u32[]{:S(2)}) collective-permute-start(bf16[8,16,3,256]{3,2,1,0:T(4,128)(2,1)S(1)} %get-tuple-element.849), channel_id=1, source_target_pairs={{28,0},{0,4},{4,8},{8,12},{12,16},{16,20},{20,24},{24,28},{29,1},{... | collective-permute-start | bytes 589832 | tf_op jit(solution)/shard_map/ppermute | solution.py:16
  274.6 89.6 %collective-permute-start.3 = (bf16[8,16,3,256]{3,2,1,0:T(4,128)(2,1)S(1)}, bf16[8,16,3,256]{3,2,1,0:T(4,128)(2,1)}, u32[]{:S(2)}, u32[]{:S(2)}) collective-permute-start(bf16[8,16,3,256]{3,2,1,0:T(4,128)(2,1)S(1)} %get-tuple-element.848), channel_id=1, source_target_pairs={{4,0},{8,4},{12,8},{16,12},{20,16},{24,20},{28,24},{0,28},{5,1},{9... | collective-permute-start | bytes 589832 | tf_op jit(solution)/shard_map/ppermute | solution.py:16
  364.4 225.2 %copy-start.13 = (f32[256]{0:T(256)S(1)}, f32[256]{0:T(256)}, u32[]{:S(2)}) copy-start(f32[256]{0:T(256)} %get-tuple-element.511) | copy-start | bytes 3076
  589.6 127.0 %copy-start.5 = (bf16[8,16,16,256]{3,2,1,0:T(8,128)(2,1)}, bf16[8,16,16,256]{3,2,1,0:T(8,128)(2,1)S(1)}, u32[]{:S(2)}) copy-start(bf16[8,16,16,256]{3,2,1,0:T(8,128)(2,1)S(1)} %get-tuple-element.509) | copy-start | bytes 3145732
  589.6 0.7 copy-start.10
  714.2 2.4 copy-start.4
  (37 other events, 23.8 us)
Sparse Core Ops, SparseCore 0:
  358.8 133.3 all-reduce.3
where the time goes:
time: 735 us; the launch traced here: 725 us
  loops' own time  196 us (27%)
  other arithmetic  185 us (25%)
  blocking collectives  121 us (16%)
  starting transfers between devices  90.5 us (12%)
  local copies, waits for them, and re-layouts  78.2 us (11%)
  matrix products  23.8 us (3%)
  waiting for transfers between devices  15.9 us (2%)
  between operations  14.2 us (2%)
    psum x1, blocking collectives, on_device(): lax.psum((dense_local[0], dense_local[1], dense_local[2], dense_local[3],...  121 us
    select_n x48, other arithmetic, masked_piece(): return jnp.where(present[which], piece, jnp.zeros_like(piece))  103 us
    another operation x1, loops' own time, on_device(): lax.fori_loop(0, live_count, backward_input, (jnp.zeros_like(my_tiles), j...  98.3 us
    another operation x1, loops' own time, on_device(): lax.fori_loop(0, live_count, forward_back, (jnp.zeros_like(my_tiles), jnp...  98.1 us
    ppermute x4, starting transfers between devices, shifted(): return lax.ppermute(block, axis, route)  90.4 us
    while x108, local copies, waits for them, and re-layouts  27 us
    dynamic_update_slice x6, other arithmetic, backward_input(): grad_buf = lax.dynamic_update_index_in_dim(grad_buf, grad_tile, slot_pos, 0)  18.2 us
    ppermute x4, waiting for transfers between devices, shifted(): return lax.ppermute(block, axis, route)  15.9 us
  transfers between devices with their start and end apart: 5, of which 4 were waited for; matrix products, arithmetic and copies ran while one was open for 18% of the time, Pallas kernels for 0%

commit v1 on v0

v1 whole, which is shorter than its diff:
```python
import functools
import math

import jax
import jax.numpy as jnp
from jax import lax
from jax.experimental import pallas as pl
from jax.experimental.pallas import tpu as pltpu
from jax.sharding import PartitionSpec as P

ROOT_TWO_PI = 0.7978845608
CUBIC_TERM = 0.044715
EPSILON = 1e-06

F32 = jnp.float32
BF16 = jnp.bfloat16
LANES = 128
TAPS = 7
RIM = 3
AXES = ("space", "dp")
VMEM_LIMIT = 56 * 1024 * 1024


def vmem_spec():
    return pl.BlockSpec(memory_space=pltpu.VMEM)


def smem_spec():
    return pl.BlockSpec(memory_space=pltpu.SMEM)


def call(body, outs, ins, scratch=(), smem=0):
    return pl.pallas_call(
        body,
        out_shape=tuple(jax.ShapeDtypeStruct(s, d) for s, d in outs),
        in_specs=[smem_spec()] * smem + [vmem_spec()] * (len(ins) - smem),
        out_specs=tuple(vmem_spec() for _ in outs),
        scratch_shapes=list(scratch),
        compiler_params=pltpu.CompilerParams(vmem_limit_bytes=VMEM_LIMIT),
    )(*ins)


def slot_pick(nbr_ref, which):
    slots = nbr_ref.shape[0]
    row = lax.broadcasted_iota(jnp.int32, (slots, LANES), 0)
    ids = jnp.full((slots, LANES), -1, jnp.int32)
    for t in range(slots):
        ids = jnp.where(row == t, nbr_ref[t, which], ids)
    present = ids >= 0
    return jnp.where(present, lax.rem(ids, slots), 0), present


def take(v, pick):
    ids, present = pick
    return jnp.where(present, jnp.take_along_axis(v, ids, axis=0, mode="promise_in_bounds"), 0.0)


def lanes(h):
    return slice(h * LANES, (h + 1) * LANES)


def pad_col(pads, h, r, c):
    west, center, east = pads
    if c < RIM:
        return west[h, r, c * 8 : c * 8 + 8, :]
    c -= RIM
    if c < 16:
        return center[h, r, c * 8 : c * 8 + 8, :]
    c -= 16
    return east[h, r, c * 8 : c * 8 + 8, :]


def spread_taps(k_ref, k8_ref, flip):
    for h in range(2):
        for tap in range(TAPS * TAPS):
            src = TAPS * TAPS - 1 - tap if flip else tap
            k8_ref[h, tap] = jnp.broadcast_to(k_ref[src : src + 1, lanes(h)], (8, LANES))


def conv_wide(pads, k8_ref, h, r, c0, n):
    accs = [None] * n
    for i in range(TAPS):
        xs = [pad_col(pads, h, r + i, c0 + c) for c in range(n + TAPS - 1)]
        for j in range(TAPS):
            kk = k8_ref[h, i * TAPS + j]
            for c in range(n):
                term = xs[c + j] * kk
                accs[c] = term if accs[c] is None else accs[c] + term
    return accs


def conv_tall(pads, k8_ref, h, r0, rows, c0, n):
    accs = [[None] * n for _ in range(rows)]
    for j in range(TAPS):
        ks = [k8_ref[h, i * TAPS + j] for i in range(TAPS)]
        for p in range(rows + TAPS - 1):
            xs = [pad_col(pads, h, r0 + p, c0 + j + c) for c in range(n)]
            for q in range(max(0, p - TAPS + 1), min(rows, p + 1)):
                for c in range(n):
                    term = xs[c] * ks[p - q]
                    accs[q][c] = term if accs[q][c] is None else accs[q][c] + term
    return accs


def gelu_pair(pre):
    sq = pre * pre
    t = jnp.tanh(pre * (ROOT_TWO_PI + (ROOT_TWO_PI * CUBIC_TERM) * sq))
    half = 0.5 + 0.5 * t
    act = pre * half
    slope = half + act * (1.0 - t) * (ROOT_TWO_PI + (3.0 * ROOT_TWO_PI * CUBIC_TERM) * sq)
    return act, slope


def fold(v):
    return jnp.sum(v.reshape(v.shape[0] // 8, 8, v.shape[1]), axis=0)


def dot(a, b):
    return jnp.dot(a, b, preferred_element_type=F32)


def dot_t(a, b):
    return lax.dot_general(a, b, (((1,), (1,)), ((), ())), preferred_element_type=F32)


def dense_block(conv, x, dy, params, dw_ref, sums_ref):
    win, wout, bias_in, bias_out, scale, gain, shift, conv_bias = params
    hidden = win.shape[1]
    channels = win.shape[0]
    conv = conv + conv_bias[...]
    centred = conv - jnp.mean(conv, axis=1, keepdims=True)
    inv_std = lax.rsqrt(jnp.mean(centred * centred, axis=1, keepdims=True) + EPSILON)
    normed = centred * inv_std
    unit = (normed * gain[...] + shift[...]).astype(BF16)
    gb = (dy * scale[...]).astype(BF16)
    unit_t = unit.T
    gb_t = gb.T
    branch = jnp.zeros(conv.shape, F32)
    grad_unit = jnp.zeros(conv.shape, F32)
    for k in range(0, hidden, 256):
        ks = slice(k, k + 256)
        pre = dot(unit, win[:, ks]) + bias_in[:, ks]
        act, slope = gelu_pair(pre)
        act = act.astype(BF16)
        gp = (dot_t(gb, wout[ks, :]) * slope).astype(BF16)
        branch = branch + dot(act, wout[ks, :])
        grad_unit = grad_unit + dot_t(gp, win[:, ks])
        dw_ref[0:channels, ks] += dot(unit_t, gp)
        dw_ref[channels : 2 * channels, ks] += dot(gb_t, act)
        sums_ref[k // 256] += fold(gp.astype(F32))
    branch = branch + bias_out[...]
    out = x + scale[...] * branch
    scaled = grad_unit * gain[...]
    grad_conv = inv_std * (
        scaled
        - jnp.mean(scaled, axis=1, keepdims=True)
        - normed * jnp.mean(scaled * normed, axis=1, keepdims=True)
    )
    grad_conv = grad_conv.astype(BF16).astype(F32)
    nk = hidden // 256
    sums_ref[nk] += fold(gb.astype(F32))
    sums_ref[nk + 1] += fold(dy * branch)
    sums_ref[nk + 2] += fold(grad_unit * normed)
    sums_ref[nk + 3] += fold(grad_unit)
    sums_ref[nk + 4] += fold(grad_conv)
    return out, grad_conv


def rows_of(ref, r0, nr, c0, n):
    blocks = []
    for q in range(nr):
        blocks.append(jnp.concatenate([ref[h, r0 + q, c0 * 8 : (c0 + n) * 8, :] for h in range(2)], axis=1))
    return jnp.concatenate(blocks, axis=0)


def rims_of(center_ref, nbr_ref):
    north = slot_pick(nbr_ref, 0)
    south = slot_pick(nbr_ref, 1)
    for h in range(2):
        for q in range(RIM):
            for c in range(16):
                cs = slice(c * 8, c * 8 + 8)
                center_ref[h, q, cs, :] = take(center_ref[h, 16 + q, cs, :], north)
                center_ref[h, 19 + q, cs, :] = take(center_ref[h, 3 + q, cs, :], south)


def side_rim(side_ref, halo_ref, nbr_ref, straight, up, down):
    mid, top, low = (slot_pick(nbr_ref, w) for w in (straight, up, down))
    for h in range(2):
        for pair in range(24):
            v = halo_ref[pair * 16 : pair * 16 + 16, lanes(h)].astype(F32)
            for s in range(2):
                r, c = divmod(pair * 2 + s, RIM)
                cs = slice(c * 8, c * 8 + 8)
                part = v[s * 8 : s * 8 + 8]
                side_ref[h, 3 + r, cs, :] = take(part, mid)
                if r >= 13:
                    side_ref[h, r - 13, cs, :] = take(part, top)
                if r < 3:
                    side_ref[h, 19 + r, cs, :] = take(part, low)


def inner_kernel(
    nbr_ref, cnt_ref, x_ref, dy_ref, k_ref, win, wout, bias_in, bias_out, scale, gain, shift, conv_bias,
    center_ref, dyt_ref, out_ref, g_ref, dw_ref, sums_ref,
    k8_ref, conv_ref,
):
    live = cnt_ref[0]
    spread_taps(k_ref, k8_ref, False)
    dw_ref[...] = jnp.zeros(dw_ref.shape, F32)
    sums_ref[...] = jnp.zeros(sums_ref.shape, F32)

    def turn(r, carry):
        for t in range(8):
            for h in range(2):
                center_ref[h, 3 + r, pl.ds(t, 16, stride=8), :] = x_ref[t, r, :, lanes(h)].astype(F32)
                dyv = dy_ref[t, r, :, lanes(h)].astype(F32)
                dyt_ref[h, r, pl.ds(t, 16, stride=8), :] = jnp.where(t < live, dyv, 0.0)
        return carry

    lax.fori_loop(0, 16, turn, 0)
    rims_of(center_ref, nbr_ref)
    params = (win, wout, bias_in, bias_out, scale, gain, shift, conv_bias)
    nr, n, c0 = 4, 10, 3
    pads = (None, center_ref, None)

    def block(m, carry):
        r0 = m * nr

        def conv(q, carry):
            for h in range(2):
                accs = conv_wide(pads, k8_ref, h, r0 + q, c0, n)
                conv_ref[pl.ds(pl.multiple_of(q * n * 8, 8), n * 8), lanes(h)] = jnp.concatenate(accs, axis=0)
            return carry

        lax.fori_loop(0, nr, conv, 0)
        x = rows_of(center_ref, r0 + 3, nr, c0, n)
        dy = rows_of(dyt_ref, r0, nr, c0, n)
        out, g = dense_block(conv_ref[...], x, dy, params, dw_ref, sums_ref)
        for q in range(nr):
            for h in range(2):
                out_ref[h, r0 + q] = out[q * n * 8 : (q + 1) * n * 8, lanes(h)]
                g_ref[h, r0 + q] = g[q * n * 8 : (q + 1) * n * 8, lanes(h)]
        return carry

    lax.fori_loop(0, 16 // nr, block, 0)


def edge_kernel(
    nbr_ref, hw_ref, he_ref, center_ref, dyt_ref, dw_in, sums_in,
    k_ref, win, wout, bias_in, bias_out, scale, gain, shift, conv_bias,
    west_ref, east_ref, out_ref, g_ref, send_l, send_r, dw_ref, sums_ref,
    k8_ref, conv_ref,
):
    spread_taps(k_ref, k8_ref, False)
    dw_ref[...] = dw_in[...]
    sums_ref[...] = sums_in[...]
    side_rim(west_ref, hw_ref, nbr_ref, 2, 4, 6)
    side_rim(east_ref, he_ref, nbr_ref, 3, 5, 7)
    params = (win, wout, bias_in, bias_out, scale, gain, shift, conv_bias)
    pads = (west_ref, center_ref, east_ref)
    nr = 8

    def block(m, carry):
        r0 = m * nr
        for h in range(2):
            for side, c0 in enumerate((0, 13)):
                accs = conv_tall(pads, k8_ref, h, r0, nr, c0, RIM)
                for q in range(nr):
                    base = (q * 2 + side) * 24
                    conv_ref[base : base + 24, lanes(h)] = jnp.concatenate(accs[q], axis=0)
        xs, dys = [], []
        for q in range(nr):
            for c0 in (0, 13):
                xs.append(rows_of(center_ref, r0 + 3 + q, 1, c0, RIM))
                dys.append(rows_of(dyt_ref, r0 + q, 1, c0, RIM))
        x = jnp.concatenate(xs, axis=0)
        dy = jnp.concatenate(dys, axis=0)
        out, g = dense_block(conv_ref[...], x, dy, params, dw_ref, sums_ref)
        for q in range(nr):
            for h in range(2):
                out_ref[h, r0 + q] = out[q * 48 : (q + 1) * 48, lanes(h)]
                g_ref[h, r0 + q] = g[q * 48 : (q + 1) * 48, lanes(h)]
        for q in range(0, nr, 2):
            for side, send in enumerate((send_l, send_r)):
                v = jnp.concatenate(
                    [g[(q + s) * 48 + side * 24 : (q + s) * 48 + side * 24 + 24] for s in range(2)], axis=0
                )
                send[pl.ds(pl.multiple_of((r0 + q) * 24, 16), 48), :] = v.astype(BF16)
        return carry

    lax.fori_loop(0, 16 // nr, block, 0)


def full_width(inner_ref, edge_ref, h, r):
    return [edge_ref[h, r, c * 8 : c * 8 + 8, :] for c in range(3)] + [
        inner_ref[h, r, c * 8 : c * 8 + 8, :] for c in range(10)
    ] + [edge_ref[h, r, c * 8 : c * 8 + 8, :] for c in range(3, 6)]


def tap_kernel(
    center_ref, west_ref, east_ref, gi_ref, ge_ref, sums_in,
    small_ref,
    acc_ref,
):
    pads = (west_ref, center_ref, east_ref)

    def row_tap(i, carry):
        for h in range(2):

            def row(r, accs):
                g = full_width(gi_ref, ge_ref, h, r)
                xs = [pad_col(pads, h, r + i, c) for c in range(22)]
                new = []
                for j in range(TAPS):
                    terms = [xs[c + j] * g[c] for c in range(16)]
                    while len(terms) > 1:
                        terms = [a + b for a, b in zip(terms[::2], terms[1::2])]
                    new.append(accs[j] + terms[0])
                return tuple(new)

            accs = lax.fori_loop(0, 16, row, tuple(jnp.zeros((8, LANES), F32) for _ in range(TAPS)))
            for j in range(TAPS):
                acc_ref[i * TAPS + j, :, lanes(h)] = accs[j]
        return carry

    lax.fori_loop(0, TAPS, row_tap, 0)
    small_ref[...] = jnp.zeros(small_ref.shape, F32)
    ns = sums_in.shape[0]
    small_ref[0:ns, :] = jnp.sum(sums_in[...], axis=1)
    small_ref[ns : ns + 49, :] = jnp.sum(acc_ref[...], axis=1)


def back_kernel(
    nbr_ref, cnt_ref, hw_ref, he_ref, gi_ref, ge_ref, dyt_ref, oi_ref, oe_ref, k_ref,
    out_ref, gx_ref,
    west_ref, east_ref, center_ref, full_ref, k8_ref,
):
    live = cnt_ref[0]
    spread_taps(k_ref, k8_ref, True)

    def place(r, carry):
        for h in range(2):
            g = full_width(gi_ref, ge_ref, h, r)
            o = full_width(oi_ref, oe_ref, h, r)
            for c in range(16):
                center_ref[h, 3 + r, c * 8 : c * 8 + 8, :] = g[c]
                full_ref[h, r, c * 8 : c * 8 + 8, :] = o[c]
        for t in range(8):
            for h in range(2):
                v = full_ref[h, r, pl.ds(t, 16, stride=8), :]
                out_ref[t, r, :, lanes(h)] = jnp.where(t < live, v, 0.0).astype(BF16)
        return carry

    lax.fori_loop(0, 16, place, 0)
    rims_of(center_ref, nbr_ref)
    side_rim(west_ref, hw_ref, nbr_ref, 2, 4, 6)
    side_rim(east_ref, he_ref, nbr_ref, 3, 5, 7)
    pads = (west_ref, center_ref, east_ref)

    def row(r, carry):
        for h in range(2):
            accs = conv_wide(pads, k8_ref, h, r, 0, 16)
            for c in range(16):
                cs = slice(c * 8, c * 8 + 8)
                full_ref[h, r, cs, :] = accs[c] + dyt_ref[h, r, cs, :]
        for t in range(8):
            for h in range(2):
                v = full_ref[h, r, pl.ds(t, 16, stride=8), :]
                gx_ref[t, r, :, lanes(h)] = jnp.where(t < live, v, 0.0).astype(BF16)
        return carry

    lax.fori_loop(0, 16, row, 0)


def shifted(block, axis, distance):
    n = lax.axis_size(axis)
    return lax.ppermute(block, axis, [((i - distance) % n, i) for i in range(n)])


def crossed(v, mask):
    n = lax.axis_size(AXES)
    return lax.ppermute(v, AXES, [(i, i ^ mask) for i in range(n)])


def stages():
    total = lax.axis_size(AXES)
    found, bit = [(1, 2)], 2
    while bit < total:
        size = min(4, total // bit)
        found.append((bit, size))
        bit *= size
    return found


def reduce_all(v):
    me = lax.axis_index(AXES)
    rows, width = v.shape
    for bit, size in stages():
        mine = (me // bit) % size
        parts = v.reshape(size, v.shape[0] // size, width)
        acc = lax.dynamic_index_in_dim(parts, mine, 0, keepdims=False).astype(F32)
        for k in range(1, size):
            sent = lax.dynamic_index_in_dim(parts, mine ^ k, 0, keepdims=False)
            acc = acc + crossed(sent, k * bit).astype(F32)
        v = acc.astype(BF16)
    for bit, size in stages()[::-1]:
        mine = (me // bit) % size
        out = jnp.zeros((size,) + v.shape, BF16)
        out = lax.dynamic_update_index_in_dim(out, v, mine, 0)
        for k in range(1, size):
            out = lax.dynamic_update_index_in_dim(out, crossed(v, k * bit), mine ^ k, 0)
        v = out.reshape(size * v.shape[0], width)
    return v


def reduce_small(v):
    for bit, size in stages():
        acc = v
        for k in range(1, size):
            acc = acc + crossed(v, k * bit)
        v = acc
    return v


def on_device(
    activations, cotangent, tile_count, neighbours, conv_kernel, conv_bias, norm_gain, norm_bias,
    proj_in, bias_in, proj_out, bias_out, layer_scale,
):
    x = activations[0]
    dy = cotangent[0]
    slots, edge, _, channels = x.shape
    hidden = proj_in.shape[1]
    taps = conv_kernel.reshape(TAPS * TAPS, channels)
    row = lambda v: v.reshape(1, -1)
    weights = (
        proj_in, proj_out, row(bias_in), row(bias_out), row(layer_scale), row(norm_gain), row(norm_bias),
        row(conv_bias),
    )

    def columns(lo):
        return x[:, :, lo : lo + RIM].transpose(1, 2, 0, 3).reshape(edge * RIM * slots, channels)

    from_east = shifted(columns(0), "space", -1)
    from_west = shifted(columns(edge - RIM), "space", 1)
    ns = hidden // 256 + 5
    half = (2, edge, edge * slots, LANES)
    k8 = pltpu.VMEM((2, TAPS * TAPS, 8, LANES), F32)
    side = (2, edge + 2 * RIM, RIM * slots, LANES)
    tall = (2, edge + 2 * RIM, edge * slots, LANES)
    inner = (2, edge, (edge - 2 * RIM) * slots, LANES)
    edges = (2, edge, 2 * RIM * slots, LANES)
    halo = (edge * RIM * slots, channels)
    dw_shape = (2 * channels, hidden)

    center, dyt, out_i, g_i, dw, sums = call(
        inner_kernel,
        [(tall, F32), (half, F32), (inner, F32), (inner, F32), (dw_shape, F32), ((ns, 8, channels), F32)],
        (neighbours, tile_count, x, dy, taps) + weights,
        [k8, pltpu.VMEM((4 * 10 * slots, channels), F32)],
        smem=2,
    )
    west, east, out_e, g_e, send_l, send_r, dw, sums = call(
        edge_kernel,
        [(side, F32), (side, F32), (edges, F32), (edges, F32), (halo, BF16), (halo, BF16),
         (dw_shape, F32), ((ns, 8, channels), F32)],
        (neighbours, from_west, from_east, center, dyt, dw, sums, taps) + weights,
        [k8, pltpu.VMEM((8 * 6 * slots, channels), F32)],
        smem=1,
    )
    grad_from_east = shifted(send_l, "space", -1)
    grad_from_west = shifted(send_r, "space", 1)
    dw = reduce_all(dw.astype(BF16))
    (small,) = call(
        tap_kernel,
        [((64, channels), F32)],
        (center, west, east, g_i, g_e, sums),
        [pltpu.VMEM((TAPS * TAPS, 8, channels), F32)],
    )
    small = reduce_small(small)
    out_tiles, grad_tiles = call(
        back_kernel,
        [((slots, edge, edge, channels), BF16)] * 2,
        (neighbours, tile_count, grad_from_west, grad_from_east, g_i, g_e, dyt, out_i, out_e, taps),
        [pltpu.VMEM(side, F32), pltpu.VMEM(side, F32), pltpu.VMEM(tall, F32), pltpu.VMEM(half, F32), k8],
        smem=2,
    )
    factor = 1.0 / math.sqrt(lax.axis_size("dp") * lax.axis_size("space") * slots * edge * edge)
    small = small * factor
    dw = dw.astype(F32) * factor
    nk = hidden // 256
    return (
        out_tiles[None],
        grad_tiles[None],
        small[ns : ns + 49].reshape(TAPS, TAPS, channels),
        small[nk + 4],
        small[nk + 2],
        small[nk + 3],
        dw[:channels],
        small[:nk].reshape(-1),
        dw[channels:].T,
        small[nk],
        small[nk + 1],
    )


def solution(mesh):
    tiles = P("dp", "space", None, None, None)
    return jax.shard_map(
        on_device,
        mesh=mesh,
        in_specs=(tiles, tiles, P("space"), P("space", None)) + (P(),) * 9,
        out_specs=(tiles, tiles) + (P(),) * 9,
        check_vma=False,
    )
```

time: 735 us -> 130 us (0.18); the launches traced: 725 us -> 130 us
  loops' own time: 196 us -> 0 us
  other arithmetic: 185 us -> 3.21 us
  blocking collectives: 121 us -> 0 us
  local copies, waits for them, and re-layouts: 78.2 us -> 9.43 us
  Pallas kernels: 0 us -> 60.6 us
  starting transfers between devices: 90.5 us -> 35 us
  matrix products: 23.8 us -> 0 us
  between operations: 14.2 us -> 1.68 us
    another operation x2 -> x0, loops' own time: 196 us -> none  [the longest x1 98.3 us: on_device(): lax.fori_loop(0, live_count, backward_input, (jnp.zeros_like(my_tiles), j...]
    psum x1 -> x0, blocking collectives: 121 us -> none  [on_device(): lax.psum((dense_local[0], dense_local[1], dense_local[2], dense_local[3],...]
    select_n x60 -> x0, other arithmetic: 111 us -> none  [the longest x48 103 us: masked_piece(): return jnp.where(present[which], piece, jnp.zeros_like(piece))]
    pallas_call x0 -> x4, Pallas kernels: none -> 60.6 us  [call(): pl.pallas_call(body, out_shape=tuple((jax.ShapeDtypeStruct(s, d) for s, d...]
    ppermute x4 -> x25, starting transfers between devices: 90.4 us -> 35 us  [the longest x21 24.1 us: crossed(): return lax.ppermute(v, AXES, [(i, i ^ mask) for i in range(n)])]
    reduce_sum x48 -> x0, other arithmetic: 36.2 us -> none  [the longest x24 15.2 us: kernel_grad(): jnp.sum(window.astype(jnp.float32) * grad_vals, axis=axes_all)]
    while x108 -> x0, local copies, waits for them, and re-layouts: 27 us -> none
    dot_general x36 -> x0, matrix products: 23.8 us -> none  [the longest x6 8.35 us: forward_back(): jnp.dot(act_bf, proj_out, preferred_element_type=jnp.float32) + bias_out]
  transfers between devices with their start and end apart: 5 -> 25, of which waited for: 4 -> 7; matrix products, arithmetic and copies ran while one was open for 18% -> 4% of each run, Pallas kernels for 0% -> 35%
where the time goes in v1:
time: 130 us
  Pallas kernels  60.6 us (47%)
  starting transfers between devices  35 us (27%)
  waiting for transfers between devices  20 us (15%)
  local copies, waits for them, and re-layouts  9.43 us (7%)
  other arithmetic  3.21 us (2%)
  between operations  1.68 us (1%)
    pallas_call x4, Pallas kernels, call(): pl.pallas_call(body, out_shape=tuple((jax.ShapeDtypeStruct(s, d) for s, d...  60.6 us
    ppermute x21, starting transfers between devices, crossed(): return lax.ppermute(v, AXES, [(i, i ^ mask) for i in range(n)])  24.1 us
    ppermute x21, waiting for transfers between devices, crossed(): return lax.ppermute(v, AXES, [(i, i ^ mask) for i in range(n)])  20 us
    ppermute x4, starting transfers between devices, shifted(): lax.ppermute(block, axis, [((i - distance) % n, i) for i in range(n)])  10.9 us
    unnamed x15, local copies, waits for them, and re-layouts  3.41 us
  transfers between devices with their start and end apart: 25, of which 7 were waited for; matrix products, arithmetic and copies ran while one was open for 4% of the time, Pallas kernels for 35%

profile of v1, /device:TPU:0, one launch (start us, length us, event | category | flops | bytes accessed | tf_op | source)
XLA Modules:
  0.0 129.9 jit_solution(15163729638484291238)
XLA Ops:
  0.6 1.5 %slice_bitcast_fusion.2 = (bf16[16,3,8,256]{3,1,0,2:T(4,128)(2,1)S(1)}, bf16[16,3,8,256]{3,1,0,2:T(4,128)(2,1)S(1)}) fusion(bf16[8,16,16,256]{3,2,1,0:T(8,128)(2,1)} %bitcast.83), kind=kLoop, calls=%fused_computation.8 | loop fusion | bytes 786432 | tf_op jit(solution)/shard_map/transpose | solution.py:442
  2.3 3.0 %collective-permute-start = (bf16[384,256]{1,0:T(8,128)(2,1)S(1)}, bf16[384,256]{1,0:T(8,128)(2,1)S(1)}, u32[]{:S(2)}, u32[]{:S(2)}) collective-permute-start(bf16[384,256]{1,0:T(8,128)(2,1)S(1)} %bitcast.96), channel_id=1, source_target_pairs={{28,0},{0,4},{4,8},{8,12},{12,16},{16,20},{20,24},{24,28},{29,1},{... | collective-permute-start | bytes 589832 | tf_op jit(solution)/shard_map/ppermute | solution.py:378
  5.4 3.1 %collective-permute-start.1 = (bf16[384,256]{1,0:T(8,128)(2,1)S(1)}, bf16[384,256]{1,0:T(8,128)(2,1)S(1)}, u32[]{:S(2)}, u32[]{:S(2)}) collective-permute-start(bf16[384,256]{1,0:T(8,128)(2,1)S(1)} %bitcast.97), channel_id=1, source_target_pairs={{4,0},{8,4},{12,8},{16,12},{20,16},{24,20},{28,24},{0,28},{5,1},{9... | collective-permute-start | bytes 589832 | tf_op jit(solution)/shard_map/ppermute | solution.py:378
  9.2 1.4 %reshape.86.k_ref = f32[49,256]{1,0:T(8,128)} reshape(f32[7,7,256]{2,1,0:T(8,128)} %param.17) | data formatting | bytes 100352 | tf_op jit(solution)/shard_map/reshape | solution.py:434
  10.6 20.7 %shard_map.212 = (f32[2,22,128,128]{3,2,1,0:T(8,128)}, f32[2,16,128,128]{3,2,1,0:T(8,128)}, f32[2,16,80,128]{3,2,1,0:T(8,128)}, f32[2,16,80,128]{3,2,1,0:T(8,128...) custom-call(s32[8,8]{1,0:T(8,128)} %nbr_ref.5, s32[1]{0:T(128)S(6)} %copy.49.cnt_ref, bf16[8,16,16,256]{3,2,1,0:T(8,128)(2,1)} %bitcast.84, ...), custom_call_target="tpu_custom_call" | custom-call | tf_op jit(solution)/shard_map/pallas_call | solution.py:33
  31.4 0.6 copy-done.2
  32.2 15.1 %shard_map.213 = (f32[2,22,24,128]{3,2,1,0:T(8,128)}, f32[2,22,24,128]{3,2,1,0:T(8,128)}, f32[2,16,48,128]{3,2,1,0:T(8,128)}, f32[2,16,48,128]{3,2,1,0:T(8,128)}...) custom-call(s32[8,8]{1,0:T(8,128)} %nbr_ref.5, ...), custom_call_target="tpu_custom_call" | custom-call | tf_op jit(solution)/shard_map/pallas_call | solution.py:33
  47.2 1.7 %convert_element_type.55 = bf16[512,1024]{1,0:T(8,128)(2,1)S(1)} convert(f32[512,1024]{1,0:T(8,128)} %get-tuple-element.42) | non-fusion elementwise | flops 524288 | bytes 3145728 | tf_op jit(solution)/shard_map/convert_element_type | solution.py:473
  49.2 1.8 %collective-permute-done.11 = bf16[256,1024]{1,0:T(8,128)(2,1)S(1)} collective-permute-done((bf16[256,1024]{1,0:T(8,128)(2,1)S(1)}, bf16[256,1024]{1,0:T(8,128)(2,1)S(1)}, u32[]{:S(2)}, u32[]{:S(2)}) %collective-permute-start.11) | collective-permute-done | bytes 524320 | tf_op jit(solution)/shard_map/ppermute | solution.py:383
  51.4 3.1 %collective-permute-start.13 = (bf16[64,1024]{1,0:T(8,128)(2,1)S(1)}, bf16[64,1024]{1,0:T(8,128)(2,1)S(1)}, u32[]{:S(2)}, u32[]{:S(2)}) collective-permute-start(bf16[64,1024]{1,0:T(8,128)(2,1)S(1)} %get-tuple-element.62), channel_id=1, source_target_pairs={{0,4},{1,5},{2,6},{3,7},{4,0},{5,1},{6,2},{7,3},{8,12},{9,13},{10,... | collective-permute-start | bytes 393224 | tf_op jit(solution)/shard_map/ppermute | solution.py:383
  54.8 12.7 %shard_map.215 = f32[64,256]{1,0:T(8,128)} custom-call(f32[2,22,128,128]{3,2,1,0:T(8,128)} %get-tuple-element.27.center_ref, f32[2,22,24,128]{3,2,1,0:T(8,128)} %get-tuple-element.39.west_ref, f32[2,22,24,128]{3,2,1,0:T(8,128)} %get-tuple-element.40.east_ref, f32[2,16,80,128]{3,2,1,0:T(8,128)} %get-tuple-element.33.gi_ref, ...), custom_call_target="tpu_custom_call" | custom-call | tf_op jit(solution)/shard_map/pallas_call | solution.py:33
  67.6 2.0 %collective-permute-start.17 = (bf16[16,1024]{1,0:T(8,128)(2,1)S(1)}, bf16[16,1024]{1,0:T(8,128)(2,1)S(1)}, u32[]{:S(2)}, u32[]{:S(2)}) collective-permute-start(bf16[16,1024]{1,0:T(8,128)(2,1)S(1)} %get-tuple-element.64), channel_id=1, source_target_pairs={{0,24},{1,25},{2,26},{3,27},{4,28},{5,29},{6,30},{7,31},{8,16},{9,... | collective-permute-start | bytes 98312 | tf_op jit(solution)/shard_map/ppermute | solution.py:383
  69.7 2.4 %collective-permute-start.15 = (bf16[16,1024]{1,0:T(8,128)(2,1)S(1)}, bf16[16,1024]{1,0:T(8,128)(2,1)S(1)}, u32[]{:S(2)}, u32[]{:S(2)}) collective-permute-start(bf16[16,1024]{1,0:T(8,128)(2,1)S(1)} %get-tuple-element.63), channel_id=1, source_target_pairs={{0,8},{1,9},{2,10},{3,11},{4,12},{5,13},{6,14},{7,15},{8,0},{9,1},... | collective-permute-start | bytes 98312 | tf_op jit(solution)/shard_map/ppermute | solution.py:383
  72.4 4.5 %collective-permute-start.3 = (bf16[384,256]{1,0:T(8,128)(2,1)S(1)}, bf16[384,256]{1,0:T(8,128)(2,1)S(1)}, u32[]{:S(2)}, u32[]{:S(2)}) collective-permute-start(bf16[384,256]{1,0:T(8,128)(2,1)S(1)} %copy-done.4), channel_id=1, source_target_pairs={{4,0},{8,4},{12,8},{16,12},{20,16},{24,20},{28,24},{0,28},{5,1},{9... | collective-permute-start | bytes 589832 | tf_op jit(solution)/shard_map/ppermute | solution.py:378
  76.8 0.8 add.107
  77.8 3.1 %collective-permute-start.6 = (f32[64,256]{1,0:T(8,128)S(1)}, f32[64,256]{1,0:T(8,128)S(1)}, u32[]{:S(2)}, u32[]{:S(2)}) collective-permute-start(f32[64,256]{1,0:T(8,128)S(1)} %add.107), channel_id=1, source_target_pairs={{0,4},{1,5},{2,6},{3,7},{4,0},{5,1},{6,2},{7,3},{8,12},{9,13},{10,... | collective-permute-start | bytes 196616 | tf_op jit(solution)/shard_map/ppermute | solution.py:383
  81.3 1.9 %collective-permute-done.7 = f32[64,256]{1,0:T(8,128)S(1)} collective-permute-done((f32[64,256]{1,0:T(8,128)S(1)}, f32[64,256]{1,0:T(8,128)S(1)}, u32[]{:S(2)}, u32[]{:S(2)}) %collective-permute-start.7) | collective-permute-done | bytes 65568 | tf_op jit(solution)/shard_map/ppermute | solution.py:383
  83.2 2.6 %collective-permute-done.6 = f32[64,256]{1,0:T(8,128)S(1)} collective-permute-done((f32[64,256]{1,0:T(8,128)S(1)}, f32[64,256]{1,0:T(8,128)S(1)}, u32[]{:S(2)}, u32[]{:S(2)}) %collective-permute-start.6) | collective-permute-done | bytes 65568 | tf_op jit(solution)/shard_map/ppermute | solution.py:383
  85.9 2.7 %collective-permute-start.10 = (f32[64,256]{1,0:T(8,128)S(1)}, f32[64,256]{1,0:T(8,128)S(1)}, u32[]{:S(2)}, u32[]{:S(2)}) collective-permute-start(f32[64,256]{1,0:T(8,128)S(1)} %add_add_fusion), channel_id=1, source_target_pairs={{0,24},{1,25},{2,26},{3,27},{4,28},{5,29},{6,30},{7,31},{8,16},{9,... | collective-permute-start | bytes 196616 | tf_op jit(solution)/shard_map/ppermute | solution.py:383
  88.5 2.9 %collective-permute-start.19 = (bf16[16,1024]{1,0:T(8,128)(2,1)S(1)}, bf16[16,1024]{1,0:T(8,128)(2,1)S(1)}, u32[]{:S(2)}, u32[]{:S(2)}) collective-permute-start(bf16[16,1024]{1,0:T(8,128)(2,1)S(1)} %get-tuple-element.55), channel_id=1, source_target_pairs={{0,16},{1,17},{2,18},{3,19},{4,20},{5,21},{6,22},{7,23},{8,24},{9,... | collective-permute-start | bytes 98312 | tf_op jit(solution)/shard_map/ppermute | solution.py:383
  91.5 4.3 %collective-permute-done.19 = bf16[16,1024]{1,0:T(8,128)(2,1)S(1)} collective-permute-done((bf16[16,1024]{1,0:T(8,128)(2,1)S(1)}, bf16[16,1024]{1,0:T(8,128)(2,1)S(1)}, u32[]{:S(2)}, u32[]{:S(2)}) %collective-permute-start.19) | collective-permute-done | bytes 32800 | tf_op jit(solution)/shard_map/ppermute | solution.py:383
  95.7 2.4 %collective-permute-start.20 = (bf16[16,1024]{1,0:T(8,128)(2,1)S(1)}, bf16[16,1024]{1,0:T(8,128)(2,1)S(1)}, u32[]{:S(2)}, u32[]{:S(2)}) collective-permute-start(bf16[16,1024]{1,0:T(8,128)(2,1)S(1)} %get-tuple-element.55), channel_id=1, source_target_pairs={{0,24},{1,25},{2,26},{3,27},{4,28},{5,29},{6,30},{7,31},{8,16},{9,... | collective-permute-start | bytes 98312 | tf_op jit(solution)/shard_map/ppermute | solution.py:383
  98.1 3.3 %collective-permute-done.20 = bf16[16,1024]{1,0:T(8,128)(2,1)S(1)} collective-permute-done((bf16[16,1024]{1,0:T(8,128)(2,1)S(1)}, bf16[16,1024]{1,0:T(8,128)(2,1)S(1)}, u32[]{:S(2)}, u32[]{:S(2)}) %collective-permute-start.20) | collective-permute-done | bytes 32800 | tf_op jit(solution)/shard_map/ppermute | solution.py:383
  101.4 1.5 %collective-permute-start.21 = (bf16[64,1024]{1,0:T(8,128)(2,1)S(1)}, bf16[64,1024]{1,0:T(8,128)(2,1)S(1)}, u32[]{:S(2)}, u32[]{:S(2)}) collective-permute-start(bf16[64,1024]{1,0:T(8,128)(2,1)S(1)} %bitcast.90), channel_id=1, source_target_pairs={{0,2},{1,3},{2,0},{3,1},{4,6},{5,7},{6,4},{7,5},{8,10},{9,11},{10,... | collective-permute-start | bytes 393224 | tf_op jit(solution)/shard_map/ppermute | solution.py:383
  103.0 2.7 %collective-permute-done.8 = f32[64,256]{1,0:T(8,128)S(1)} collective-permute-done((f32[64,256]{1,0:T(8,128)S(1)}, f32[64,256]{1,0:T(8,128)S(1)}, u32[]{:S(2)}, u32[]{:S(2)}) %collective-permute-start.8) | collective-permute-done | bytes 65568 | tf_op jit(solution)/shard_map/ppermute | solution.py:383
  105.7 0.6 reshape.93
  106.4 2.9 %collective-permute-start.23 = (bf16[64,1024]{1,0:T(8,128)(2,1)S(1)}, bf16[64,1024]{1,0:T(8,128)(2,1)S(1)}, u32[]{:S(2)}, u32[]{:S(2)}) collective-permute-start(bf16[64,1024]{1,0:T(8,128)(2,1)S(1)} %bitcast.92), channel_id=1, source_target_pairs={{0,6},{1,7},{2,4},{3,5},{4,2},{5,3},{6,0},{7,1},{8,14},{9,15},{10,... | collective-permute-start | bytes 393224 | tf_op jit(solution)/shard_map/ppermute | solution.py:383
  109.4 3.3 %collective-permute-done.22 = bf16[64,1024]{1,0:T(8,128)(2,1)S(1)} collective-permute-done((bf16[64,1024]{1,0:T(8,128)(2,1)S(1)}, bf16[64,1024]{1,0:T(8,128)(2,1)S(1)}, u32[]{:S(2)}, u32[]{:S(2)}) %collective-permute-start.22) | collective-permute-done | bytes 131104 | tf_op jit(solution)/shard_map/ppermute | solution.py:383
  113.5 0.7 copy-done
  114.2 12.1 %shard_map.214 = (bf16[8,16,16,256]{3,2,1,0:T(8,128)(2,1)}, bf16[8,16,16,256]{3,2,1,0:T(8,128)(2,1)}) custom-call(s32[8,8]{1,0:T(8,128)} %nbr_ref.5, s32[1]{0:T(128)S(6)} %copy.49.cnt_ref, bf16[384,256]{1,0:T(8,128)(2,1)} %copy-done, bf16[384,256]{1,0:T(8,128)(2,1)} %copy-done.1, f32[2,16,80,128]{3,2,1,0:T(8,128)} %get-tuple-element.33.gi_ref, ...), custom_call_target="tpu_custom_call" | custom-call | tf_op jit(solution)/shard_map/pallas_call | solution.py:33
  127.4 1.2 slice_bitcast_fusion
  128.6 1.3 %copy.37 = f32[1024,256]{1,0:T(8,128)} copy(f32[1024,256]{0,1:T(8,128)S(1)} %get-tuple-element.56) | data formatting | bytes 2097152
  (68 shorter events, 4.1 us)
Async XLA Ops:
  2.3 29.1 %collective-permute-start = (bf16[384,256]{1,0:T(8,128)(2,1)S(1)}, bf16[384,256]{1,0:T(8,128)(2,1)S(1)}, u32[]{:S(2)}, u32[]{:S(2)}) collective-permute-start(bf16[384,256]{1,0:T(8,128)(2,1)S(1)} %bitcast.96), channel_id=1, source_target_pairs={{28,0},{0,4},{4,8},{8,12},{12,16},{16,20},{20,24},{24,28},{29,1},{... | collective-permute-start | bytes 589832 | tf_op jit(solution)/shard_map/ppermute | solution.py:378
  5.4 26.0 %collective-permute-start.1 = (bf16[384,256]{1,0:T(8,128)(2,1)S(1)}, bf16[384,256]{1,0:T(8,128)(2,1)S(1)}, u32[]{:S(2)}, u32[]{:S(2)}) collective-permute-start(bf16[384,256]{1,0:T(8,128)(2,1)S(1)} %bitcast.97), channel_id=1, source_target_pairs={{4,0},{8,4},{12,8},{16,12},{20,16},{24,20},{28,24},{0,28},{5,1},{9... | collective-permute-start | bytes 589832 | tf_op jit(solution)/shard_map/ppermute | solution.py:378
  31.4 0.7 copy-start.2
  31.4 0.8 copy-start.3
  49.0 2.0 %collective-permute-start.11 = (bf16[256,1024]{1,0:T(8,128)(2,1)S(1)}, bf16[256,1024]{1,0:T(8,128)(2,1)S(1)}, u32[]{:S(2)}, u32[]{:S(2)}) collective-permute-start(bf16[256,1024]{1,0:T(8,128)(2,1)S(1)} %dynamic-slice_bitcast_fusion), channel_id=1, source_target_pairs={{0,1},{1,0},{2,3},{3,2},{4,5},{5,4},{6,7},{7,6},{8,9},{9,8},{10,11... | collective-permute-start | bytes 1572872 | tf_op jit(solution)/shard_map/ppermute | solution.py:383
  51.3 16.2 %collective-permute-start.14 = (bf16[64,1024]{1,0:T(8,128)(2,1)S(1)}, bf16[64,1024]{1,0:T(8,128)(2,1)S(1)}, u32[]{:S(2)}, u32[]{:S(2)}) collective-permute-start(bf16[64,1024]{1,0:T(8,128)(2,1)S(1)} %get-tuple-element.61), channel_id=1, source_target_pairs={{0,6},{1,7},{2,4},{3,5},{4,2},{5,3},{6,0},{7,1},{8,14},{9,15},{10,... | collective-permute-start | bytes 393224 | tf_op jit(solution)/shard_map/ppermute | solution.py:383
  51.4 16.2 %collective-permute-start.13 = (bf16[64,1024]{1,0:T(8,128)(2,1)S(1)}, bf16[64,1024]{1,0:T(8,128)(2,1)S(1)}, u32[]{:S(2)}, u32[]{:S(2)}) collective-permute-start(bf16[64,1024]{1,0:T(8,128)(2,1)S(1)} %get-tuple-element.62), channel_id=1, source_target_pairs={{0,4},{1,5},{2,6},{3,7},{4,0},{5,1},{6,2},{7,3},{8,12},{9,13},{10,... | collective-permute-start | bytes 393224 | tf_op jit(solution)/shard_map/ppermute | solution.py:383
  54.4 13.1 %collective-permute-start.12 = (bf16[64,1024]{1,0:T(8,128)(2,1)S(1)}, bf16[64,1024]{1,0:T(8,128)(2,1)S(1)}, u32[]{:S(2)}, u32[]{:S(2)}) collective-permute-start(bf16[64,1024]{1,0:T(8,128)(2,1)S(1)} %get-tuple-element.60), channel_id=1, source_target_pairs={{0,2},{1,3},{2,0},{3,1},{4,6},{5,7},{6,4},{7,5},{8,10},{9,11},{10,... | collective-permute-start | bytes 393224 | tf_op jit(solution)/shard_map/ppermute | solution.py:383
  54.8 17.3 %copy-start.5 = (bf16[384,256]{1,0:T(8,128)(2,1)S(1)}, bf16[384,256]{1,0:T(8,128)(2,1)}, u32[]{:S(2)}) copy-start(bf16[384,256]{1,0:T(8,128)(2,1)} %get-tuple-element.31) | copy-start | bytes 589828
  54.8 17.5 %copy-start.4 = (bf16[384,256]{1,0:T(8,128)(2,1)S(1)}, bf16[384,256]{1,0:T(8,128)(2,1)}, u32[]{:S(2)}) copy-start(bf16[384,256]{1,0:T(8,128)(2,1)} %get-tuple-element.32) | copy-start | bytes 589828
  67.5 4.9 %collective-permute-start.4 = (f32[64,256]{1,0:T(8,128)}, f32[64,256]{1,0:T(8,128)S(1)}, u32[]{:S(2)}, u32[]{:S(2)}) collective-permute-start(f32[64,256]{1,0:T(8,128)} %shard_map.215), channel_id=1, source_target_pairs={{0,1},{1,0},{2,3},{3,2},{4,5},{5,4},{6,7},{7,6},{8,9},{9,8},{10,11... | collective-permute-start | bytes 196616 | tf_op jit(solution)/shard_map/ppermute | solution.py:383
  67.6 10.0 %collective-permute-start.17 = (bf16[16,1024]{1,0:T(8,128)(2,1)S(1)}, bf16[16,1024]{1,0:T(8,128)(2,1)S(1)}, u32[]{:S(2)}, u32[]{:S(2)}) collective-permute-start(bf16[16,1024]{1,0:T(8,128)(2,1)S(1)} %get-tuple-element.64), channel_id=1, source_target_pairs={{0,24},{1,25},{2,26},{3,27},{4,28},{5,29},{6,30},{7,31},{8,16},{9,... | collective-permute-start | bytes 98312 | tf_op jit(solution)/shard_map/ppermute | solution.py:383
  69.7 8.1 %collective-permute-start.16 = (bf16[16,1024]{1,0:T(8,128)(2,1)S(1)}, bf16[16,1024]{1,0:T(8,128)(2,1)S(1)}, u32[]{:S(2)}, u32[]{:S(2)}) collective-permute-start(bf16[16,1024]{1,0:T(8,128)(2,1)S(1)} %get-tuple-element.65), channel_id=1, source_target_pairs={{0,16},{1,17},{2,18},{3,19},{4,20},{5,21},{6,22},{7,23},{8,24},{9,... | collective-permute-start | bytes 98312 | tf_op jit(solution)/shard_map/ppermute | solution.py:383
  69.7 11.2 %collective-permute-start.15 = (bf16[16,1024]{1,0:T(8,128)(2,1)S(1)}, bf16[16,1024]{1,0:T(8,128)(2,1)S(1)}, u32[]{:S(2)}, u32[]{:S(2)}) collective-permute-start(bf16[16,1024]{1,0:T(8,128)(2,1)S(1)} %get-tuple-element.63), channel_id=1, source_target_pairs={{0,8},{1,9},{2,10},{3,11},{4,12},{5,13},{6,14},{7,15},{8,0},{9,1},... | collective-permute-start | bytes 98312 | tf_op jit(solution)/shard_map/ppermute | solution.py:383
  72.1 41.4 %collective-permute-start.2 = (bf16[384,256]{1,0:T(8,128)(2,1)S(1)}, bf16[384,256]{1,0:T(8,128)(2,1)S(1)}, u32[]{:S(2)}, u32[]{:S(2)}) collective-permute-start(bf16[384,256]{1,0:T(8,128)(2,1)S(1)} %copy-done.5), channel_id=1, source_target_pairs={{28,0},{0,4},{4,8},{8,12},{12,16},{16,20},{20,24},{24,28},{29,1},{... | collective-permute-start | bytes 589832 | tf_op jit(solution)/shard_map/ppermute | solution.py:378
  72.4 41.1 %collective-permute-start.3 = (bf16[384,256]{1,0:T(8,128)(2,1)S(1)}, bf16[384,256]{1,0:T(8,128)(2,1)S(1)}, u32[]{:S(2)}, u32[]{:S(2)}) collective-permute-start(bf16[384,256]{1,0:T(8,128)(2,1)S(1)} %copy-done.4), channel_id=1, source_target_pairs={{4,0},{8,4},{12,8},{16,12},{20,16},{24,20},{28,24},{0,28},{5,1},{9... | collective-permute-start | bytes 589832 | tf_op jit(solution)/shard_map/ppermute | solution.py:378
  77.7 5.5 %collective-permute-start.7 = (f32[64,256]{1,0:T(8,128)S(1)}, f32[64,256]{1,0:T(8,128)S(1)}, u32[]{:S(2)}, u32[]{:S(2)}) collective-permute-start(f32[64,256]{1,0:T(8,128)S(1)} %add.107), channel_id=1, source_target_pairs={{0,6},{1,7},{2,4},{3,5},{4,2},{5,3},{6,0},{7,1},{8,14},{9,15},{10,... | collective-permute-start | bytes 196616 | tf_op jit(solution)/shard_map/ppermute | solution.py:383
  77.8 8.1 %collective-permute-start.6 = (f32[64,256]{1,0:T(8,128)S(1)}, f32[64,256]{1,0:T(8,128)S(1)}, u32[]{:S(2)}, u32[]{:S(2)}) collective-permute-start(f32[64,256]{1,0:T(8,128)S(1)} %add.107), channel_id=1, source_target_pairs={{0,4},{1,5},{2,6},{3,7},{4,0},{5,1},{6,2},{7,3},{8,12},{9,13},{10,... | collective-permute-start | bytes 196616 | tf_op jit(solution)/shard_map/ppermute | solution.py:383
  80.9 5.0 %collective-permute-start.5 = (f32[64,256]{1,0:T(8,128)S(1)}, f32[64,256]{1,0:T(8,128)S(1)}, u32[]{:S(2)}, u32[]{:S(2)}) collective-permute-start(f32[64,256]{1,0:T(8,128)S(1)} %add.107), channel_id=1, source_target_pairs={{0,2},{1,3},{2,0},{3,1},{4,6},{5,7},{6,4},{7,5},{8,10},{9,11},{10,... | collective-permute-start | bytes 196616 | tf_op jit(solution)/shard_map/ppermute | solution.py:383
  83.2 5.3 %collective-permute-start.18 = (bf16[16,1024]{1,0:T(8,128)(2,1)S(1)}, bf16[16,1024]{1,0:T(8,128)(2,1)S(1)}, u32[]{:S(2)}, u32[]{:S(2)}) collective-permute-start(bf16[16,1024]{1,0:T(8,128)(2,1)S(1)} %get-tuple-element.55), channel_id=1, source_target_pairs={{0,8},{1,9},{2,10},{3,11},{4,12},{5,13},{6,14},{7,15},{8,0},{9,1},... | collective-permute-start | bytes 98312 | tf_op jit(solution)/shard_map/ppermute | solution.py:383
  85.9 15.6 %collective-permute-start.10 = (f32[64,256]{1,0:T(8,128)S(1)}, f32[64,256]{1,0:T(8,128)S(1)}, u32[]{:S(2)}, u32[]{:S(2)}) collective-permute-start(f32[64,256]{1,0:T(8,128)S(1)} %add_add_fusion), channel_id=1, source_target_pairs={{0,24},{1,25},{2,26},{3,27},{4,28},{5,29},{6,30},{7,31},{8,16},{9,... | collective-permute-start | bytes 196616 | tf_op jit(solution)/shard_map/ppermute | solution.py:383
  88.5 14.4 %collective-permute-start.9 = (f32[64,256]{1,0:T(8,128)S(1)}, f32[64,256]{1,0:T(8,128)S(1)}, u32[]{:S(2)}, u32[]{:S(2)}) collective-permute-start(f32[64,256]{1,0:T(8,128)S(1)} %add_add_fusion), channel_id=1, source_target_pairs={{0,16},{1,17},{2,18},{3,19},{4,20},{5,21},{6,22},{7,23},{8,24},{9,... | collective-permute-start | bytes 196616 | tf_op jit(solution)/shard_map/ppermute | solution.py:383
  88.5 7.2 %collective-permute-start.19 = (bf16[16,1024]{1,0:T(8,128)(2,1)S(1)}, bf16[16,1024]{1,0:T(8,128)(2,1)S(1)}, u32[]{:S(2)}, u32[]{:S(2)}) collective-permute-start(bf16[16,1024]{1,0:T(8,128)(2,1)S(1)} %get-tuple-element.55), channel_id=1, source_target_pairs={{0,16},{1,17},{2,18},{3,19},{4,20},{5,21},{6,22},{7,23},{8,24},{9,... | collective-permute-start | bytes 98312 | tf_op jit(solution)/shard_map/ppermute | solution.py:383
  95.7 5.7 %collective-permute-start.20 = (bf16[16,1024]{1,0:T(8,128)(2,1)S(1)}, bf16[16,1024]{1,0:T(8,128)(2,1)S(1)}, u32[]{:S(2)}, u32[]{:S(2)}) collective-permute-start(bf16[16,1024]{1,0:T(8,128)(2,1)S(1)} %get-tuple-element.55), channel_id=1, source_target_pairs={{0,24},{1,25},{2,26},{3,27},{4,28},{5,29},{6,30},{7,31},{8,16},{9,... | collective-permute-start | bytes 98312 | tf_op jit(solution)/shard_map/ppermute | solution.py:383
  101.4 4.3 %collective-permute-start.8 = (f32[64,256]{1,0:T(8,128)S(1)}, f32[64,256]{1,0:T(8,128)S(1)}, u32[]{:S(2)}, u32[]{:S(2)}) collective-permute-start(f32[64,256]{1,0:T(8,128)S(1)} %add_add_fusion), channel_id=1, source_target_pairs={{0,8},{1,9},{2,10},{3,11},{4,12},{5,13},{6,14},{7,15},{8,0},{9,1},... | collective-permute-start | bytes 196616 | tf_op jit(solution)/shard_map/ppermute | solution.py:383
  101.4 7.9 %collective-permute-start.21 = (bf16[64,1024]{1,0:T(8,128)(2,1)S(1)}, bf16[64,1024]{1,0:T(8,128)(2,1)S(1)}, u32[]{:S(2)}, u32[]{:S(2)}) collective-permute-start(bf16[64,1024]{1,0:T(8,128)(2,1)S(1)} %bitcast.90), channel_id=1, source_target_pairs={{0,2},{1,3},{2,0},{3,1},{4,6},{5,7},{6,4},{7,5},{8,10},{9,11},{10,... | collective-permute-start | bytes 393224 | tf_op jit(solution)/shard_map/ppermute | solution.py:383
  106.4 6.4 %collective-permute-start.22 = (bf16[64,1024]{1,0:T(8,128)(2,1)S(1)}, bf16[64,1024]{1,0:T(8,128)(2,1)S(1)}, u32[]{:S(2)}, u32[]{:S(2)}) collective-permute-start(bf16[64,1024]{1,0:T(8,128)(2,1)S(1)} %bitcast.91), channel_id=1, source_target_pairs={{0,4},{1,5},{2,6},{3,7},{4,0},{5,1},{6,2},{7,3},{8,12},{9,13},{10,... | collective-permute-start | bytes 393224 | tf_op jit(solution)/shard_map/ppermute | solution.py:383
  106.4 6.4 %collective-permute-start.23 = (bf16[64,1024]{1,0:T(8,128)(2,1)S(1)}, bf16[64,1024]{1,0:T(8,128)(2,1)S(1)}, u32[]{:S(2)}, u32[]{:S(2)}) collective-permute-start(bf16[64,1024]{1,0:T(8,128)(2,1)S(1)} %bitcast.92), channel_id=1, source_target_pairs={{0,6},{1,7},{2,4},{3,5},{4,2},{5,3},{6,0},{7,1},{8,14},{9,15},{10,... | collective-permute-start | bytes 393224 | tf_op jit(solution)/shard_map/ppermute | solution.py:383
  112.8 14.3 %collective-permute-start.24 = (bf16[256,1024]{1,0:T(8,128)(2,1)S(1)}, bf16[256,1024]{1,0:T(8,128)(2,1)S(1)}, u32[]{:S(2)}, u32[]{:S(2)}) collective-permute-start(bf16[256,1024]{1,0:T(8,128)(2,1)S(1)} %bitcast.87), channel_id=1, source_target_pairs={{0,1},{1,0},{2,3},{3,2},{4,5},{5,4},{6,7},{7,6},{8,9},{9,8},{10,11... | collective-permute-start | bytes 1572872 | tf_op jit(solution)/shard_map/ppermute | solution.py:383
  113.5 0.7 copy-start
  113.5 0.7 copy-start.1

commit v2 on v1

v2 whole, which is shorter than its diff:
```python
import functools
import math

import jax
import jax.numpy as jnp
import numpy as np
from jax import lax
from jax.experimental import pallas as pl
from jax.experimental.pallas import tpu as pltpu
from jax.sharding import PartitionSpec as P

ROOT_TWO_PI = 0.7978845608
CUBIC_TERM = 0.044715
EPSILON = 1e-06

F32 = jnp.float32
BF16 = jnp.bfloat16
LANES = 128
TAPS = 7
RIM = 3
AXES = ("space", "dp")
VMEM_LIMIT = 32 * 1024 * 1024
KEEP = True


def vmem_spec():
    return pl.BlockSpec(memory_space=pltpu.VMEM)


def smem_spec():
    return pl.BlockSpec(memory_space=pltpu.SMEM)


def call(body, outs, ins, scratch=(), smem=0, alias=None, after=(), token=False):
    n_ins = len(ins)
    n_out = len(outs) + token
    outs = list(outs) + [((8, LANES), F32, KEEP)] * token

    def kernel(*refs):
        rest = list(refs[n_ins + len(after) :])
        if token:
            rest.pop(n_out - 1)[...] = jnp.zeros((8, LANES), F32)
        body(*refs[:n_ins], *rest)

    res = pl.pallas_call(
        kernel,
        out_shape=tuple(pltpu.VMEM(o[0], o[1]) if len(o) > 2 else jax.ShapeDtypeStruct(o[0], o[1]) for o in outs),
        in_specs=[smem_spec()] * smem + [vmem_spec()] * (n_ins - smem + len(after)),
        out_specs=tuple(vmem_spec() for _ in outs),
        scratch_shapes=list(scratch),
        input_output_aliases=alias or {},
        compiler_params=pltpu.CompilerParams(vmem_limit_bytes=VMEM_LIMIT),
    )(*[placed(v) for v in (*ins, *after)])
    return tuple(Kept(r) if len(o) > 2 else r for r, o in zip(res, outs))


def placed(v):
    if isinstance(v, Kept):
        return pltpu.with_memory_space_constraint(v.value, pltpu.VMEM)
    if isinstance(v, Far):
        return pltpu.with_memory_space_constraint(v.value, pltpu.HBM)
    return v


class Far:
    def __init__(self, value):
        self.value = value


class Kept:
    def __init__(self, value):
        self.value = value


def slot_pick(nbr_ref, which):
    slots = nbr_ref.shape[0]
    row = lax.broadcasted_iota(jnp.int32, (slots, LANES), 0)
    ids = jnp.full((slots, LANES), -1, jnp.int32)
    for t in range(slots):
        ids = jnp.where(row == t, nbr_ref[t, which], ids)
    present = ids >= 0
    return jnp.where(present, lax.rem(ids, slots), 0), present


def take(v, pick):
    ids, present = pick
    return jnp.where(present, jnp.take_along_axis(v, ids, axis=0, mode="promise_in_bounds"), 0.0)


def lanes(h):
    return slice(h * LANES, (h + 1) * LANES)


def pad_col(pads, h, r, c):
    west, center, east = pads
    if c < RIM:
        return west[h, r, c * 8 : c * 8 + 8, :]
    c -= RIM
    if c < 16:
        return center[h, r, c * 8 : c * 8 + 8, :]
    c -= 16
    return east[h, r, c * 8 : c * 8 + 8, :]


def spread_taps(k_ref, k8_ref, flip):
    for h in range(2):
        for tap in range(TAPS * TAPS):
            i, j = divmod(TAPS * TAPS - 1 - tap if flip else tap, TAPS)
            k8_ref[h, tap] = jnp.broadcast_to(k_ref[i, j : j + 1, lanes(h)], (8, LANES))


def conv_wide(pads, k8_ref, h, r, c0, n):
    accs = [None] * n
    for i in range(TAPS):
        xs = [pad_col(pads, h, r + i, c0 + c) for c in range(n + TAPS - 1)]
        for j in range(TAPS):
            kk = k8_ref[h, i * TAPS + j]
            for c in range(n):
                term = xs[c + j] * kk
                accs[c] = term if accs[c] is None else accs[c] + term
    return accs


def conv_tall(pads, k8_ref, h, r0, rows, c0, n):
    accs = [[None] * n for _ in range(rows)]
    for j in range(TAPS):
        ks = [k8_ref[h, i * TAPS + j] for i in range(TAPS)]
        for p in range(rows + TAPS - 1):
            xs = [pad_col(pads, h, r0 + p, c0 + j + c) for c in range(n)]
            for q in range(max(0, p - TAPS + 1), min(rows, p + 1)):
                for c in range(n):
                    term = xs[c] * ks[p - q]
                    accs[q][c] = term if accs[q][c] is None else accs[q][c] + term
    return accs


def gelu_pair(pre):
    sq = pre * pre
    t = jnp.tanh(pre * (ROOT_TWO_PI + (ROOT_TWO_PI * CUBIC_TERM) * sq))
    half = 0.5 + 0.5 * t
    act = pre * half
    slope = half + act * (1.0 - t) * (ROOT_TWO_PI + (3.0 * ROOT_TWO_PI * CUBIC_TERM) * sq)
    return act, slope


def fold(v):
    return jnp.sum(v.reshape(v.shape[0] // 8, 8, v.shape[1]), axis=0)


def dot(a, b):
    return jnp.dot(a, b, preferred_element_type=F32)


def dot_t(a, b):
    return lax.dot_general(a, b, (((1,), (1,)), ((), ())), preferred_element_type=F32)


def dense_block(conv, x, dy, params, add_dw, sums_ref):
    win, wout, bias_in, bias_out, scale, gain, shift, conv_bias = params
    hidden = win.shape[1]
    channels = win.shape[0]
    conv = conv + conv_bias[...]
    centred = conv - jnp.mean(conv, axis=1, keepdims=True)
    inv_std = lax.rsqrt(jnp.mean(centred * centred, axis=1, keepdims=True) + EPSILON)
    normed = centred * inv_std
    unit = (normed * gain[...] + shift[...]).astype(BF16)
    gb = (dy * scale[...]).astype(BF16)
    unit_t = unit.T
    gb_t = gb.T
    branch = jnp.zeros(conv.shape, F32)
    grad_unit = jnp.zeros(conv.shape, F32)
    for k in range(0, hidden, 256):
        ks = slice(k, k + 256)
        pre = dot(unit, win[:, ks]) + bias_in[:, ks]
        act, slope = gelu_pair(pre)
        act = act.astype(BF16)
        gp = (dot_t(gb, wout[ks, :]) * slope).astype(BF16)
        branch = branch + dot(act, wout[ks, :])
        grad_unit = grad_unit + dot_t(gp, win[:, ks])
        add_dw(0, k, dot(unit_t, gp))
        add_dw(1, k, dot(gb_t, act))
        sums_ref[k // 256] += fold(gp.astype(F32))
    branch = branch + bias_out[...]
    out = x + scale[...] * branch
    scaled = grad_unit * gain[...]
    grad_conv = inv_std * (
        scaled
        - jnp.mean(scaled, axis=1, keepdims=True)
        - normed * jnp.mean(scaled * normed, axis=1, keepdims=True)
    )
    grad_conv = grad_conv.astype(BF16).astype(F32)
    nk = hidden // 256
    sums_ref[nk] += fold(gb.astype(F32))
    sums_ref[nk + 1] += fold(dy * branch)
    sums_ref[nk + 2] += fold(grad_unit * normed)
    sums_ref[nk + 3] += fold(grad_unit)
    sums_ref[nk + 4] += fold(grad_conv)
    return out, grad_conv


def rows_of(ref, r0, nr, c0, n):
    blocks = []
    for q in range(nr):
        blocks.append(jnp.concatenate([ref[h, r0 + q, c0 * 8 : (c0 + n) * 8, :] for h in range(2)], axis=1))
    return jnp.concatenate(blocks, axis=0)


def rims_of(center_ref, nbr_ref):
    north = slot_pick(nbr_ref, 0)
    south = slot_pick(nbr_ref, 1)
    for h in range(2):
        for q in range(RIM):
            for c in range(16):
                cs = slice(c * 8, c * 8 + 8)
                center_ref[h, q, cs, :] = take(center_ref[h, 16 + q, cs, :], north)
                center_ref[h, 19 + q, cs, :] = take(center_ref[h, 3 + q, cs, :], south)


def side_rim(side_ref, halo_ref, nbr_ref, straight, up, down):
    mid, top, low = (slot_pick(nbr_ref, w) for w in (straight, up, down))
    for h in range(2):
        for pair in range(24):
            v = halo_ref[pair * 16 : pair * 16 + 16, lanes(h)].astype(F32)
            for s in range(2):
                r, c = divmod(pair * 2 + s, RIM)
                cs = slice(c * 8, c * 8 + 8)
                part = v[s * 8 : s * 8 + 8]
                side_ref[h, 3 + r, cs, :] = take(part, mid)
                if r >= 13:
                    side_ref[h, r - 13, cs, :] = take(part, top)
                if r < 3:
                    side_ref[h, 19 + r, cs, :] = take(part, low)


def inner_kernel(
    nbr_ref, cnt_ref, place_ref, x_ref, dy_ref, k_ref, win, wout, bias_in, bias_out, scale, gain, shift, conv_bias,
    center_ref, dyt_ref, out_ref, g_ref, dw_ref, sums_ref,
    k8_ref, conv_ref,
):
    live = cnt_ref[0]
    channels = win.shape[0]
    spread_taps(k_ref, k8_ref, False)
    dw_ref[...] = jnp.zeros(dw_ref.shape, F32)
    sums_ref[...] = jnp.zeros(sums_ref.shape, F32)

    def turn(r, carry):
        for t in range(8):
            for h in range(2):
                center_ref[h, 3 + r, pl.ds(t, 16, stride=8), :] = x_ref[t, r, :, lanes(h)].astype(F32)
                dyv = dy_ref[t, r, :, lanes(h)].astype(F32)
                dyt_ref[h, r, pl.ds(t, 16, stride=8), :] = jnp.where(t < live, dyv, 0.0)
        return carry

    lax.fori_loop(0, 16, turn, 0)
    rims_of(center_ref, nbr_ref)
    params = (win, wout, bias_in, bias_out, scale, gain, shift, conv_bias)
    nr, n, c0 = 4, 10, 3
    cols = slice(c0 * 8, (c0 + n) * 8)
    pads = (None, center_ref, None)

    def add_dw(which, k, v):
        dw_ref[which * channels : (which + 1) * channels, k : k + 256] += v

    def block(m, carry):
        r0 = m * nr

        def conv(q, carry):
            for h in range(2):
                accs = conv_wide(pads, k8_ref, h, r0 + q, c0, n)
                conv_ref[pl.ds(pl.multiple_of(q * n * 8, 8), n * 8), lanes(h)] = jnp.concatenate(accs, axis=0)
            return carry

        lax.fori_loop(0, nr, conv, 0)
        x = rows_of(center_ref, r0 + 3, nr, c0, n)
        dy = rows_of(dyt_ref, r0, nr, c0, n)
        out, g = dense_block(conv_ref[...], x, dy, params, add_dw, sums_ref)
        for q in range(nr):
            for h in range(2):
                out_ref[h, r0 + q, cols, :] = out[q * n * 8 : (q + 1) * n * 8, lanes(h)]
                g_ref[h, 3 + r0 + q, cols, :] = g[q * n * 8 : (q + 1) * n * 8, lanes(h)]
        return carry

    lax.fori_loop(0, 16 // nr, block, 0)


def edge_kernel(
    nbr_ref, core_ref, hw_ref, he_ref, center_ref, dyt_ref, dw_in, sums_in, out_in, g_in,
    k_ref, win, wout, bias_in, bias_out, scale, gain, shift, conv_bias,
    west_ref, east_ref, out_ref, g_ref, send_l, send_r, own_ref, sent_ref, sums_ref,
    k8_ref, conv_ref, dw_ref,
):
    core = core_ref[0]
    channels = win.shape[0]
    hidden = win.shape[1]
    spread_taps(k_ref, k8_ref, False)
    sums_ref[...] = sums_in[...]
    side_rim(west_ref, hw_ref, nbr_ref, 2, 4, 6)
    side_rim(east_ref, he_ref, nbr_ref, 3, 5, 7)
    params = (win, wout, bias_in, bias_out, scale, gain, shift, conv_bias)
    pads = (west_ref, center_ref, east_ref)
    nr = 8
    n_blocks = 16 // nr

    for m in range(n_blocks):
        r0 = m * nr
        src, last = (dw_in, m == n_blocks - 1) if m == 0 else (dw_ref, m == n_blocks - 1)

        def add_dw(which, k, v, src=src, last=last):
            at = slice(which * channels, (which + 1) * channels), slice(k, k + 256)
            v = src[at] + v
            if not last:
                dw_ref[at] = v
                return
            if which == 1:
                v = v.T
            v = v.astype(BF16)
            for side in range(2):
                row = k * 2 + side * 256 if which == 0 else side * hidden + k
                piece = v[:, lanes(side)]

                @pl.when(core == which)
                def _():
                    own_ref[row : row + 256, :] = piece

                @pl.when(core != which)
                def _():
                    sent_ref[row : row + 256, :] = piece

        for h in range(2):
            for side, c0 in enumerate((0, 13)):
                accs = conv_tall(pads, k8_ref, h, r0, nr, c0, RIM)
                for q in range(nr):
                    base = (q * 2 + side) * 24
                    conv_ref[base : base + 24, lanes(h)] = jnp.concatenate(accs[q], axis=0)
        xs, dys = [], []
        for q in range(nr):
            for c0 in (0, 13):
                xs.append(rows_of(center_ref, r0 + 3 + q, 1, c0, RIM))
                dys.append(rows_of(dyt_ref, r0 + q, 1, c0, RIM))
        x = jnp.concatenate(xs, axis=0)
        dy = jnp.concatenate(dys, axis=0)
        out, g = dense_block(conv_ref[...], x, dy, params, add_dw, sums_ref)
        for q in range(nr):
            for side, c0 in enumerate((0, 13)):
                part = slice((q * 2 + side) * 24, (q * 2 + side) * 24 + 24)
                cols = slice(c0 * 8, c0 * 8 + 24)
                for h in range(2):
                    out_ref[h, r0 + q, cols, :] = out[part, lanes(h)]
                    g_ref[h, 3 + r0 + q, cols, :] = g[part, lanes(h)]
        for q in range(0, nr, 2):
            for side, send in enumerate((send_l, send_r)):
                v = jnp.concatenate(
                    [g[(q + s) * 48 + side * 24 : (q + s) * 48 + side * 24 + 24] for s in range(2)], axis=0
                )
                send[(r0 + q) * 24 : (r0 + q) * 24 + 48, :] = v.astype(BF16)


def turn_out(out_ref, src_ref, live, r):
    for t in range(8):
        for h in range(2):
            v = src_ref[h, r, pl.ds(t, 16, stride=8), :]
            out_ref[t, r, :, lanes(h)] = jnp.where(t < live, v, 0.0).astype(BF16)


def tiles_kernel(nbr_ref, cnt_ref, full_ref, g_in, out_ref, g_ref):
    live = cnt_ref[0]
    rims_of(g_ref, nbr_ref)

    def row(r, carry):
        turn_out(out_ref, full_ref, live, r)
        return carry

    lax.fori_loop(0, 16, row, 0)


def tap_kernel(h, center_ref, west_ref, east_ref, g_ref, acc_ref):
    pads = (west_ref, center_ref, east_ref)

    def row_tap(i, carry):
        def row(r, accs):
            g = [g_ref[h, 3 + r, c * 8 : c * 8 + 8, :] for c in range(16)]
            xs = [pad_col(pads, h, r + i, c) for c in range(22)]
            new = []
            for j in range(TAPS):
                terms = [xs[c + j] * g[c] for c in range(16)]
                while len(terms) > 1:
                    terms = [a + b for a, b in zip(terms[::2], terms[1::2])]
                new.append(accs[j] + terms[0])
            return tuple(new)

        accs = lax.fori_loop(0, 16, row, tuple(jnp.zeros((8, LANES), F32) for _ in range(TAPS)))
        for j in range(TAPS):
            acc_ref[i * TAPS + j] = accs[j]
        return carry

    lax.fori_loop(0, TAPS, row_tap, 0)


def small_kernel(tap0, tap1, sums, small_ref):
    ns = sums.shape[0]
    small_ref[...] = jnp.zeros(small_ref.shape, F32)
    small_ref[0:ns, :] = jnp.sum(sums[...], axis=1)
    small_ref[ns : ns + 49, lanes(0)] = jnp.sum(tap0[...], axis=1)
    small_ref[ns : ns + 49, lanes(1)] = jnp.sum(tap1[...], axis=1)


def sides_kernel(nbr_ref, hw_ref, he_ref, west_ref, east_ref):
    side_rim(west_ref, hw_ref, nbr_ref, 2, 4, 6)
    side_rim(east_ref, he_ref, nbr_ref, 3, 5, 7)


def back_kernel(first, last, cnt_ref, west_ref, east_ref, g_ref, dyt_ref, k_ref, *refs):
    gx_ref, full_ref, k8_ref = refs[-3:]
    live = cnt_ref[0]
    spread_taps(k_ref, k8_ref, True)
    pads = (west_ref, g_ref, east_ref)

    def row(r, carry):
        for h in range(2):
            accs = conv_wide(pads, k8_ref, h, r, 0, 16)
            for c in range(16):
                cs = slice(c * 8, c * 8 + 8)
                full_ref[h, r, cs, :] = accs[c] + dyt_ref[h, r, cs, :]
        turn_out(gx_ref, full_ref, live, r)
        return carry

    lax.fori_loop(first, last, row, 0)


def scatter_kernel(level, size, mine_ref, *refs):
    n_out = size
    held, outs = refs[:-n_out], refs[-n_out:]
    total = held[0][...].astype(F32)
    for h in held[1:]:
        total = total + h[...].astype(F32)
    total = total.astype(BF16)
    rows = total.shape[0] // size
    if size == 1:
        outs[0][...] = total
        return
    mine = mine_ref[level]
    for p in range(size):
        piece = total[p * rows : (p + 1) * rows]
        for k in range(size):

            @pl.when((mine ^ k) == p)
            def _(k=k, piece=piece):
                outs[k][...] = piece


def gather_kernel(level, size, mine_ref, *refs):
    parts, out = refs[:-1], refs[-1]
    rows = parts[0].shape[0]
    mine = mine_ref[level]
    for k in range(size):
        out[pl.ds(pl.multiple_of((mine ^ k) * rows, 16), rows), :] = parts[k][...]


def last_kernel(factor, core_ref, own_ref, other_ref, win_ref, wout_ref):
    core = core_ref[0]
    hidden = wout_ref.shape[0]

    def put_in(ref):
        for b in range(hidden // LANES):
            win_ref[:, b * LANES : (b + 1) * LANES] = ref[b * 256 : b * 256 + 256, :].astype(F32) * factor

    def put_out(ref):
        for side in range(2):
            wout_ref[:, lanes(side)] = ref[side * hidden : (side + 1) * hidden, :].astype(F32) * factor

    @pl.when(core == 0)
    def _():
        put_in(own_ref)
        put_out(other_ref)

    @pl.when(core != 0)
    def _():
        put_in(other_ref)
        put_out(own_ref)


def shifted(block, axis, distance):
    n = lax.axis_size(axis)
    return lax.ppermute(block, axis, [((i - distance) % n, i) for i in range(n)])


def crossed(v, mask):
    n = lax.axis_size(AXES)
    return lax.ppermute(v, AXES, [(i, i ^ mask) for i in range(n)])


def groups():
    total = lax.axis_size(AXES)
    found, bit = [(1, 2)], 2
    while bit < total:
        size = min(4, total // bit)
        found.append((bit, size))
        bit *= size
    return found


def on_device(
    activations, cotangent, tile_count, neighbours, conv_kernel, conv_bias, norm_gain, norm_bias,
    proj_in, bias_in, proj_out, bias_out, layer_scale,
):
    x = activations[0]
    dy = cotangent[0]
    slots, edge, _, channels = x.shape
    hidden = proj_in.shape[1]
    row = lambda v: v.reshape(1, -1)
    weights = (
        proj_in, proj_out, row(bias_in), row(bias_out), row(layer_scale), row(norm_gain), row(norm_bias),
        row(conv_bias),
    )
    weights = tuple(Far(w) for w in weights)
    conv_kernel = Far(conv_kernel)
    places = np.array([[(d // bit) % size for bit, size in groups()] for d in range(lax.axis_size(AXES))], np.int32)
    place = lax.dynamic_index_in_dim(jnp.asarray(places), lax.axis_index(AXES), 0, keepdims=False)

    def columns(lo):
        return x[:, :, lo : lo + RIM].transpose(1, 2, 0, 3).reshape(edge * RIM * slots, channels)

    from_east = shifted(columns(0), "space", -1)
    from_west = shifted(columns(edge - RIM), "space", 1)
    ns = hidden // 256 + 5
    half = (2, edge, edge * slots, LANES)
    k8 = pltpu.VMEM((2, TAPS * TAPS, 8, LANES), F32)
    side = (2, edge + 2 * RIM, RIM * slots, LANES)
    tall = (2, edge + 2 * RIM, edge * slots, LANES)
    halo = (edge * RIM * slots, channels)
    dw_shape = (2 * channels, hidden)
    sums_shape = (ns, 8, channels)
    tiles = (slots, edge, edge, channels)
    travel = (channels * hidden // LANES, LANES)

    center, dyt, full, g, dw, sums = call(
        inner_kernel,
        [(tall, F32, KEEP), (half, F32, KEEP), (half, F32, KEEP), (tall, F32, KEEP), (dw_shape, F32, KEEP),
         (sums_shape, F32, KEEP)],
        (neighbours, tile_count, place, Far(x), Far(dy), conv_kernel) + weights,
        [k8, pltpu.VMEM((4 * 10 * slots, channels), F32)],
        smem=3,
    )
    west, east, full, g, send_l, send_r, held, sent, sums = call(
        edge_kernel,
        [(side, F32, KEEP), (side, F32, KEEP), (half, F32, KEEP), (tall, F32, KEEP), (halo, BF16), (halo, BF16),
         (travel, BF16), (travel, BF16), (sums_shape, F32, KEEP)],
        (neighbours, place, from_west, from_east, center, dyt, dw, sums, full, g, conv_kernel) + weights,
        [k8, pltpu.VMEM((8 * 6 * slots, channels), F32), pltpu.VMEM(dw_shape, F32)],
        smem=2,
        alias={8: 2, 9: 3},
    )
    later = groups()[1:]
    arrived = [crossed(sent, 1)]
    grad_from_east = shifted(send_l, "space", -1)
    grad_from_west = shifted(send_r, "space", 1)

    out_tiles, g, done = call(
        tiles_kernel, [(tiles, BF16), (tall, F32, KEEP)], (neighbours, tile_count, full, g), smem=2, alias={3: 1},
        token=True,
    )
    filler = (done,)
    taps = []

    def tap(h):
        v, done = call(
            functools.partial(tap_kernel, h), [((TAPS * TAPS, 8, LANES), F32, KEEP)], (center, west, east, g),
            after=(begun,), token=True,
        )
        taps.append(v)
        return done

    for n, (bit, size) in enumerate(later):
        level = n + 1
        held, *parts, begun = call(
            functools.partial(scatter_kernel, level, size),
            [((held.shape[0] // size, LANES), BF16)] * size,
            (place, held, *arrived),
            smem=1,
            after=filler,
            token=True,
        )
        arrived = [crossed(p, k * bit) for k, p in enumerate(parts, 1)]
        filler = (tap(n),) if n < 2 else ()
    small, done = call(small_kernel, [((64, channels), F32)], (*taps, sums), after=filler, token=True)
    held, begun = call(
        functools.partial(scatter_kernel, 0, 1), [(held.shape, BF16)], (place, held, *arrived), smem=1, after=(done,),
        token=True,
    )

    sides = None
    gx = None
    for n, (bit, size) in enumerate(later[::-1]):
        level = len(later) - n
        parts = [held] + [crossed(held, k * bit) for k in range(1, size)]
        small = sum((crossed(small, k * bit) for k in range(1, size)), small)
        filler = ()
        if n < 2:
            if n == 0:
                sides = call(
                    sides_kernel, [(side, F32, KEEP)] * 2, (neighbours, grad_from_west, grad_from_east), smem=1,
                    after=(begun,),
                )
            gx, done = call(
                functools.partial(back_kernel, n * edge // 2, (n + 1) * edge // 2),
                [(tiles, BF16, KEEP)],
                (tile_count, *sides, g, dyt, conv_kernel) + ((gx,) if n else ()),
                [pltpu.VMEM(half, F32), k8],
                smem=1,
                alias={6: 0} if n else None,
                after=(begun,),
                token=True,
            )
            filler = (done,)
        held, begun = call(
            functools.partial(gather_kernel, level, size), [((held.shape[0] * size, LANES), BF16)],
            (place, *parts), smem=1, after=filler, token=True,
        )
    small = small + crossed(small, 1)
    factor = 1.0 / math.sqrt(lax.axis_size("dp") * lax.axis_size("space") * slots * edge * edge)
    grad_in, grad_out = call(
        functools.partial(last_kernel, factor),
        [((channels, hidden), F32), ((hidden, channels), F32)],
        (place, held, crossed(held, 1)),
        smem=1,
    )
    small = small * factor
    nk = hidden // 256
    return (
        out_tiles[None],
        gx.value[None],
        small[ns : ns + 49].reshape(TAPS, TAPS, channels),
        small[nk + 4],
        small[nk + 2],
        small[nk + 3],
        grad_in,
        small[:nk].reshape(-1),
        grad_out,
        small[nk],
        small[nk + 1],
    )


def solution(mesh):
    tiles = P("dp", "space", None, None, None)
    return jax.shard_map(
        on_device,
        mesh=mesh,
        in_specs=(tiles, tiles, P("space"), P("space", None)) + (P(),) * 9,
        out_specs=(tiles, tiles) + (P(),) * 9,
        check_vma=False,
    )
```

time: 130 us -> 106 us (0.82)
  waiting for transfers between devices: 20 us -> 8.26 us
  local copies, waits for them, and re-layouts: 9.43 us -> 5.93 us
  other arithmetic: 3.21 us -> 0.05 us
  Pallas kernels: 60.6 us -> 57.6 us
  starting transfers between devices: 35 us -> 32.3 us
    ppermute x21, waiting for transfers between devices: 20 us -> 5.62 us  [crossed(): return lax.ppermute(v, AXES, [(i, i ^ mask) for i in range(n)])]
    pallas_call x4 -> x15, Pallas kernels: 60.6 us -> 57.6 us  [call(): pl.pallas_call(kernel, out_shape=tuple((pltpu.VMEM(o[0], o[1]) if len(o)...]
    ppermute x4, waiting for transfers between devices: 0.01 us -> 2.65 us  [shifted(): lax.ppermute(block, axis, [((i - distance) % n, i) for i in range(n)])]
    ppermute x21, starting transfers between devices: 24.1 us -> 21.8 us  [crossed(): return lax.ppermute(v, AXES, [(i, i ^ mask) for i in range(n)])]
    convert_element_type x3 -> x0, other arithmetic: 2.03 us -> none  [the longest x1 1.75 us: on_device(): dw = reduce_all(dw.astype(BF16))]
    reshape x1 -> x0, local copies, waits for them, and re-layouts: 1.44 us -> none  [on_device(): taps = conv_kernel.reshape(TAPS * TAPS, channels)]
    unnamed x15 -> x7, local copies, waits for them, and re-layouts: 3.41 us -> 2.26 us
  transfers between devices with their start and end apart: 25 -> 25, of which waited for: 7 -> 5; matrix products, arithmetic and copies ran while one was open for 4% -> 3% of each run, Pallas kernels for 35% -> 39%
where the time goes in v2:
time: 106 us
  Pallas kernels  57.6 us (54%)
  starting transfers between devices  32.3 us (30%)
  waiting for transfers between devices  8.26 us (8%)
  local copies, waits for them, and re-layouts  5.93 us (6%)
  between operations  1.54 us (1%)
    pallas_call x15, Pallas kernels, call(): pl.pallas_call(kernel, out_shape=tuple((pltpu.VMEM(o[0], o[1]) if len(o)...  57.6 us
    ppermute x21, starting transfers between devices, crossed(): return lax.ppermute(v, AXES, [(i, i ^ mask) for i in range(n)])  21.8 us
    ppermute x4, starting transfers between devices, shifted(): lax.ppermute(block, axis, [((i - distance) % n, i) for i in range(n)])  10.5 us
    ppermute x21, waiting for transfers between devices, crossed(): return lax.ppermute(v, AXES, [(i, i ^ mask) for i in range(n)])  5.62 us
    ppermute x4, waiting for transfers between devices, shifted(): lax.ppermute(block, axis, [((i - distance) % n, i) for i in range(n)])  2.65 us
    unnamed x7, local copies, waits for them, and re-layouts  2.26 us
  transfers between devices with their start and end apart: 25, of which 5 were waited for; matrix products, arithmetic and copies ran while one was open for 3% of the time, Pallas kernels for 39%

profile of v2, /device:TPU:0, one launch (start us, length us, event | category | flops | bytes accessed | tf_op | source)
XLA Modules:
  0.0 105.7 jit_solution(16716787832907878331)
XLA Ops:
  0.6 1.5 %slice_bitcast_fusion = (bf16[16,3,8,256]{3,1,0,2:T(4,128)(2,1)S(1)}, bf16[16,3,8,256]{3,1,0,2:T(4,128)(2,1)S(1)}) fusion(bf16[8,16,16,256]{3,2,1,0:T(8,128)(2,1)} %bitcast.27), kind=kLoop, calls=%fused_computation | loop fusion | bytes 786432 | tf_op jit(solution)/shard_map/transpose | solution.py:521
  2.3 3.0 %collective-permute-start = (bf16[384,256]{1,0:T(8,128)(2,1)S(1)}, bf16[384,256]{1,0:T(8,128)(2,1)S(1)}, u32[]{:S(2)}, u32[]{:S(2)}) collective-permute-start(bf16[384,256]{1,0:T(8,128)(2,1)S(1)} %bitcast.30), channel_id=1, source_target_pairs={{28,0},{0,4},{4,8},{8,12},{12,16},{16,20},{20,24},{24,28},{29,1},{... | collective-permute-start | bytes 589832 | tf_op jit(solution)/shard_map/ppermute | solution.py:484
  5.4 3.1 %collective-permute-start.1 = (bf16[384,256]{1,0:T(8,128)(2,1)S(1)}, bf16[384,256]{1,0:T(8,128)(2,1)S(1)}, u32[]{:S(2)}, u32[]{:S(2)}) collective-permute-start(bf16[384,256]{1,0:T(8,128)(2,1)S(1)} %bitcast.31), channel_id=1, source_target_pairs={{4,0},{8,4},{12,8},{16,12},{20,16},{24,20},{28,24},{0,28},{5,1},{9... | collective-permute-start | bytes 589832 | tf_op jit(solution)/shard_map/ppermute | solution.py:484
  10.6 18.2 %shard_map.221 = (f32[2,22,128,128]{3,2,1,0:T(8,128)S(1)}, f32[2,16,128,128]{3,2,1,0:T(8,128)S(1)}, f32[2,16,128,128]{3,2,1,0:T(8,128)S(1)}, f32[2,22,128,128]{3...) custom-call(s32[8,8]{1,0:T(8,128)S(1)} %copy-done, s32[1]{0:T(128)S(6)} %copy.37.refs_1_.refs_0_, ...), custom_call_target="tpu_custom_call" | custom-call | tf_op jit(solution)/shard_map/pallas_call | solution.py:45
  28.8 12.9 %shard_map.222 = (f32[2,22,24,128]{3,2,1,0:T(8,128)S(1)}, f32[2,22,24,128]{3,2,1,0:T(8,128)S(1)}, f32[2,16,128,128]{3,2,1,0:T(8,128)S(1)}, f32[2,22,128,128]{3,2...) custom-call(s32[8,8]{1,0:T(8,128)S(1)} %copy-done, ...), custom_call_target="tpu_custom_call", output_to_operand_aliasing={{2}: (8, {}), {3}: (9, {})} | custom-call | tf_op jit(solution)/shard_map/pallas_call | solution.py:45
  41.8 2.2 %shard_map.223 = (bf16[8,16,16,256]{3,2,1,0:T(8,128)(2,1)}, f32[2,22,128,128]{3,2,1,0:T(8,128)S(1)}, f32[8,128]{1,0:T(8,128)S(1)}) custom-call(s32[8,8]{1,0:T(8,128)S(1)} %copy-done, s32[1]{0:T(128)S(6)} %copy.37.refs_1_.refs_0_, f32[2,16,128,128]{3,2,1,0:T(8,128)S(1)} %get-tuple-element.64.refs_2_, ...), custom_call_target="tpu_custom_call", output_to_operand_aliasing={{1}: (3, {})} | custom-call | tf_op jit(solution)/shard_map/pallas_call | solution.py:45
  44.0 0.9 shard_map.224
  44.9 1.7 %collective-permute-start.5 = (bf16[512,128]{1,0:T(8,128)(2,1)S(1)}, bf16[512,128]{1,0:T(8,128)(2,1)S(1)}, u32[]{:S(2)}, u32[]{:S(2)}) collective-permute-start(bf16[512,128]{1,0:T(8,128)(2,1)S(1)} %get-tuple-element.73), channel_id=1, source_target_pairs={{0,2},{1,3},{2,0},{3,1},{4,6},{5,7},{6,4},{7,5},{8,10},{9,11},{10,... | collective-permute-start | bytes 393224 | tf_op jit(solution)/shard_map/ppermute | solution.py:489
  46.6 1.8 %collective-permute-start.7 = (bf16[512,128]{1,0:T(8,128)(2,1)S(1)}, bf16[512,128]{1,0:T(8,128)(2,1)S(1)}, u32[]{:S(2)}, u32[]{:S(2)}) collective-permute-start(bf16[512,128]{1,0:T(8,128)(2,1)S(1)} %get-tuple-element.75), channel_id=1, source_target_pairs={{0,6},{1,7},{2,4},{3,5},{4,2},{5,3},{6,0},{7,1},{8,14},{9,15},{10,... | collective-permute-start | bytes 393224 | tf_op jit(solution)/shard_map/ppermute | solution.py:489
  48.5 4.4 %shard_map.225 = (f32[49,8,128]{2,1,0:T(8,128)S(1)}, f32[8,128]{1,0:T(8,128)S(1)}) custom-call(f32[2,22,128,128]{3,2,1,0:T(8,128)S(1)} %get-tuple-element.58.refs_4_.refs_0_, f32[2,22,24,128]{3,2,1,0:T(8,128)S(1)} %get-tuple-element.76.refs_1_, f32[2,22,24,128]{3,2,1,0:T(8,128)S(1)} %get-tuple-element.77.refs_2_, ...), custom_call_target="tpu_custom_call" | custom-call | tf_op jit(solution)/shard_map/pallas_call | solution.py:45
  52.9 2.2 %collective-permute-done.6.refs_3_ = bf16[512,128]{1,0:T(8,128)(2,1)S(1)} collective-permute-done((bf16[512,128]{1,0:T(8,128)(2,1)S(1)}, bf16[512,128]{1,0:T(8,128)(2,1)S(1)}, u32[]{:S(2)}, u32[]{:S(2)}) %collective-permute-start.6) | collective-permute-done | bytes 131104 | tf_op jit(solution)/shard_map/ppermute | solution.py:489
  55.8 4.3 %shard_map.227 = (f32[49,8,128]{2,1,0:T(8,128)S(1)}, f32[8,128]{1,0:T(8,128)S(1)}) custom-call(f32[2,22,128,128]{3,2,1,0:T(8,128)S(1)} %get-tuple-element.58.refs_4_.refs_0_, f32[2,22,24,128]{3,2,1,0:T(8,128)S(1)} %get-tuple-element.76.refs_1_, f32[2,22,24,128]{3,2,1,0:T(8,128)S(1)} %get-tuple-element.77.refs_2_, ...), custom_call_target="tpu_custom_call" | custom-call | tf_op jit(solution)/shard_map/pallas_call | solution.py:45
  60.3 2.3 %collective-permute-start.16 = (f32[64,256]{1,0:T(8,128)S(1)}, f32[64,256]{1,0:T(8,128)S(1)}, u32[]{:S(2)}, u32[]{:S(2)}) collective-permute-start(f32[64,256]{1,0:T(8,128)S(1)} %get-tuple-element.99), channel_id=1, source_target_pairs={{0,24},{1,25},{2,26},{3,27},{4,28},{5,29},{6,30},{7,31},{8,16},{9,... | collective-permute-start | bytes 196616 | tf_op jit(solution)/shard_map/ppermute | solution.py:489
  62.6 1.2 %collective-permute-start.15 = (f32[64,256]{1,0:T(8,128)S(1)}, f32[64,256]{1,0:T(8,128)S(1)}, u32[]{:S(2)}, u32[]{:S(2)}) collective-permute-start(f32[64,256]{1,0:T(8,128)S(1)} %get-tuple-element.99), channel_id=1, source_target_pairs={{0,16},{1,17},{2,18},{3,19},{4,20},{5,21},{6,22},{7,23},{8,24},{9,... | collective-permute-start | bytes 196616 | tf_op jit(solution)/shard_map/ppermute | solution.py:489
  63.8 0.9 collective-permute-start.14
  64.8 1.4 %collective-permute-start.9 = (bf16[128,128]{1,0:T(8,128)(2,1)S(1)}, bf16[128,128]{1,0:T(8,128)(2,1)S(1)}, u32[]{:S(2)}, u32[]{:S(2)}) collective-permute-start(bf16[128,128]{1,0:T(8,128)(2,1)S(1)} %get-tuple-element.83), channel_id=1, source_target_pairs={{0,16},{1,17},{2,18},{3,19},{4,20},{5,21},{6,22},{7,23},{8,24},{9,... | collective-permute-start | bytes 98312 | tf_op jit(solution)/shard_map/ppermute | solution.py:489
  66.2 2.0 %collective-permute-start.10 = (bf16[128,128]{1,0:T(8,128)(2,1)S(1)}, bf16[128,128]{1,0:T(8,128)(2,1)S(1)}, u32[]{:S(2)}, u32[]{:S(2)}) collective-permute-start(bf16[128,128]{1,0:T(8,128)(2,1)S(1)} %get-tuple-element.84), channel_id=1, source_target_pairs={{0,24},{1,25},{2,26},{3,27},{4,28},{5,29},{6,30},{7,31},{8,16},{9,... | collective-permute-start | bytes 98312 | tf_op jit(solution)/shard_map/ppermute | solution.py:489
  68.2 3.0 %collective-permute-done.9.refs_3_ = bf16[128,128]{1,0:T(8,128)(2,1)S(1)} collective-permute-done((bf16[128,128]{1,0:T(8,128)(2,1)S(1)}, bf16[128,128]{1,0:T(8,128)(2,1)S(1)}, u32[]{:S(2)}, u32[]{:S(2)}) %collective-permute-start.9) | collective-permute-done | bytes 32800 | tf_op jit(solution)/shard_map/ppermute | solution.py:489
  71.9 4.0 %collective-permute-start.3 = (bf16[384,256]{1,0:T(8,128)(2,1)S(1)}, bf16[384,256]{1,0:T(8,128)(2,1)S(1)}, u32[]{:S(2)}, u32[]{:S(2)}) collective-permute-start(bf16[384,256]{1,0:T(8,128)(2,1)S(1)} %get-tuple-element.68), channel_id=1, source_target_pairs={{4,0},{8,4},{12,8},{16,12},{20,16},{24,20},{28,24},{0,28},{5,1},{9... | collective-permute-start | bytes 589832 | tf_op jit(solution)/shard_map/ppermute | solution.py:484
  76.7 0.9 collective-permute-start.19
  77.6 1.3 %collective-permute-start.18 = (f32[64,256]{1,0:T(8,128)S(1)}, f32[64,256]{1,0:T(8,128)S(1)}, u32[]{:S(2)}, u32[]{:S(2)}) collective-permute-start(f32[64,256]{1,0:T(8,128)S(1)} %add_add_fusion.1), channel_id=1, source_target_pairs={{0,4},{1,5},{2,6},{3,7},{4,0},{5,1},{6,2},{7,3},{8,12},{9,13},{10,... | collective-permute-start | bytes 196616 | tf_op jit(solution)/shard_map/ppermute | solution.py:489
  78.9 1.9 %collective-permute-done.2.refs_1_ = bf16[384,256]{1,0:T(8,128)(2,1)S(1)} collective-permute-done((bf16[384,256]{1,0:T(8,128)(2,1)S(1)}, bf16[384,256]{1,0:T(8,128)(2,1)S(1)}, u32[]{:S(2)}, u32[]{:S(2)}) %collective-permute-start.2) | collective-permute-done | bytes 196640 | tf_op jit(solution)/shard_map/ppermute | solution.py:484
  80.8 2.1 %collective-permute-start.17 = (f32[64,256]{1,0:T(8,128)S(1)}, f32[64,256]{1,0:T(8,128)S(1)}, u32[]{:S(2)}, u32[]{:S(2)}) collective-permute-start(f32[64,256]{1,0:T(8,128)S(1)} %add_add_fusion.1), channel_id=1, source_target_pairs={{0,2},{1,3},{2,0},{3,1},{4,6},{5,7},{6,4},{7,5},{8,10},{9,11},{10,... | collective-permute-start | bytes 196616 | tf_op jit(solution)/shard_map/ppermute | solution.py:489
  83.7 1.6 %collective-permute-start.11 = (bf16[128,128]{1,0:T(8,128)(2,1)S(1)}, bf16[128,128]{1,0:T(8,128)(2,1)S(1)}, u32[]{:S(2)}, u32[]{:S(2)}) collective-permute-start(bf16[128,128]{1,0:T(8,128)(2,1)S(1)} %get-tuple-element.95.refs_1_), channel_id=1, source_target_pairs={{0,8},{1,9},{2,10},{3,11},{4,12},{5,13},{6,14},{7,15},{8,0},{9,1},... | collective-permute-start | bytes 98312 | tf_op jit(solution)/shard_map/ppermute | solution.py:489
  86.0 4.4 %shard_map.231 = (bf16[8,16,16,256]{3,2,1,0:T(8,128)(2,1)S(1)}, f32[8,128]{1,0:T(8,128)S(1)}) custom-call(s32[1]{0:T(128)S(6)} %copy.37.refs_1_.refs_0_, f32[2,22,24,128]{3,2,1,0:T(8,128)S(1)} %get-tuple-element.92.refs_1_, f32[2,22,24,128]{3,2,1,0:T(8,128)S(1)} %get-tuple-element.93.refs_2_, f32[2,22,128,128]{3,2,1,0:T(8,128)S(1)} %get-tuple-element.78.refs_3_, ...), custom_call_target="tpu_custom_call" | custom-call | tf_op jit(solution)/shard_map/pallas_call | solution.py:45
  91.0 1.3 %collective-permute-start.23 = (bf16[512,128]{1,0:T(8,128)(2,1)S(1)}, bf16[512,128]{1,0:T(8,128)(2,1)S(1)}, u32[]{:S(2)}, u32[]{:S(2)}) collective-permute-start(bf16[512,128]{1,0:T(8,128)(2,1)S(1)} %get-tuple-element.100.refs_1_), channel_id=1, source_target_pairs={{0,6},{1,7},{2,4},{3,5},{4,2},{5,3},{6,0},{7,1},{8,14},{9,15},{10,... | collective-permute-start | bytes 393224 | tf_op jit(solution)/shard_map/ppermute | solution.py:489
  92.3 1.1 %collective-permute-start.22 = (bf16[512,128]{1,0:T(8,128)(2,1)S(1)}, bf16[512,128]{1,0:T(8,128)(2,1)S(1)}, u32[]{:S(2)}, u32[]{:S(2)}) collective-permute-start(bf16[512,128]{1,0:T(8,128)(2,1)S(1)} %get-tuple-element.100.refs_1_), channel_id=1, source_target_pairs={{0,4},{1,5},{2,6},{3,7},{4,0},{5,1},{6,2},{7,3},{8,12},{9,13},{10,... | collective-permute-start | bytes 393224 | tf_op jit(solution)/shard_map/ppermute | solution.py:489
  93.4 1.2 %collective-permute-start.21 = (bf16[512,128]{1,0:T(8,128)(2,1)S(1)}, bf16[512,128]{1,0:T(8,128)(2,1)S(1)}, u32[]{:S(2)}, u32[]{:S(2)}) collective-permute-start(bf16[512,128]{1,0:T(8,128)(2,1)S(1)} %get-tuple-element.100.refs_1_), channel_id=1, source_target_pairs={{0,2},{1,3},{2,0},{3,1},{4,6},{5,7},{6,4},{7,5},{8,10},{9,11},{10,... | collective-permute-start | bytes 393224 | tf_op jit(solution)/shard_map/ppermute | solution.py:489
  94.7 4.4 %shard_map.233 = (bf16[8,16,16,256]{3,2,1,0:T(8,128)(2,1)S(1)}, f32[8,128]{1,0:T(8,128)S(1)}) custom-call(s32[1]{0:T(128)S(6)} %copy.37.refs_1_.refs_0_, f32[2,22,24,128]{3,2,1,0:T(8,128)S(1)} %get-tuple-element.92.refs_1_, f32[2,22,24,128]{3,2,1,0:T(8,128)S(1)} %get-tuple-element.93.refs_2_, ...), custom_call_target="tpu_custom_call", output_to_operand_aliasing={{0}: (6, {})} | custom-call | tf_op jit(solution)/shard_map/pallas_call | solution.py:45
  99.2 1.0 copy.36
  100.1 1.1 %shard_map.234 = (bf16[2048,128]{1,0:T(8,128)(2,1)S(1)}, f32[8,128]{1,0:T(8,128)}) custom-call(s32[3]{0:T(128)S(1)} %dynamic-slice_bitcast_fusion.refs_2_.refs_1_.refs_0_, bf16[512,128]{1,0:T(8,128)(2,1)S(1)} %get-tuple-element.100.refs_1_, bf16[512,128]{1,0:T(8,128)(2,1)S(1)} %collective-permute-done.21.refs_2_, ...), custom_call_target="tpu_custom_call" | custom-call | tf_op jit(solution)/shard_map/pallas_call | solution.py:45
  103.6 2.1 %shard_map.235 = (f32[256,1024]{1,0:T(8,128)}, f32[1024,256]{1,0:T(8,128)}) custom-call(s32[3]{0:T(128)S(1)} %dynamic-slice_bitcast_fusion.refs_2_.refs_1_.refs_0_, bf16[2048,128]{1,0:T(8,128)(2,1)S(1)} %get-tuple-element.102.refs_1_, bf16[2048,128]{1,0:T(8,128)(2,1)S(1)} %collective-permute-done.24.refs_2_), custom_call_target="tpu_custom_call" | custom-call | tf_op jit(solution)/shard_map/pallas_call | solution.py:45
  (50 shorter events, 8.6 us)
Async XLA Ops:
  2.3 26.6 %collective-permute-start = (bf16[384,256]{1,0:T(8,128)(2,1)S(1)}, bf16[384,256]{1,0:T(8,128)(2,1)S(1)}, u32[]{:S(2)}, u32[]{:S(2)}) collective-permute-start(bf16[384,256]{1,0:T(8,128)(2,1)S(1)} %bitcast.30), channel_id=1, source_target_pairs={{28,0},{0,4},{4,8},{8,12},{12,16},{16,20},{20,24},{24,28},{29,1},{... | collective-permute-start | bytes 589832 | tf_op jit(solution)/shard_map/ppermute | solution.py:484
  5.4 23.4 %collective-permute-start.1 = (bf16[384,256]{1,0:T(8,128)(2,1)S(1)}, bf16[384,256]{1,0:T(8,128)(2,1)S(1)}, u32[]{:S(2)}, u32[]{:S(2)}) collective-permute-start(bf16[384,256]{1,0:T(8,128)(2,1)S(1)} %bitcast.31), channel_id=1, source_target_pairs={{4,0},{8,4},{12,8},{16,12},{20,16},{24,20},{28,24},{0,28},{5,1},{9... | collective-permute-start | bytes 589832 | tf_op jit(solution)/shard_map/ppermute | solution.py:484
  9.9 0.7 copy-start
  41.8 2.3 %collective-permute-start.4 = (bf16[2048,128]{1,0:T(8,128)(2,1)S(1)}, bf16[2048,128]{1,0:T(8,128)(2,1)S(1)}, u32[]{:S(2)}, u32[]{:S(2)}) collective-permute-start(bf16[2048,128]{1,0:T(8,128)(2,1)S(1)} %get-tuple-element.70), channel_id=1, source_target_pairs={{0,1},{1,0},{2,3},{3,2},{4,5},{5,4},{6,7},{7,6},{8,9},{9,8},{10,11... | collective-permute-start | bytes 1572872 | tf_op jit(solution)/shard_map/ppermute | solution.py:489
  44.9 7.9 %collective-permute-start.5 = (bf16[512,128]{1,0:T(8,128)(2,1)S(1)}, bf16[512,128]{1,0:T(8,128)(2,1)S(1)}, u32[]{:S(2)}, u32[]{:S(2)}) collective-permute-start(bf16[512,128]{1,0:T(8,128)(2,1)S(1)} %get-tuple-element.73), channel_id=1, source_target_pairs={{0,2},{1,3},{2,0},{3,1},{4,6},{5,7},{6,4},{7,5},{8,10},{9,11},{10,... | collective-permute-start | bytes 393224 | tf_op jit(solution)/shard_map/ppermute | solution.py:489
  46.6 8.4 %collective-permute-start.6 = (bf16[512,128]{1,0:T(8,128)(2,1)S(1)}, bf16[512,128]{1,0:T(8,128)(2,1)S(1)}, u32[]{:S(2)}, u32[]{:S(2)}) collective-permute-start(bf16[512,128]{1,0:T(8,128)(2,1)S(1)} %get-tuple-element.74), channel_id=1, source_target_pairs={{0,4},{1,5},{2,6},{3,7},{4,0},{5,1},{6,2},{7,3},{8,12},{9,13},{10,... | collective-permute-start | bytes 393224 | tf_op jit(solution)/shard_map/ppermute | solution.py:489
  46.6 8.4 %collective-permute-start.7 = (bf16[512,128]{1,0:T(8,128)(2,1)S(1)}, bf16[512,128]{1,0:T(8,128)(2,1)S(1)}, u32[]{:S(2)}, u32[]{:S(2)}) collective-permute-start(bf16[512,128]{1,0:T(8,128)(2,1)S(1)} %get-tuple-element.75), channel_id=1, source_target_pairs={{0,6},{1,7},{2,4},{3,5},{4,2},{5,3},{6,0},{7,1},{8,14},{9,15},{10,... | collective-permute-start | bytes 393224 | tf_op jit(solution)/shard_map/ppermute | solution.py:489
  55.7 10.5 %collective-permute-start.8 = (bf16[128,128]{1,0:T(8,128)(2,1)S(1)}, bf16[128,128]{1,0:T(8,128)(2,1)S(1)}, u32[]{:S(2)}, u32[]{:S(2)}) collective-permute-start(bf16[128,128]{1,0:T(8,128)(2,1)S(1)} %get-tuple-element.82), channel_id=1, source_target_pairs={{0,8},{1,9},{2,10},{3,11},{4,12},{5,13},{6,14},{7,15},{8,0},{9,1},... | collective-permute-start | bytes 98312 | tf_op jit(solution)/shard_map/ppermute | solution.py:489
  55.8 29.5 %copy-start.1 = (s32[8,8]{1,0:T(8,128)S(1)}, s32[8,8]{1,0:T(8,128)}, u32[]{:S(2)}) copy-start(s32[8,8]{1,0:T(8,128)} %refs_0_.9) | copy-start | bytes 772
  60.3 16.2 %collective-permute-start.16 = (f32[64,256]{1,0:T(8,128)S(1)}, f32[64,256]{1,0:T(8,128)S(1)}, u32[]{:S(2)}, u32[]{:S(2)}) collective-permute-start(f32[64,256]{1,0:T(8,128)S(1)} %get-tuple-element.99), channel_id=1, source_target_pairs={{0,24},{1,25},{2,26},{3,27},{4,28},{5,29},{6,30},{7,31},{8,16},{9,... | collective-permute-start | bytes 196616 | tf_op jit(solution)/shard_map/ppermute | solution.py:489
  62.6 14.1 %collective-permute-start.15 = (f32[64,256]{1,0:T(8,128)S(1)}, f32[64,256]{1,0:T(8,128)S(1)}, u32[]{:S(2)}, u32[]{:S(2)}) collective-permute-start(f32[64,256]{1,0:T(8,128)S(1)} %get-tuple-element.99), channel_id=1, source_target_pairs={{0,16},{1,17},{2,18},{3,19},{4,20},{5,21},{6,22},{7,23},{8,24},{9,... | collective-permute-start | bytes 196616 | tf_op jit(solution)/shard_map/ppermute | solution.py:489
  63.8 12.9 %collective-permute-start.14 = (f32[64,256]{1,0:T(8,128)S(1)}, f32[64,256]{1,0:T(8,128)S(1)}, u32[]{:S(2)}, u32[]{:S(2)}) collective-permute-start(f32[64,256]{1,0:T(8,128)S(1)} %get-tuple-element.99), channel_id=1, source_target_pairs={{0,8},{1,9},{2,10},{3,11},{4,12},{5,13},{6,14},{7,15},{8,0},{9,1},... | collective-permute-start | bytes 196616 | tf_op jit(solution)/shard_map/ppermute | solution.py:489
  64.8 6.5 %collective-permute-start.9 = (bf16[128,128]{1,0:T(8,128)(2,1)S(1)}, bf16[128,128]{1,0:T(8,128)(2,1)S(1)}, u32[]{:S(2)}, u32[]{:S(2)}) collective-permute-start(bf16[128,128]{1,0:T(8,128)(2,1)S(1)} %get-tuple-element.83), channel_id=1, source_target_pairs={{0,16},{1,17},{2,18},{3,19},{4,20},{5,21},{6,22},{7,23},{8,24},{9,... | collective-permute-start | bytes 98312 | tf_op jit(solution)/shard_map/ppermute | solution.py:489
  66.2 5.7 %collective-permute-start.10 = (bf16[128,128]{1,0:T(8,128)(2,1)S(1)}, bf16[128,128]{1,0:T(8,128)(2,1)S(1)}, u32[]{:S(2)}, u32[]{:S(2)}) collective-permute-start(bf16[128,128]{1,0:T(8,128)(2,1)S(1)} %get-tuple-element.84), channel_id=1, source_target_pairs={{0,24},{1,25},{2,26},{3,27},{4,28},{5,29},{6,30},{7,31},{8,16},{9,... | collective-permute-start | bytes 98312 | tf_op jit(solution)/shard_map/ppermute | solution.py:489
  71.2 9.6 %collective-permute-start.2 = (bf16[384,256]{1,0:T(8,128)(2,1)S(1)}, bf16[384,256]{1,0:T(8,128)(2,1)S(1)}, u32[]{:S(2)}, u32[]{:S(2)}) collective-permute-start(bf16[384,256]{1,0:T(8,128)(2,1)S(1)} %get-tuple-element.67), channel_id=1, source_target_pairs={{28,0},{0,4},{4,8},{8,12},{12,16},{16,20},{20,24},{24,28},{29,1},{... | collective-permute-start | bytes 589832 | tf_op jit(solution)/shard_map/ppermute | solution.py:484
  71.9 11.7 %collective-permute-start.3 = (bf16[384,256]{1,0:T(8,128)(2,1)S(1)}, bf16[384,256]{1,0:T(8,128)(2,1)S(1)}, u32[]{:S(2)}, u32[]{:S(2)}) collective-permute-start(bf16[384,256]{1,0:T(8,128)(2,1)S(1)} %get-tuple-element.68), channel_id=1, source_target_pairs={{4,0},{8,4},{12,8},{16,12},{20,16},{24,20},{28,24},{0,28},{5,1},{9... | collective-permute-start | bytes 589832 | tf_op jit(solution)/shard_map/ppermute | solution.py:484
  76.5 7.1 %collective-permute-start.13 = (bf16[128,128]{1,0:T(8,128)(2,1)S(1)}, bf16[128,128]{1,0:T(8,128)(2,1)S(1)}, u32[]{:S(2)}, u32[]{:S(2)}) collective-permute-start(bf16[128,128]{1,0:T(8,128)(2,1)S(1)} %get-tuple-element.95.refs_1_), channel_id=1, source_target_pairs={{0,24},{1,25},{2,26},{3,27},{4,28},{5,29},{6,30},{7,31},{8,16},{9,... | collective-permute-start | bytes 98312 | tf_op jit(solution)/shard_map/ppermute | solution.py:489
  76.7 16.7 %collective-permute-start.19 = (f32[64,256]{1,0:T(8,128)S(1)}, f32[64,256]{1,0:T(8,128)S(1)}, u32[]{:S(2)}, u32[]{:S(2)}) collective-permute-start(f32[64,256]{1,0:T(8,128)S(1)} %add_add_fusion.1), channel_id=1, source_target_pairs={{0,6},{1,7},{2,4},{3,5},{4,2},{5,3},{6,0},{7,1},{8,14},{9,15},{10,... | collective-permute-start | bytes 196616 | tf_op jit(solution)/shard_map/ppermute | solution.py:489
  77.6 17.0 %collective-permute-start.18 = (f32[64,256]{1,0:T(8,128)S(1)}, f32[64,256]{1,0:T(8,128)S(1)}, u32[]{:S(2)}, u32[]{:S(2)}) collective-permute-start(f32[64,256]{1,0:T(8,128)S(1)} %add_add_fusion.1), channel_id=1, source_target_pairs={{0,4},{1,5},{2,6},{3,7},{4,0},{5,1},{6,2},{7,3},{8,12},{9,13},{10,... | collective-permute-start | bytes 196616 | tf_op jit(solution)/shard_map/ppermute | solution.py:489
  80.8 13.8 %collective-permute-start.17 = (f32[64,256]{1,0:T(8,128)S(1)}, f32[64,256]{1,0:T(8,128)S(1)}, u32[]{:S(2)}, u32[]{:S(2)}) collective-permute-start(f32[64,256]{1,0:T(8,128)S(1)} %add_add_fusion.1), channel_id=1, source_target_pairs={{0,2},{1,3},{2,0},{3,1},{4,6},{5,7},{6,4},{7,5},{8,10},{9,11},{10,... | collective-permute-start | bytes 196616 | tf_op jit(solution)/shard_map/ppermute | solution.py:489
  83.6 6.8 %collective-permute-start.12 = (bf16[128,128]{1,0:T(8,128)(2,1)S(1)}, bf16[128,128]{1,0:T(8,128)(2,1)S(1)}, u32[]{:S(2)}, u32[]{:S(2)}) collective-permute-start(bf16[128,128]{1,0:T(8,128)(2,1)S(1)} %get-tuple-element.95.refs_1_), channel_id=1, source_target_pairs={{0,16},{1,17},{2,18},{3,19},{4,20},{5,21},{6,22},{7,23},{8,24},{9,... | collective-permute-start | bytes 98312 | tf_op jit(solution)/shard_map/ppermute | solution.py:489
  83.7 6.8 %collective-permute-start.11 = (bf16[128,128]{1,0:T(8,128)(2,1)S(1)}, bf16[128,128]{1,0:T(8,128)(2,1)S(1)}, u32[]{:S(2)}, u32[]{:S(2)}) collective-permute-start(bf16[128,128]{1,0:T(8,128)(2,1)S(1)} %get-tuple-element.95.refs_1_), channel_id=1, source_target_pairs={{0,8},{1,9},{2,10},{3,11},{4,12},{5,13},{6,14},{7,15},{8,0},{9,1},... | collective-permute-start | bytes 98312 | tf_op jit(solution)/shard_map/ppermute | solution.py:489
  91.0 9.1 %collective-permute-start.23 = (bf16[512,128]{1,0:T(8,128)(2,1)S(1)}, bf16[512,128]{1,0:T(8,128)(2,1)S(1)}, u32[]{:S(2)}, u32[]{:S(2)}) collective-permute-start(bf16[512,128]{1,0:T(8,128)(2,1)S(1)} %get-tuple-element.100.refs_1_), channel_id=1, source_target_pairs={{0,6},{1,7},{2,4},{3,5},{4,2},{5,3},{6,0},{7,1},{8,14},{9,15},{10,... | collective-permute-start | bytes 393224 | tf_op jit(solution)/shard_map/ppermute | solution.py:489
  92.3 7.8 %collective-permute-start.22 = (bf16[512,128]{1,0:T(8,128)(2,1)S(1)}, bf16[512,128]{1,0:T(8,128)(2,1)S(1)}, u32[]{:S(2)}, u32[]{:S(2)}) collective-permute-start(bf16[512,128]{1,0:T(8,128)(2,1)S(1)} %get-tuple-element.100.refs_1_), channel_id=1, source_target_pairs={{0,4},{1,5},{2,6},{3,7},{4,0},{5,1},{6,2},{7,3},{8,12},{9,13},{10,... | collective-permute-start | bytes 393224 | tf_op jit(solution)/shard_map/ppermute | solution.py:489
  93.4 6.7 %collective-permute-start.21 = (bf16[512,128]{1,0:T(8,128)(2,1)S(1)}, bf16[512,128]{1,0:T(8,128)(2,1)S(1)}, u32[]{:S(2)}, u32[]{:S(2)}) collective-permute-start(bf16[512,128]{1,0:T(8,128)(2,1)S(1)} %get-tuple-element.100.refs_1_), channel_id=1, source_target_pairs={{0,2},{1,3},{2,0},{3,1},{4,6},{5,7},{6,4},{7,5},{8,10},{9,11},{10,... | collective-permute-start | bytes 393224 | tf_op jit(solution)/shard_map/ppermute | solution.py:489
  94.6 7.1 %collective-permute-start.20 = (f32[64,256]{1,0:T(8,128)S(1)}, f32[64,256]{1,0:T(8,128)S(1)}, u32[]{:S(2)}, u32[]{:S(2)}) collective-permute-start(f32[64,256]{1,0:T(8,128)S(1)} %add_add_fusion), channel_id=1, source_target_pairs={{0,1},{1,0},{2,3},{3,2},{4,5},{5,4},{6,7},{7,6},{8,9},{9,8},{10,11... | collective-permute-start | bytes 196616 | tf_op jit(solution)/shard_map/ppermute | solution.py:489
  101.3 2.3 %collective-permute-start.24 = (bf16[2048,128]{1,0:T(8,128)(2,1)S(1)}, bf16[2048,128]{1,0:T(8,128)(2,1)S(1)}, u32[]{:S(2)}, u32[]{:S(2)}) collective-permute-start(bf16[2048,128]{1,0:T(8,128)(2,1)S(1)} %get-tuple-element.102.refs_1_), channel_id=1, source_target_pairs={{0,1},{1,0},{2,3},{3,2},{4,5},{5,4},{6,7},{7,6},{8,9},{9,8},{10,11... | collective-permute-start | bytes 1572872 | tf_op jit(solution)/shard_map/ppermute | solution.py:489

commit v3 on v2

--- a/solution.py
+++ b/solution.py
@@ -3,7 +3,6 @@
 
 import jax
 import jax.numpy as jnp
-import numpy as np
 from jax import lax
 from jax.experimental import pallas as pl
 from jax.experimental.pallas import tpu as pltpu
@@ -155,7 +154,7 @@
     return lax.dot_general(a, b, (((1,), (1,)), ((), ())), preferred_element_type=F32)
 
 
-def dense_block(conv, x, dy, params, add_dw, sums_ref):
+def dense_block(conv, x, dy, params, add_dw, add_sum):
     win, wout, bias_in, bias_out, scale, gain, shift, conv_bias = params
     hidden = win.shape[1]
     channels = win.shape[0]
@@ -179,7 +178,7 @@
         grad_unit = grad_unit + dot_t(gp, win[:, ks])
         add_dw(0, k, dot(unit_t, gp))
         add_dw(1, k, dot(gb_t, act))
-        sums_ref[k // 256] += fold(gp.astype(F32))
+        add_sum(k // 256, fold(gp.astype(F32)))
     branch = branch + bias_out[...]
     out = x + scale[...] * branch
     scaled = grad_unit * gain[...]
@@ -190,11 +189,11 @@
     )
     grad_conv = grad_conv.astype(BF16).astype(F32)
     nk = hidden // 256
-    sums_ref[nk] += fold(gb.astype(F32))
-    sums_ref[nk + 1] += fold(dy * branch)
-    sums_ref[nk + 2] += fold(grad_unit * normed)
-    sums_ref[nk + 3] += fold(grad_unit)
-    sums_ref[nk + 4] += fold(grad_conv)
+    add_sum(nk + 0, fold(gb.astype(F32)))
+    add_sum(nk + 1, fold(dy * branch))
+    add_sum(nk + 2, fold(grad_unit * normed))
+    add_sum(nk + 3, fold(grad_unit))
+    add_sum(nk + 4, fold(grad_conv))
     return out, grad_conv
 
 
@@ -233,15 +232,19 @@
 
 
 def inner_kernel(
-    nbr_ref, cnt_ref, place_ref, x_ref, dy_ref, k_ref, win, wout, bias_in, bias_out, scale, gain, shift, conv_bias,
-    center_ref, dyt_ref, out_ref, g_ref, dw_ref, sums_ref,
-    k8_ref, conv_ref,
+    n_place, nbr_ref, cnt_ref, *refs,
 ):
+    (x_ref, dy_ref, k_ref, win, wout, bias_in, bias_out, scale, gain, shift, conv_bias) = refs[n_place : n_place + 11]
+    center_ref, dyt_ref, out_ref, g_ref, dw_ref, sums_ref, k8_ref, win_kept, wout_kept, vec_kept, conv_ref = refs[
+        n_place + 11 :
+    ]
     live = cnt_ref[0]
     channels = win.shape[0]
     spread_taps(k_ref, k8_ref, False)
-    dw_ref[...] = jnp.zeros(dw_ref.shape, F32)
-    sums_ref[...] = jnp.zeros(sums_ref.shape, F32)
+    win_kept[...] = win[...]
+    wout_kept[...] = wout[...]
+    for i, v in enumerate((bias_in, bias_out, scale, gain, shift, conv_bias)):
+        vec_kept[i : i + 1, 0 : v.shape[1]] = v[...]
 
     def turn(r, carry):
         for t in range(8):
@@ -254,105 +257,89 @@
     lax.fori_loop(0, 16, turn, 0)
     rims_of(center_ref, nbr_ref)
     params = (win, wout, bias_in, bias_out, scale, gain, shift, conv_bias)
-    nr, n, c0 = 4, 10, 3
+    n, c0 = 10, 3
     cols = slice(c0 * 8, (c0 + n) * 8)
     pads = (None, center_ref, None)
 
     def add_dw(which, k, v):
-        dw_ref[which * channels : (which + 1) * channels, k : k + 256] += v
-
-    def block(m, carry):
-        r0 = m * nr
-
-        def conv(q, carry):
-            for h in range(2):
-                accs = conv_wide(pads, k8_ref, h, r0 + q, c0, n)
-                conv_ref[pl.ds(pl.multiple_of(q * n * 8, 8), n * 8), lanes(h)] = jnp.concatenate(accs, axis=0)
-            return carry
-
-        lax.fori_loop(0, nr, conv, 0)
-        x = rows_of(center_ref, r0 + 3, nr, c0, n)
-        dy = rows_of(dyt_ref, r0, nr, c0, n)
-        out, g = dense_block(conv_ref[...], x, dy, params, add_dw, sums_ref)
-        for q in range(nr):
-            for h in range(2):
-                out_ref[h, r0 + q, cols, :] = out[q * n * 8 : (q + 1) * n * 8, lanes(h)]
-                g_ref[h, 3 + r0 + q, cols, :] = g[q * n * 8 : (q + 1) * n * 8, lanes(h)]
+        dw_ref[which * channels : (which + 1) * channels, k : k + 256] = v
+
+    def add_sum(which, v):
+        sums_ref[which] = v
+
+    def conv(q, carry):
+        for h in range(2):
+            accs = conv_wide(pads, k8_ref, h, q, c0, n)
+            conv_ref[pl.ds(pl.multiple_of(q * n * 8, 8), n * 8), lanes(h)] = jnp.concatenate(accs, axis=0)
         return carry
 
-    lax.fori_loop(0, 16 // nr, block, 0)
+    lax.fori_loop(0, 16, conv, 0)
+    x = rows_of(center_ref, 3, 16, c0, n)
+    dy = rows_of(dyt_ref, 0, 16, c0, n)
+    out, g = dense_block(conv_ref[...], x, dy, params, add_dw, add_sum)
+    for q in range(16):
+        for h in range(2):
+            out_ref[h, q, cols, :] = out[q * n * 8 : (q + 1) * n * 8, lanes(h)]
+            g_ref[h, 3 + q, cols, :] = g[q * n * 8 : (q + 1) * n * 8, lanes(h)]
 
 
 def edge_kernel(
-    nbr_ref, core_ref, hw_ref, he_ref, center_ref, dyt_ref, dw_in, sums_in, out_in, g_in,
-    k_ref, win, wout, bias_in, bias_out, scale, gain, shift, conv_bias,
+    nbr_ref, place_ref, hw_ref, he_ref, center_ref, dyt_ref, dw_in, sums_in, out_in, g_in, k8_ref, win, wout, vec,
     west_ref, east_ref, out_ref, g_ref, send_l, send_r, own_ref, sent_ref, sums_ref,
-    k8_ref, conv_ref, dw_ref,
+    conv_ref, travel_ref,
 ):
-    core = core_ref[0]
-    channels = win.shape[0]
-    hidden = win.shape[1]
-    spread_taps(k_ref, k8_ref, False)
-    sums_ref[...] = sums_in[...]
+    core = place_ref[0]
+    channels, hidden = win.shape
     side_rim(west_ref, hw_ref, nbr_ref, 2, 4, 6)
     side_rim(east_ref, he_ref, nbr_ref, 3, 5, 7)
-    params = (win, wout, bias_in, bias_out, scale, gain, shift, conv_bias)
+    widths = (hidden,) + (channels,) * 5
+    params = (win, wout) + tuple(vec.at[i : i + 1, 0:w] for i, w in enumerate(widths))
     pads = (west_ref, center_ref, east_ref)
-    nr = 8
-    n_blocks = 16 // nr
-
-    for m in range(n_blocks):
-        r0 = m * nr
-        src, last = (dw_in, m == n_blocks - 1) if m == 0 else (dw_ref, m == n_blocks - 1)
-
-        def add_dw(which, k, v, src=src, last=last):
-            at = slice(which * channels, (which + 1) * channels), slice(k, k + 256)
-            v = src[at] + v
-            if not last:
-                dw_ref[at] = v
-                return
-            if which == 1:
-                v = v.T
-            v = v.astype(BF16)
-            for side in range(2):
-                row = k * 2 + side * 256 if which == 0 else side * hidden + k
-                piece = v[:, lanes(side)]
-
-                @pl.when(core == which)
-                def _():
-                    own_ref[row : row + 256, :] = piece
-
-                @pl.when(core != which)
-                def _():
-                    sent_ref[row : row + 256, :] = piece
-
+
+    def add_dw(which, k, v):
+        v = dw_in[which * channels : (which + 1) * channels, k : k + 256] + v
+        if which == 1:
+            v = v.T
+        v = v.astype(BF16)
+        for side in range(2):
+            row = k * 2 + side * 256 if which == 0 else side * hidden + k
+            travel_ref[which, row : row + 256, :] = v[:, lanes(side)]
+
+    def add_sum(which, v):
+        sums_ref[which] = sums_in[which] + v
+
+    def conv(m, carry):
+        r0 = m * 8
         for h in range(2):
             for side, c0 in enumerate((0, 13)):
-                accs = conv_tall(pads, k8_ref, h, r0, nr, c0, RIM)
-                for q in range(nr):
-                    base = (q * 2 + side) * 24
-                    conv_ref[base : base + 24, lanes(h)] = jnp.concatenate(accs[q], axis=0)
-        xs, dys = [], []
-        for q in range(nr):
-            for c0 in (0, 13):
-                xs.append(rows_of(center_ref, r0 + 3 + q, 1, c0, RIM))
-                dys.append(rows_of(dyt_ref, r0 + q, 1, c0, RIM))
-        x = jnp.concatenate(xs, axis=0)
-        dy = jnp.concatenate(dys, axis=0)
-        out, g = dense_block(conv_ref[...], x, dy, params, add_dw, sums_ref)
-        for q in range(nr):
-            for side, c0 in enumerate((0, 13)):
-                part = slice((q * 2 + side) * 24, (q * 2 + side) * 24 + 24)
-                cols = slice(c0 * 8, c0 * 8 + 24)
-                for h in range(2):
-                    out_ref[h, r0 + q, cols, :] = out[part, lanes(h)]
-                    g_ref[h, 3 + r0 + q, cols, :] = g[part, lanes(h)]
-        for q in range(0, nr, 2):
-            for side, send in enumerate((send_l, send_r)):
-                v = jnp.concatenate(
-                    [g[(q + s) * 48 + side * 24 : (q + s) * 48 + side * 24 + 24] for s in range(2)], axis=0
-                )
-                send[(r0 + q) * 24 : (r0 + q) * 24 + 48, :] = v.astype(BF16)
+                accs = conv_tall(pads, k8_ref, h, r0, 8, c0, RIM)
+                for q in range(8):
+                    at = pl.multiple_of(((r0 + q) * 2 + side) * 24, 8)
+                    conv_ref[pl.ds(at, 24), lanes(h)] = jnp.concatenate(accs[q], axis=0)
+        return carry
+
+    lax.fori_loop(0, 2, conv, 0)
+    xs, dys = [], []
+    for q in range(16):
+        for c0 in (0, 13):
+            xs.append(rows_of(center_ref, 3 + q, 1, c0, RIM))
+            dys.append(rows_of(dyt_ref, q, 1, c0, RIM))
+    x = jnp.concatenate(xs, axis=0)
+    dy = jnp.concatenate(dys, axis=0)
+    out, g = dense_block(conv_ref[...], x, dy, params, add_dw, add_sum)
+    for q in range(16):
+        for side, c0 in enumerate((0, 13)):
+            part = slice((q * 2 + side) * 24, (q * 2 + side) * 24 + 24)
+            cols = slice(c0 * 8, c0 * 8 + 24)
+            for h in range(2):
+                out_ref[h, q, cols, :] = out[part, lanes(h)]
+                g_ref[h, 3 + q, cols, :] = g[part, lanes(h)]
+    for q in range(0, 16, 2):
+        for side, send in enumerate((send_l, send_r)):
+            v = [g[(q + s) * 48 + side * 24 : (q + s) * 48 + side * 24 + 24] for s in range(2)]
+            send[q * 24 : q * 24 + 48, :] = jnp.concatenate(v, axis=0).astype(BF16)
+    own_ref[...] = travel_ref[core]
+    sent_ref[...] = travel_ref[1 - core]
 
 
 def turn_out(out_ref, src_ref, live, r):
@@ -362,9 +349,8 @@
             out_ref[t, r, :, lanes(h)] = jnp.where(t < live, v, 0.0).astype(BF16)
 
 
-def tiles_kernel(nbr_ref, cnt_ref, full_ref, g_in, out_ref, g_ref):
+def tiles_kernel(cnt_ref, full_ref, out_ref):
     live = cnt_ref[0]
-    rims_of(g_ref, nbr_ref)
 
     def row(r, carry):
         turn_out(out_ref, full_ref, live, r)
@@ -396,15 +382,8 @@
     lax.fori_loop(0, TAPS, row_tap, 0)
 
 
-def small_kernel(tap0, tap1, sums, small_ref):
-    ns = sums.shape[0]
-    small_ref[...] = jnp.zeros(small_ref.shape, F32)
-    small_ref[0:ns, :] = jnp.sum(sums[...], axis=1)
-    small_ref[ns : ns + 49, lanes(0)] = jnp.sum(tap0[...], axis=1)
-    small_ref[ns : ns + 49, lanes(1)] = jnp.sum(tap1[...], axis=1)
-
-
-def sides_kernel(nbr_ref, hw_ref, he_ref, west_ref, east_ref):
+def sides_kernel(nbr_ref, hw_ref, he_ref, g_in, west_ref, east_ref, g_ref):
+    rims_of(g_ref, nbr_ref)
     side_rim(west_ref, hw_ref, nbr_ref, 2, 4, 6)
     side_rim(east_ref, he_ref, nbr_ref, 3, 5, 7)
 
@@ -414,6 +393,8 @@
     live = cnt_ref[0]
     spread_taps(k_ref, k8_ref, True)
     pads = (west_ref, g_ref, east_ref)
+    if len(refs) > 3:
+        gx_ref[:, :first] = refs[0][...]
 
     def row(r, carry):
         for h in range(2):
@@ -427,18 +408,18 @@
     lax.fori_loop(first, last, row, 0)
 
 
-def scatter_kernel(level, size, mine_ref, *refs):
-    n_out = size
-    held, outs = refs[:-n_out], refs[-n_out:]
+def added(held):
     total = held[0][...].astype(F32)
     for h in held[1:]:
         total = total + h[...].astype(F32)
-    total = total.astype(BF16)
+    return total.astype(BF16)
+
+
+def scatter_kernel(size, place_ref, *refs):
+    held, outs = refs[:-size], refs[-size:]
+    total = added(held)
     rows = total.shape[0] // size
-    if size == 1:
-        outs[0][...] = total
-        return
-    mine = mine_ref[level]
+    mine = place_ref[0]
     for p in range(size):
         piece = total[p * rows : (p + 1) * rows]
         for k in range(size):
@@ -448,17 +429,37 @@
                 outs[k][...] = piece
 
 
-def gather_kernel(level, size, mine_ref, *refs):
+def finish_kernel(tap0, tap1, sums, *refs):
+    held, out = refs[:-1], refs[-1]
+    ns = sums.shape[0]
+    total = added(held)
+    rows = total.shape[0]
+    out[0:rows, :] = total
+    dense = jnp.sum(sums[...], axis=1)
+    rest = jnp.zeros((64 - ns - 49, LANES), F32)
+    for h, tap in enumerate((tap0, tap1)):
+        part = jnp.concatenate([dense[:, lanes(h)], jnp.sum(tap[...], axis=1), rest], axis=0)
+        out[rows + 64 * h : rows + 64 * h + 64, :] = part.astype(BF16)
+
+
+def gather_kernel(place_ref, *refs):
     parts, out = refs[:-1], refs[-1]
-    rows = parts[0].shape[0]
-    mine = mine_ref[level]
-    for k in range(size):
-        out[pl.ds(pl.multiple_of((mine ^ k) * rows, 16), rows), :] = parts[k][...]
-
-
-def last_kernel(factor, core_ref, own_ref, other_ref, win_ref, wout_ref):
-    core = core_ref[0]
+    rows = parts[0].shape[0] - LANES
+    mine = place_ref[0]
+    total = jnp.zeros((LANES, LANES), F32)
+    for k, part in enumerate(parts):
+        out[pl.ds(pl.multiple_of((mine ^ k) * rows, 16), rows), :] = part[0:rows, :]
+        total = total + part[rows : rows + LANES, :].astype(F32)
+    out[len(parts) * rows : len(parts) * rows + LANES, :] = total.astype(BF16)
+
+
+def last_kernel(
+    factor, place_ref, own_ref, other_ref,
+    taps_ref, conv_bias_ref, gain_ref, shift_ref, win_ref, bias_in_ref, wout_ref, bias_out_ref, scale_ref,
+):
+    core = place_ref[0]
     hidden = wout_ref.shape[0]
+    rows = 2 * hidden
 
     def put_in(ref):
         for b in range(hidden // LANES):
@@ -477,6 +478,18 @@
     def _():
         put_in(other_ref)
         put_out(own_ref)
+
+    nk = hidden // 256
+    for h in range(2):
+        at = slice(rows + 64 * h, rows + 64 * h + 64)
+        small = (own_ref[at, :].astype(F32) + other_ref[at, :].astype(F32)) * factor
+        for k in range(nk):
+            bias_in_ref[:, k * 256 + h * LANES : k * 256 + (h + 1) * LANES] = small[k : k + 1]
+        for k, ref in enumerate((bias_out_ref, scale_ref, gain_ref, shift_ref, conv_bias_ref)):
+            ref[:, lanes(h)] = small[nk + k : nk + k + 1]
+        for i in range(TAPS):
+            at = nk + 5 + i * TAPS
+            taps_ref[i, :, lanes(h)] = small[at : at + TAPS]
 
 
 def shifted(block, axis, distance):
@@ -514,8 +527,9 @@
     )
     weights = tuple(Far(w) for w in weights)
     conv_kernel = Far(conv_kernel)
-    places = np.array([[(d // bit) % size for bit, size in groups()] for d in range(lax.axis_size(AXES))], np.int32)
-    place = lax.dynamic_index_in_dim(jnp.asarray(places), lax.axis_index(AXES), 0, keepdims=False)
+    me = lax.axis_index(AXES)
+    place = [((me // bit) % size).astype(jnp.int32).reshape(1) for bit, size in groups()]
+    neighbours = Far(neighbours)
 
     def columns(lo):
         return x[:, :, lo : lo + RIM].transpose(1, 2, 0, 3).reshape(edge * RIM * slots, channels)
@@ -533,20 +547,22 @@
     tiles = (slots, edge, edge, channels)
     travel = (channels * hidden // LANES, LANES)
 
-    center, dyt, full, g, dw, sums = call(
-        inner_kernel,
+    spread = (2, TAPS * TAPS, 8, LANES)
+    center, dyt, full, g, dw, sums, *kept = call(
+        functools.partial(inner_kernel, len(place)),
         [(tall, F32, KEEP), (half, F32, KEEP), (half, F32, KEEP), (tall, F32, KEEP), (dw_shape, F32, KEEP),
-         (sums_shape, F32, KEEP)],
-        (neighbours, tile_count, place, Far(x), Far(dy), conv_kernel) + weights,
-        [k8, pltpu.VMEM((4 * 10 * slots, channels), F32)],
-        smem=3,
+         (sums_shape, F32, KEEP), (spread, F32, KEEP), (proj_in.shape, BF16, KEEP), (proj_out.shape, BF16, KEEP),
+         ((8, hidden), F32, KEEP)],
+        (neighbours, tile_count, *place, Far(x), Far(dy), conv_kernel) + weights,
+        [pltpu.VMEM((edge * (edge - 2 * RIM) * slots, channels), F32)],
+        smem=2 + len(place),
     )
     west, east, full, g, send_l, send_r, held, sent, sums = call(
         edge_kernel,
         [(side, F32, KEEP), (side, F32, KEEP), (half, F32, KEEP), (tall, F32, KEEP), (halo, BF16), (halo, BF16),
          (travel, BF16), (travel, BF16), (sums_shape, F32, KEEP)],
-        (neighbours, place, from_west, from_east, center, dyt, dw, sums, full, g, conv_kernel) + weights,
-        [k8, pltpu.VMEM((8 * 6 * slots, channels), F32), pltpu.VMEM(dw_shape, F32)],
+        (neighbours, place[0], from_west, from_east, center, dyt, dw, sums, full, g, *kept),
+        [pltpu.VMEM((edge * 2 * RIM * slots, channels), F32), pltpu.VMEM((2,) + travel, BF16)],
         smem=2,
         alias={8: 2, 9: 3},
     )
@@ -555,11 +571,7 @@
     grad_from_east = shifted(send_l, "space", -1)
     grad_from_west = shifted(send_r, "space", 1)
 
-    out_tiles, g, done = call(
-        tiles_kernel, [(tiles, BF16), (tall, F32, KEEP)], (neighbours, tile_count, full, g), smem=2, alias={3: 1},
-        token=True,
-    )
-    filler = (done,)
+    filler = ()
     taps = []
 
     def tap(h):
@@ -570,75 +582,69 @@
         taps.append(v)
         return done
 
+    sides = None
+    gx = ()
+    cuts = [0, 4, 9, edge]
+
+    def back():
+        nonlocal gx
+        first = gx[0].value.shape[1] if gx else 0
+        last = cuts[cuts.index(first) + 1]
+        *gx, done = call(
+            functools.partial(back_kernel, first, last),
+            [((slots, last, edge, channels), BF16, KEEP) if last < edge else (tiles, BF16)],
+            (tile_count, *sides, g, dyt, conv_kernel, *gx),
+            [pltpu.VMEM(half, F32), k8],
+            smem=1,
+            after=(begun,),
+            token=True,
+        )
+        return done
+
     for n, (bit, size) in enumerate(later):
-        level = n + 1
         held, *parts, begun = call(
-            functools.partial(scatter_kernel, level, size),
+            functools.partial(scatter_kernel, size),
             [((held.shape[0] // size, LANES), BF16)] * size,
-            (place, held, *arrived),
+            (place[n + 1], held, *arrived),
             smem=1,
             after=filler,
             token=True,
         )
         arrived = [crossed(p, k * bit) for k, p in enumerate(parts, 1)]
-        filler = (tap(n),) if n < 2 else ()
-    small, done = call(small_kernel, [((64, channels), F32)], (*taps, sums), after=filler, token=True)
+        filler = ()
+        if n == 0:
+            filler = (tap(0), tap(1))
+        if n == 1:
+            *sides, g = call(
+                sides_kernel, [(side, F32, KEEP), (side, F32, KEEP), (tall, F32, KEEP)],
+                (neighbours, grad_from_west, grad_from_east, g), smem=1, alias={3: 2}, after=(begun,),
+            )
+            filler = (back(),)
     held, begun = call(
-        functools.partial(scatter_kernel, 0, 1), [(held.shape, BF16)], (place, held, *arrived), smem=1, after=(done,),
-        token=True,
+        finish_kernel, [((held.shape[0] + LANES, LANES), BF16)], (*taps, sums, held, *arrived), after=filler, token=True
     )
 
-    sides = None
-    gx = None
     for n, (bit, size) in enumerate(later[::-1]):
-        level = len(later) - n
         parts = [held] + [crossed(held, k * bit) for k in range(1, size)]
-        small = sum((crossed(small, k * bit) for k in range(1, size)), small)
-        filler = ()
-        if n < 2:
-            if n == 0:
-                sides = call(
-                    sides_kernel, [(side, F32, KEEP)] * 2, (neighbours, grad_from_west, grad_from_east), smem=1,
-                    after=(begun,),
-                )
-            gx, done = call(
-                functools.partial(back_kernel, n * edge // 2, (n + 1) * edge // 2),
-                [(tiles, BF16, KEEP)],
-                (tile_count, *sides, g, dyt, conv_kernel) + ((gx,) if n else ()),
-                [pltpu.VMEM(half, F32), k8],
-                smem=1,
-                alias={6: 0} if n else None,
-                after=(begun,),
-                token=True,
-            )
-            filler = (done,)
+        filler = (back(),) if n < 2 else ()
+        rows = (held.shape[0] - LANES) * size + LANES
         held, begun = call(
-            functools.partial(gather_kernel, level, size), [((held.shape[0] * size, LANES), BF16)],
-            (place, *parts), smem=1, after=filler, token=True,
+            gather_kernel, [((rows, LANES), BF16)],
+            (place[len(later) - n], *parts), smem=1, after=filler, token=True,
         )
-    small = small + crossed(small, 1)
+    out_tiles, done = call(tiles_kernel, [(tiles, BF16)], (tile_count, full), smem=1, after=(begun,), token=True)
     factor = 1.0 / math.sqrt(lax.axis_size("dp") * lax.axis_size("space") * slots * edge * edge)
-    grad_in, grad_out = call(
+    vec = ((1, channels), F32)
+    small = [((TAPS, TAPS, channels), F32), vec, vec, vec]
+    grads = call(
         functools.partial(last_kernel, factor),
-        [((channels, hidden), F32), ((hidden, channels), F32)],
-        (place, held, crossed(held, 1)),
+        [*small, ((channels, hidden), F32), ((1, hidden), F32), ((hidden, channels), F32), vec, vec],
+        (place[0], held, crossed(held, 1)),
         smem=1,
+        after=(done,),
     )
-    small = small * factor
-    nk = hidden // 256
-    return (
-        out_tiles[None],
-        gx.value[None],
-        small[ns : ns + 49].reshape(TAPS, TAPS, channels),
-        small[nk + 4],
-        small[nk + 2],
-        small[nk + 3],
-        grad_in,
-        small[:nk].reshape(-1),
-        grad_out,
-        small[nk],
-        small[nk + 1],
-    )
+    grads = [v.reshape(-1) if v.shape[0] == 1 else v for v in grads]
+    return (out_tiles[None], gx[0][None], *grads)
 
 
 def solution(mesh):

time: 106 us -> 80.6 us (0.76)
  Pallas kernels: 57.6 us -> 48.2 us
  waiting for transfers between devices: 8.26 us -> 1.68 us
  starting transfers between devices: 32.3 us -> 27.1 us
  local copies, waits for them, and re-layouts: 5.93 us -> 1.75 us
    pallas_call x15, Pallas kernels: 57.6 us -> 48.2 us  [call(): pl.pallas_call(kernel, out_shape=tuple((pltpu.VMEM(o[0], o[1]) if len(o)...]
    ppermute x21 -> x14, starting transfers between devices: 21.8 us -> 16.2 us  [crossed(): return lax.ppermute(v, AXES, [(i, i ^ mask) for i in range(n)])]
    ppermute x21 -> x14, waiting for transfers between devices: 5.62 us -> 1.67 us  [crossed(): return lax.ppermute(v, AXES, [(i, i ^ mask) for i in range(n)])]
    ppermute x4, waiting for transfers between devices: 2.65 us -> 0.01 us  [shifted(): lax.ppermute(block, axis, [((i - distance) % n, i) for i in range(n)])]
    unnamed x7 -> x0, local copies, waits for them, and re-layouts: 2.26 us -> none
  transfers between devices with their start and end apart: 25 -> 18, of which waited for: 5 -> 3; matrix products, arithmetic and copies ran while one was open for 3% -> 0% of each run, Pallas kernels for 39% -> 48%
where the time goes in v3:
time: 80.6 us; the launch traced here: 80.2 us
  Pallas kernels  48.2 us (60%)
  starting transfers between devices  27.1 us (34%)
  local copies, waits for them, and re-layouts  1.75 us (2%)
  waiting for transfers between devices  1.68 us (2%)
  between operations  1.5 us (2%)
    pallas_call x15, Pallas kernels, call(): pl.pallas_call(kernel, out_shape=tuple((pltpu.VMEM(o[0], o[1]) if len(o)...  48.2 us
    ppermute x14, starting transfers between devices, crossed(): return lax.ppermute(v, AXES, [(i, i ^ mask) for i in range(n)])  16.2 us
    ppermute x4, starting transfers between devices, shifted(): lax.ppermute(block, axis, [((i - distance) % n, i) for i in range(n)])  10.9 us
    transpose x3, local copies, waits for them, and re-layouts, columns(): x[:, :, lo:lo + RIM].transpose(1, 2, 0, 3)  1.75 us
    ppermute x14, waiting for transfers between devices, crossed(): return lax.ppermute(v, AXES, [(i, i ^ mask) for i in range(n)])  1.67 us
  transfers between devices with their start and end apart: 18, of which 3 were waited for; matrix products, arithmetic and copies ran while one was open for 0% of the time, Pallas kernels for 48%

profile of v3, /device:TPU:0, one launch (start us, length us, event | category | flops | bytes accessed | tf_op | source)
XLA Modules:
  0.0 80.2 jit_solution(15427222868875429157)
XLA Ops:
  0.6 1.5 %slice_bitcast_fusion = (bf16[16,3,8,256]{3,1,0,2:T(4,128)(2,1)S(1)}, bf16[16,3,8,256]{3,1,0,2:T(4,128)(2,1)S(1)}) fusion(bf16[8,16,16,256]{3,2,1,0:T(8,128)(2,1)} %bitcast.25), kind=kLoop, calls=%fused_computation | loop fusion | bytes 786432 | tf_op jit(solution)/shard_map/transpose | solution.py:535
  2.1 0.1 copy.27
  2.3 3.0 %collective-permute-start = (bf16[384,256]{1,0:T(8,128)(2,1)S(1)}, bf16[384,256]{1,0:T(8,128)(2,1)S(1)}, u32[]{:S(2)}, u32[]{:S(2)}) collective-permute-start(bf16[384,256]{1,0:T(8,128)(2,1)S(1)} %bitcast.28), channel_id=1, source_target_pairs={{28,0},{0,4},{4,8},{8,12},{12,16},{16,20},{20,24},{24,28},{29,1},{... | collective-permute-start | bytes 589832 | tf_op jit(solution)/shard_map/ppermute | solution.py:497
  5.3 0.1 copy.28
  5.4 3.1 %collective-permute-start.1 = (bf16[384,256]{1,0:T(8,128)(2,1)S(1)}, bf16[384,256]{1,0:T(8,128)(2,1)S(1)}, u32[]{:S(2)}, u32[]{:S(2)}) collective-permute-start(bf16[384,256]{1,0:T(8,128)(2,1)S(1)} %bitcast.29), channel_id=1, source_target_pairs={{4,0},{8,4},{12,8},{16,12},{20,16},{24,20},{28,24},{0,28},{5,1},{9... | collective-permute-start | bytes 589832 | tf_op jit(solution)/shard_map/ppermute | solution.py:497
  9.2 16.0 %shard_map.212 = (f32[2,22,128,128]{3,2,1,0:T(8,128)S(1)}, f32[2,16,128,128]{3,2,1,0:T(8,128)S(1)}, f32[2,16,128,128]{3,2,1,0:T(8,128)S(1)}, f32[2,22,128,128]{3...) custom-call(s32[8,8]{1,0:T(8,128)} %refs_0_.9, ...), custom_call_target="tpu_custom_call" | custom-call | tf_op jit(solution)/shard_map/pallas_call | solution.py:44
  25.3 8.1 %shard_map.213 = (f32[2,22,24,128]{3,2,1,0:T(8,128)S(1)}, f32[2,22,24,128]{3,2,1,0:T(8,128)S(1)}, f32[2,16,128,128]{3,2,1,0:T(8,128)S(1)}, f32[2,22,128,128]{3,2...) custom-call(s32[8,8]{1,0:T(8,128)} %refs_0_.9, ...), custom_call_target="tpu_custom_call", output_to_operand_aliasing={{2}: (8, {}), {3}: (9, {})} | custom-call | tf_op jit(solution)/shard_map/pallas_call | solution.py:44
  33.5 4.7 %collective-permute-start.10 = (bf16[384,256]{1,0:T(8,128)(2,1)S(1)}, bf16[384,256]{1,0:T(8,128)(2,1)S(1)}, u32[]{:S(2)}, u32[]{:S(2)}) collective-permute-start(bf16[384,256]{1,0:T(8,128)(2,1)S(1)} %get-tuple-element.101), channel_id=1, source_target_pairs={{4,0},{8,4},{12,8},{16,12},{20,16},{24,20},{28,24},{0,28},{5,1},{9... | collective-permute-start | bytes 589832 | tf_op jit(solution)/shard_map/ppermute | solution.py:497
  38.2 0.3 shard_map.214
  38.5 1.7 %collective-permute-start.3 = (bf16[512,128]{1,0:T(8,128)(2,1)S(1)}, bf16[512,128]{1,0:T(8,128)(2,1)S(1)}, u32[]{:S(2)}, u32[]{:S(2)}) collective-permute-start(bf16[512,128]{1,0:T(8,128)(2,1)S(1)} %get-tuple-element.91), channel_id=1, source_target_pairs={{0,2},{1,3},{2,0},{3,1},{4,6},{5,7},{6,4},{7,5},{8,10},{9,11},{10,... | collective-permute-start | bytes 393224 | tf_op jit(solution)/shard_map/ppermute | solution.py:502
  40.2 1.8 %collective-permute-start.5 = (bf16[512,128]{1,0:T(8,128)(2,1)S(1)}, bf16[512,128]{1,0:T(8,128)(2,1)S(1)}, u32[]{:S(2)}, u32[]{:S(2)}) collective-permute-start(bf16[512,128]{1,0:T(8,128)(2,1)S(1)} %get-tuple-element.93), channel_id=1, source_target_pairs={{0,6},{1,7},{2,4},{3,5},{4,2},{5,3},{6,0},{7,1},{8,14},{9,15},{10,... | collective-permute-start | bytes 393224 | tf_op jit(solution)/shard_map/ppermute | solution.py:502
  42.1 4.3 %shard_map.216 = (f32[49,8,128]{2,1,0:T(8,128)S(1)}, f32[8,128]{1,0:T(8,128)S(1)}) custom-call(f32[2,22,128,128]{3,2,1,0:T(8,128)S(1)} %get-tuple-element.70.refs_4_.refs_0_, f32[2,22,24,128]{3,2,1,0:T(8,128)S(1)} %get-tuple-element.81.refs_1_, f32[2,22,24,128]{3,2,1,0:T(8,128)S(1)} %get-tuple-element.82.refs_2_, ...), custom_call_target="tpu_custom_call" | custom-call | tf_op jit(solution)/shard_map/pallas_call | solution.py:44
  46.4 4.4 %shard_map.215 = (f32[49,8,128]{2,1,0:T(8,128)S(1)}, f32[8,128]{1,0:T(8,128)S(1)}) custom-call(f32[2,22,128,128]{3,2,1,0:T(8,128)S(1)} %get-tuple-element.70.refs_4_.refs_0_, f32[2,22,24,128]{3,2,1,0:T(8,128)S(1)} %get-tuple-element.81.refs_1_, f32[2,22,24,128]{3,2,1,0:T(8,128)S(1)} %get-tuple-element.82.refs_2_, ...), custom_call_target="tpu_custom_call" | custom-call | tf_op jit(solution)/shard_map/pallas_call | solution.py:44
  50.9 0.2 shard_map.217
  51.0 0.6 collective-permute-start.6
  51.6 2.6 %collective-permute-start.7 = (bf16[128,128]{1,0:T(8,128)(2,1)S(1)}, bf16[128,128]{1,0:T(8,128)(2,1)S(1)}, u32[]{:S(2)}, u32[]{:S(2)}) collective-permute-start(bf16[128,128]{1,0:T(8,128)(2,1)S(1)} %get-tuple-element.98), channel_id=1, source_target_pairs={{0,16},{1,17},{2,18},{3,19},{4,20},{5,21},{6,22},{7,23},{8,24},{9,... | collective-permute-start | bytes 98312 | tf_op jit(solution)/shard_map/ppermute | solution.py:502
  54.2 1.3 %collective-permute-start.8 = (bf16[128,128]{1,0:T(8,128)(2,1)S(1)}, bf16[128,128]{1,0:T(8,128)(2,1)S(1)}, u32[]{:S(2)}, u32[]{:S(2)}) collective-permute-start(bf16[128,128]{1,0:T(8,128)(2,1)S(1)} %get-tuple-element.99), channel_id=1, source_target_pairs={{0,24},{1,25},{2,26},{3,27},{4,28},{5,29},{6,30},{7,31},{8,16},{9,... | collective-permute-start | bytes 98312 | tf_op jit(solution)/shard_map/ppermute | solution.py:502
  55.5 0.9 %shard_map.218 = (f32[2,22,24,128]{3,2,1,0:T(8,128)S(1)}, f32[2,22,24,128]{3,2,1,0:T(8,128)S(1)}, f32[2,22,128,128]{3,2,1,0:T(8,128)S(1)}) custom-call(s32[8,8]{1,0:T(8,128)} %refs_0_.9, bf16[384,256]{1,0:T(8,128)(2,1)S(1)} %collective-permute-done.9.refs_1_, bf16[384,256]{1,0:T(8,128)(2,1)S(1)} %collective-permute-done.10.refs_2_, ...), custom_call_target="tpu_custom_call", output_to_operand_aliasing={{2}: (3, {})} | custom-call | tf_op jit(solution)/shard_map/pallas_call | solution.py:44
  56.4 2.6 %shard_map.219 = (bf16[8,4,16,256]{3,2,1,0:T(8,128)(2,1)S(1)}, f32[8,128]{1,0:T(8,128)S(1)}) custom-call(s32[1]{0:T(128)S(6)} %copy.32.refs_1_.refs_0_, f32[2,22,24,128]{3,2,1,0:T(8,128)S(1)} %get-tuple-element.103.refs_1_, f32[2,22,24,128]{3,2,1,0:T(8,128)S(1)} %get-tuple-element.104.refs_2_, f32[2,22,128,128]{3,2,1,0:T(8,128)S(1)} %get-tuple-element.105.refs_3_, ...), custom_call_target="tpu_custom_call" | custom-call | tf_op jit(solution)/shard_map/pallas_call | solution.py:44
  59.1 0.9 %collective-permute-done.8.refs_6_ = bf16[128,128]{1,0:T(8,128)(2,1)S(1)} collective-permute-done((bf16[128,128]{1,0:T(8,128)(2,1)S(1)}, bf16[128,128]{1,0:T(8,128)(2,1)S(1)}, u32[]{:S(2)}, u32[]{:S(2)}) %collective-permute-start.8) | collective-permute-done | bytes 32800 | tf_op jit(solution)/shard_map/ppermute | solution.py:502
  59.9 0.1 shard_map.220
  60.1 1.8 %collective-permute-start.13 = (bf16[256,128]{1,0:T(8,128)(2,1)S(1)}, bf16[256,128]{1,0:T(8,128)(2,1)S(1)}, u32[]{:S(2)}, u32[]{:S(2)}) collective-permute-start(bf16[256,128]{1,0:T(8,128)(2,1)S(1)} %get-tuple-element.107.refs_1_), channel_id=1, source_target_pairs={{0,24},{1,25},{2,26},{3,27},{4,28},{5,29},{6,30},{7,31},{8,16},{9,... | collective-permute-start | bytes 196616 | tf_op jit(solution)/shard_map/ppermute | solution.py:502
  61.8 2.7 %collective-permute-start.11 = (bf16[256,128]{1,0:T(8,128)(2,1)S(1)}, bf16[256,128]{1,0:T(8,128)(2,1)S(1)}, u32[]{:S(2)}, u32[]{:S(2)}) collective-permute-start(bf16[256,128]{1,0:T(8,128)(2,1)S(1)} %get-tuple-element.107.refs_1_), channel_id=1, source_target_pairs={{0,8},{1,9},{2,10},{3,11},{4,12},{5,13},{6,14},{7,15},{8,0},{9,1},... | collective-permute-start | bytes 196616 | tf_op jit(solution)/shard_map/ppermute | solution.py:502
  64.5 3.1 %shard_map.221 = (bf16[8,9,16,256]{3,2,1,0:T(8,128)(2,1)S(1)}, f32[8,128]{1,0:T(8,128)S(1)}) custom-call(s32[1]{0:T(128)S(6)} %copy.32.refs_1_.refs_0_, f32[2,22,24,128]{3,2,1,0:T(8,128)S(1)} %get-tuple-element.103.refs_1_, f32[2,22,24,128]{3,2,1,0:T(8,128)S(1)} %get-tuple-element.104.refs_2_, f32[2,22,128,128]{3,2,1,0:T(8,128)S(1)} %get-tuple-element.105.refs_3_, ...), custom_call_target="tpu_custom_call" | custom-call | tf_op jit(solution)/shard_map/pallas_call | solution.py:44
  67.6 0.4 collective-permute-done.12.refs_3_
  68.0 0.7 collective-permute-start.16
  68.7 2.3 %collective-permute-start.15 = (bf16[640,128]{1,0:T(8,128)(2,1)S(1)}, bf16[640,128]{1,0:T(8,128)(2,1)S(1)}, u32[]{:S(2)}, u32[]{:S(2)}) collective-permute-start(bf16[640,128]{1,0:T(8,128)(2,1)S(1)} %get-tuple-element.111.refs_1_), channel_id=1, source_target_pairs={{0,4},{1,5},{2,6},{3,7},{4,0},{5,1},{6,2},{7,3},{8,12},{9,13},{10,... | collective-permute-start | bytes 491528 | tf_op jit(solution)/shard_map/ppermute | solution.py:502
  71.1 0.5 collective-permute-start.14
  71.6 5.0 %shard_map.223 = (bf16[8,16,16,256]{3,2,1,0:T(8,128)(2,1)}, f32[8,128]{1,0:T(8,128)S(1)}) custom-call(s32[1]{0:T(128)S(6)} %copy.32.refs_1_.refs_0_, f32[2,22,24,128]{3,2,1,0:T(8,128)S(1)} %get-tuple-element.103.refs_1_, f32[2,22,24,128]{3,2,1,0:T(8,128)S(1)} %get-tuple-element.104.refs_2_, f32[2,22,128,128]{3,2,1,0:T(8,128)S(1)} %get-tuple-element.105.refs_3_, ...), custom_call_target="tpu_custom_call" | custom-call | tf_op jit(solution)/shard_map/pallas_call | solution.py:44
  76.7 1.5 %shard_map.225 = (bf16[8,16,16,256]{3,2,1,0:T(8,128)(2,1)}, f32[8,128]{1,0:T(8,128)S(1)}) custom-call(s32[1]{0:T(128)S(6)} %copy.32.refs_1_.refs_0_, f32[2,16,128,128]{3,2,1,0:T(8,128)S(1)} %get-tuple-element.80.refs_1_, f32[8,128]{1,0:T(8,128)S(1)} %get-tuple-element.115.refs_2_), custom_call_target="tpu_custom_call" | custom-call | tf_op jit(solution)/shard_map/pallas_call | solution.py:44
  78.3 0.4 collective-permute-done.17.refs_2_
  78.7 1.5 %shard_map.226 = (f32[7,7,256]{2,1,0:T(8,128)}, f32[1,256]{1,0:T(1,128)}, f32[1,256]{1,0:T(1,128)}, f32[1,256]{1,0:T(1,128)}, f32[256,1024]{1,0:T(8,128)}, /*ind...) custom-call(s32[1]{0:T(128)} %bitcast.refs_2_.refs_1_.refs_0_, ...), custom_call_target="tpu_custom_call" | custom-call | tf_op jit(solution)/shard_map/pallas_call | solution.py:44
  (22 shorter events, 0.3 us)
Async XLA Ops:
  2.3 23.0 %collective-permute-start = (bf16[384,256]{1,0:T(8,128)(2,1)S(1)}, bf16[384,256]{1,0:T(8,128)(2,1)S(1)}, u32[]{:S(2)}, u32[]{:S(2)}) collective-permute-start(bf16[384,256]{1,0:T(8,128)(2,1)S(1)} %bitcast.28), channel_id=1, source_target_pairs={{28,0},{0,4},{4,8},{8,12},{12,16},{16,20},{20,24},{24,28},{29,1},{... | collective-permute-start | bytes 589832 | tf_op jit(solution)/shard_map/ppermute | solution.py:497
  5.4 19.8 %collective-permute-start.1 = (bf16[384,256]{1,0:T(8,128)(2,1)S(1)}, bf16[384,256]{1,0:T(8,128)(2,1)S(1)}, u32[]{:S(2)}, u32[]{:S(2)}) collective-permute-start(bf16[384,256]{1,0:T(8,128)(2,1)S(1)} %bitcast.29), channel_id=1, source_target_pairs={{4,0},{8,4},{12,8},{16,12},{20,16},{24,20},{28,24},{0,28},{5,1},{9... | collective-permute-start | bytes 589832 | tf_op jit(solution)/shard_map/ppermute | solution.py:497
  33.4 4.9 %collective-permute-start.2 = (bf16[2048,128]{1,0:T(8,128)(2,1)S(1)}, bf16[2048,128]{1,0:T(8,128)(2,1)S(1)}, u32[]{:S(2)}, u32[]{:S(2)}) collective-permute-start(bf16[2048,128]{1,0:T(8,128)(2,1)S(1)} %get-tuple-element.85), channel_id=1, source_target_pairs={{0,1},{1,0},{2,3},{3,2},{4,5},{5,4},{6,7},{7,6},{8,9},{9,8},{10,11... | collective-permute-start | bytes 1572872 | tf_op jit(solution)/shard_map/ppermute | solution.py:502
  33.4 22.1 %collective-permute-start.9 = (bf16[384,256]{1,0:T(8,128)(2,1)S(1)}, bf16[384,256]{1,0:T(8,128)(2,1)S(1)}, u32[]{:S(2)}, u32[]{:S(2)}) collective-permute-start(bf16[384,256]{1,0:T(8,128)(2,1)S(1)} %get-tuple-element.100), channel_id=1, source_target_pairs={{28,0},{0,4},{4,8},{8,12},{12,16},{16,20},{20,24},{24,28},{29,1},{... | collective-permute-start | bytes 589832 | tf_op jit(solution)/shard_map/ppermute | solution.py:497
  33.5 22.0 %collective-permute-start.10 = (bf16[384,256]{1,0:T(8,128)(2,1)S(1)}, bf16[384,256]{1,0:T(8,128)(2,1)S(1)}, u32[]{:S(2)}, u32[]{:S(2)}) collective-permute-start(bf16[384,256]{1,0:T(8,128)(2,1)S(1)} %get-tuple-element.101), channel_id=1, source_target_pairs={{4,0},{8,4},{12,8},{16,12},{20,16},{24,20},{28,24},{0,28},{5,1},{9... | collective-permute-start | bytes 589832 | tf_op jit(solution)/shard_map/ppermute | solution.py:497
  38.5 12.3 %collective-permute-start.3 = (bf16[512,128]{1,0:T(8,128)(2,1)S(1)}, bf16[512,128]{1,0:T(8,128)(2,1)S(1)}, u32[]{:S(2)}, u32[]{:S(2)}) collective-permute-start(bf16[512,128]{1,0:T(8,128)(2,1)S(1)} %get-tuple-element.91), channel_id=1, source_target_pairs={{0,2},{1,3},{2,0},{3,1},{4,6},{5,7},{6,4},{7,5},{8,10},{9,11},{10,... | collective-permute-start | bytes 393224 | tf_op jit(solution)/shard_map/ppermute | solution.py:502
  40.2 10.6 %collective-permute-start.4 = (bf16[512,128]{1,0:T(8,128)(2,1)S(1)}, bf16[512,128]{1,0:T(8,128)(2,1)S(1)}, u32[]{:S(2)}, u32[]{:S(2)}) collective-permute-start(bf16[512,128]{1,0:T(8,128)(2,1)S(1)} %get-tuple-element.92), channel_id=1, source_target_pairs={{0,4},{1,5},{2,6},{3,7},{4,0},{5,1},{6,2},{7,3},{8,12},{9,13},{10,... | collective-permute-start | bytes 393224 | tf_op jit(solution)/shard_map/ppermute | solution.py:502
  40.2 10.6 %collective-permute-start.5 = (bf16[512,128]{1,0:T(8,128)(2,1)S(1)}, bf16[512,128]{1,0:T(8,128)(2,1)S(1)}, u32[]{:S(2)}, u32[]{:S(2)}) collective-permute-start(bf16[512,128]{1,0:T(8,128)(2,1)S(1)} %get-tuple-element.93), channel_id=1, source_target_pairs={{0,6},{1,7},{2,4},{3,5},{4,2},{5,3},{6,0},{7,1},{8,14},{9,15},{10,... | collective-permute-start | bytes 393224 | tf_op jit(solution)/shard_map/ppermute | solution.py:502
  51.0 8.0 %collective-permute-start.6 = (bf16[128,128]{1,0:T(8,128)(2,1)S(1)}, bf16[128,128]{1,0:T(8,128)(2,1)S(1)}, u32[]{:S(2)}, u32[]{:S(2)}) collective-permute-start(bf16[128,128]{1,0:T(8,128)(2,1)S(1)} %get-tuple-element.97), channel_id=1, source_target_pairs={{0,8},{1,9},{2,10},{3,11},{4,12},{5,13},{6,14},{7,15},{8,0},{9,1},... | collective-permute-start | bytes 98312 | tf_op jit(solution)/shard_map/ppermute | solution.py:502
  51.6 7.4 %collective-permute-start.7 = (bf16[128,128]{1,0:T(8,128)(2,1)S(1)}, bf16[128,128]{1,0:T(8,128)(2,1)S(1)}, u32[]{:S(2)}, u32[]{:S(2)}) collective-permute-start(bf16[128,128]{1,0:T(8,128)(2,1)S(1)} %get-tuple-element.98), channel_id=1, source_target_pairs={{0,16},{1,17},{2,18},{3,19},{4,20},{5,21},{6,22},{7,23},{8,24},{9,... | collective-permute-start | bytes 98312 | tf_op jit(solution)/shard_map/ppermute | solution.py:502
  54.2 5.7 %collective-permute-start.8 = (bf16[128,128]{1,0:T(8,128)(2,1)S(1)}, bf16[128,128]{1,0:T(8,128)(2,1)S(1)}, u32[]{:S(2)}, u32[]{:S(2)}) collective-permute-start(bf16[128,128]{1,0:T(8,128)(2,1)S(1)} %get-tuple-element.99), channel_id=1, source_target_pairs={{0,24},{1,25},{2,26},{3,27},{4,28},{5,29},{6,30},{7,31},{8,16},{9,... | collective-permute-start | bytes 98312 | tf_op jit(solution)/shard_map/ppermute | solution.py:502
  60.1 7.6 %collective-permute-start.13 = (bf16[256,128]{1,0:T(8,128)(2,1)S(1)}, bf16[256,128]{1,0:T(8,128)(2,1)S(1)}, u32[]{:S(2)}, u32[]{:S(2)}) collective-permute-start(bf16[256,128]{1,0:T(8,128)(2,1)S(1)} %get-tuple-element.107.refs_1_), channel_id=1, source_target_pairs={{0,24},{1,25},{2,26},{3,27},{4,28},{5,29},{6,30},{7,31},{8,16},{9,... | collective-permute-start | bytes 196616 | tf_op jit(solution)/shard_map/ppermute | solution.py:502
  61.8 6.2 %collective-permute-start.12 = (bf16[256,128]{1,0:T(8,128)(2,1)S(1)}, bf16[256,128]{1,0:T(8,128)(2,1)S(1)}, u32[]{:S(2)}, u32[]{:S(2)}) collective-permute-start(bf16[256,128]{1,0:T(8,128)(2,1)S(1)} %get-tuple-element.107.refs_1_), channel_id=1, source_target_pairs={{0,16},{1,17},{2,18},{3,19},{4,20},{5,21},{6,22},{7,23},{8,24},{9,... | collective-permute-start | bytes 196616 | tf_op jit(solution)/shard_map/ppermute | solution.py:502
  61.8 6.2 %collective-permute-start.11 = (bf16[256,128]{1,0:T(8,128)(2,1)S(1)}, bf16[256,128]{1,0:T(8,128)(2,1)S(1)}, u32[]{:S(2)}, u32[]{:S(2)}) collective-permute-start(bf16[256,128]{1,0:T(8,128)(2,1)S(1)} %get-tuple-element.107.refs_1_), channel_id=1, source_target_pairs={{0,8},{1,9},{2,10},{3,11},{4,12},{5,13},{6,14},{7,15},{8,0},{9,1},... | collective-permute-start | bytes 196616 | tf_op jit(solution)/shard_map/ppermute | solution.py:502
  68.0 8.5 %collective-permute-start.16 = (bf16[640,128]{1,0:T(8,128)(2,1)S(1)}, bf16[640,128]{1,0:T(8,128)(2,1)S(1)}, u32[]{:S(2)}, u32[]{:S(2)}) collective-permute-start(bf16[640,128]{1,0:T(8,128)(2,1)S(1)} %get-tuple-element.111.refs_1_), channel_id=1, source_target_pairs={{0,6},{1,7},{2,4},{3,5},{4,2},{5,3},{6,0},{7,1},{8,14},{9,15},{10,... | collective-permute-start | bytes 491528 | tf_op jit(solution)/shard_map/ppermute | solution.py:502
  68.7 7.8 %collective-permute-start.15 = (bf16[640,128]{1,0:T(8,128)(2,1)S(1)}, bf16[640,128]{1,0:T(8,128)(2,1)S(1)}, u32[]{:S(2)}, u32[]{:S(2)}) collective-permute-start(bf16[640,128]{1,0:T(8,128)(2,1)S(1)} %get-tuple-element.111.refs_1_), channel_id=1, source_target_pairs={{0,4},{1,5},{2,6},{3,7},{4,0},{5,1},{6,2},{7,3},{8,12},{9,13},{10,... | collective-permute-start | bytes 491528 | tf_op jit(solution)/shard_map/ppermute | solution.py:502
  71.1 5.5 %collective-permute-start.14 = (bf16[640,128]{1,0:T(8,128)(2,1)S(1)}, bf16[640,128]{1,0:T(8,128)(2,1)S(1)}, u32[]{:S(2)}, u32[]{:S(2)}) collective-permute-start(bf16[640,128]{1,0:T(8,128)(2,1)S(1)} %get-tuple-element.111.refs_1_), channel_id=1, source_target_pairs={{0,2},{1,3},{2,0},{3,1},{4,6},{5,7},{6,4},{7,5},{8,10},{9,11},{10,... | collective-permute-start | bytes 491528 | tf_op jit(solution)/shard_map/ppermute | solution.py:502
  76.7 2.0 %collective-permute-start.17 = (bf16[2176,128]{1,0:T(8,128)(2,1)S(1)}, bf16[2176,128]{1,0:T(8,128)(2,1)S(1)}, u32[]{:S(2)}, u32[]{:S(2)}) collective-permute-start(bf16[2176,128]{1,0:T(8,128)(2,1)S(1)} %get-tuple-element.118.refs_1_), channel_id=1, source_target_pairs={{0,1},{1,0},{2,3},{3,2},{4,5},{5,4},{6,7},{7,6},{8,9},{9,8},{10,11... | collective-permute-start | bytes 1671176 | tf_op jit(solution)/shard_map/ppermute | solution.py:502

commit v4 on v3

--- a/solution.py
+++ b/solution.py
@@ -20,6 +20,7 @@
 AXES = ("space", "dp")
 VMEM_LIMIT = 32 * 1024 * 1024
 KEEP = True
+WORK = 8_000_000_000
 
 
 def vmem_spec():
@@ -30,7 +31,7 @@
     return pl.BlockSpec(memory_space=pltpu.SMEM)
 
 
-def call(body, outs, ins, scratch=(), smem=0, alias=None, after=(), token=False):
+def call(body, outs, ins, scratch=(), smem=0, alias=None, after=(), token=False, work=0):
     n_ins = len(ins)
     n_out = len(outs) + token
     outs = list(outs) + [((8, LANES), F32, KEEP)] * token
@@ -48,6 +49,7 @@
         out_specs=tuple(vmem_spec() for _ in outs),
         scratch_shapes=list(scratch),
         input_output_aliases=alias or {},
+        cost_estimate=pl.CostEstimate(flops=work, transcendentals=0, bytes_accessed=work // 256) if work else None,
         compiler_params=pltpu.CompilerParams(vmem_limit_bytes=VMEM_LIMIT),
     )(*[placed(v) for v in (*ins, *after)])
     return tuple(Kept(r) if len(o) > 2 else r for r, o in zip(res, outs))
@@ -166,19 +168,19 @@
     gb = (dy * scale[...]).astype(BF16)
     unit_t = unit.T
     gb_t = gb.T
-    branch = jnp.zeros(conv.shape, F32)
-    grad_unit = jnp.zeros(conv.shape, F32)
+    acts, gps = [], []
     for k in range(0, hidden, 256):
         ks = slice(k, k + 256)
-        pre = dot(unit, win[:, ks]) + bias_in[:, ks]
-        act, slope = gelu_pair(pre)
-        act = act.astype(BF16)
+        act, slope = gelu_pair(dot(unit, win[:, ks]) + bias_in[:, ks])
         gp = (dot_t(gb, wout[ks, :]) * slope).astype(BF16)
-        branch = branch + dot(act, wout[ks, :])
-        grad_unit = grad_unit + dot_t(gp, win[:, ks])
+        add_sum(k // 256, fold(gp.astype(F32)))
+        acts.append(act.astype(BF16))
+        gps.append(gp)
+    for k, act, gp in zip(range(0, hidden, 256), acts, gps):
         add_dw(0, k, dot(unit_t, gp))
         add_dw(1, k, dot(gb_t, act))
-        add_sum(k // 256, fold(gp.astype(F32)))
+    branch = dot(jnp.concatenate(acts, axis=1), wout[...])
+    grad_unit = dot_t(jnp.concatenate(gps, axis=1), win[...])
     branch = branch + bias_out[...]
     out = x + scale[...] * branch
     scaled = grad_unit * gain[...]
@@ -235,11 +237,8 @@
     n_place, nbr_ref, cnt_ref, *refs,
 ):
     (x_ref, dy_ref, k_ref, win, wout, bias_in, bias_out, scale, gain, shift, conv_bias) = refs[n_place : n_place + 11]
-    center_ref, dyt_ref, out_ref, g_ref, dw_ref, sums_ref, k8_ref, win_kept, wout_kept, vec_kept, conv_ref = refs[
-        n_place + 11 :
-    ]
+    center_ref, dyt_ref, conv_ref, k8_ref, win_kept, wout_kept, vec_kept = refs[n_place + 11 :]
     live = cnt_ref[0]
-    channels = win.shape[0]
     spread_taps(k_ref, k8_ref, False)
     win_kept[...] = win[...]
     wout_kept[...] = wout[...]
@@ -256,57 +255,34 @@
 
     lax.fori_loop(0, 16, turn, 0)
     rims_of(center_ref, nbr_ref)
-    params = (win, wout, bias_in, bias_out, scale, gain, shift, conv_bias)
     n, c0 = 10, 3
-    cols = slice(c0 * 8, (c0 + n) * 8)
     pads = (None, center_ref, None)
-
-    def add_dw(which, k, v):
-        dw_ref[which * channels : (which + 1) * channels, k : k + 256] = v
-
-    def add_sum(which, v):
-        sums_ref[which] = v
 
     def conv(q, carry):
         for h in range(2):
             accs = conv_wide(pads, k8_ref, h, q, c0, n)
-            conv_ref[pl.ds(pl.multiple_of(q * n * 8, 8), n * 8), lanes(h)] = jnp.concatenate(accs, axis=0)
+            conv_ref[h, q, c0 * 8 : (c0 + n) * 8, :] = jnp.concatenate(accs, axis=0)
         return carry
 
-    lax.fori_loop(0, 16, conv, 0)
-    x = rows_of(center_ref, 3, 16, c0, n)
-    dy = rows_of(dyt_ref, 0, 16, c0, n)
-    out, g = dense_block(conv_ref[...], x, dy, params, add_dw, add_sum)
-    for q in range(16):
-        for h in range(2):
-            out_ref[h, q, cols, :] = out[q * n * 8 : (q + 1) * n * 8, lanes(h)]
-            g_ref[h, 3 + q, cols, :] = g[q * n * 8 : (q + 1) * n * 8, lanes(h)]
+    lax.fori_loop(0, 16, conv, 0, unroll=2)
 
 
 def edge_kernel(
-    nbr_ref, place_ref, hw_ref, he_ref, center_ref, dyt_ref, dw_in, sums_in, out_in, g_in, k8_ref, win, wout, vec,
-    west_ref, east_ref, out_ref, g_ref, send_l, send_r, own_ref, sent_ref, sums_ref,
-    conv_ref, travel_ref,
+    nbr_ref, hw_ref, he_ref, center_ref, dyt_ref, k8_ref, win, wout, vec,
+    west_ref, east_ref, out_ref, g_ref, send_l, send_r, dw_ref, sums_ref,
+    conv_ref,
 ):
-    core = place_ref[0]
-    channels, hidden = win.shape
+    channels = win.shape[0]
     side_rim(west_ref, hw_ref, nbr_ref, 2, 4, 6)
     side_rim(east_ref, he_ref, nbr_ref, 3, 5, 7)
-    widths = (hidden,) + (channels,) * 5
-    params = (win, wout) + tuple(vec.at[i : i + 1, 0:w] for i, w in enumerate(widths))
+    params = (win, wout) + vectors(vec, win)
     pads = (west_ref, center_ref, east_ref)
 
     def add_dw(which, k, v):
-        v = dw_in[which * channels : (which + 1) * channels, k : k + 256] + v
-        if which == 1:
-            v = v.T
-        v = v.astype(BF16)
-        for side in range(2):
-            row = k * 2 + side * 256 if which == 0 else side * hidden + k
-            travel_ref[which, row : row + 256, :] = v[:, lanes(side)]
+        dw_ref[which * channels : (which + 1) * channels, k : k + 256] = v
 
     def add_sum(which, v):
-        sums_ref[which] = sums_in[which] + v
+        sums_ref[which] = v
 
     def conv(m, carry):
         r0 = m * 8
@@ -338,6 +314,43 @@
         for side, send in enumerate((send_l, send_r)):
             v = [g[(q + s) * 48 + side * 24 : (q + s) * 48 + side * 24 + 24] for s in range(2)]
             send[q * 24 : q * 24 + 48, :] = jnp.concatenate(v, axis=0).astype(BF16)
+
+
+def vectors(vec, win):
+    channels, hidden = win.shape
+    return tuple(vec.at[i : i + 1, 0:w] for i, w in enumerate((hidden,) + (channels,) * 5))
+
+
+def middle_kernel(
+    place_ref, center_ref, dyt_ref, conv_ref, dw_in, sums_in, out_in, g_in, win, wout, vec,
+    out_ref, g_ref, own_ref, sent_ref, sums_ref,
+    travel_ref,
+):
+    core = place_ref[0]
+    channels, hidden = win.shape
+    params = (win, wout) + vectors(vec, win)
+    n, c0 = 10, 3
+    cols = slice(c0 * 8, (c0 + n) * 8)
+
+    def add_dw(which, k, v):
+        v = dw_in[which * channels : (which + 1) * channels, k : k + 256] + v
+        if which == 1:
+            v = v.T
+        v = v.astype(BF16)
+        for side in range(2):
+            row = k * 2 + side * 256 if which == 0 else side * hidden + k
+            travel_ref[which, row : row + 256, :] = v[:, lanes(side)]
+
+    def add_sum(which, v):
+        sums_ref[which] = sums_in[which] + v
+
+    x = rows_of(center_ref, 3, 16, c0, n)
+    dy = rows_of(dyt_ref, 0, 16, c0, n)
+    out, g = dense_block(rows_of(conv_ref, 0, 16, c0, n), x, dy, params, add_dw, add_sum)
+    for q in range(16):
+        for h in range(2):
+            out_ref[h, q, cols, :] = out[q * n * 8 : (q + 1) * n * 8, lanes(h)]
+            g_ref[h, 3 + q, cols, :] = g[q * n * 8 : (q + 1) * n * 8, lanes(h)]
     own_ref[...] = travel_ref[core]
     sent_ref[...] = travel_ref[1 - core]
 
@@ -374,7 +387,7 @@
                 new.append(accs[j] + terms[0])
             return tuple(new)
 
-        accs = lax.fori_loop(0, 16, row, tuple(jnp.zeros((8, LANES), F32) for _ in range(TAPS)))
+        accs = lax.fori_loop(0, 16, row, tuple(jnp.zeros((8, LANES), F32) for _ in range(TAPS)), unroll=4)
         for j in range(TAPS):
             acc_ref[i * TAPS + j] = accs[j]
         return carry
@@ -448,7 +461,8 @@
     mine = place_ref[0]
     total = jnp.zeros((LANES, LANES), F32)
     for k, part in enumerate(parts):
-        out[pl.ds(pl.multiple_of((mine ^ k) * rows, 16), rows), :] = part[0:rows, :]
+        at = mine ^ k
+        out[pl.ds(pl.multiple_of(at * rows, 16), rows), :] = part[0:rows, :]
         total = total + part[rows : rows + LANES, :].astype(F32)
     out[len(parts) * rows : len(parts) * rows + LANES, :] = total.astype(BF16)
 
@@ -528,7 +542,7 @@
     weights = tuple(Far(w) for w in weights)
     conv_kernel = Far(conv_kernel)
     me = lax.axis_index(AXES)
-    place = [((me // bit) % size).astype(jnp.int32).reshape(1) for bit, size in groups()]
+    place = {g: ((me // g[0]) % g[1]).astype(jnp.int32).reshape(1) for g in groups()}
     neighbours = Far(neighbours)
 
     def columns(lo):
@@ -542,49 +556,58 @@
     side = (2, edge + 2 * RIM, RIM * slots, LANES)
     tall = (2, edge + 2 * RIM, edge * slots, LANES)
     halo = (edge * RIM * slots, channels)
-    dw_shape = (2 * channels, hidden)
     sums_shape = (ns, 8, channels)
     tiles = (slots, edge, edge, channels)
     travel = (channels * hidden // LANES, LANES)
+    dw_shape = (2 * channels, hidden)
 
     spread = (2, TAPS * TAPS, 8, LANES)
-    center, dyt, full, g, dw, sums, *kept = call(
+    center, dyt, conv, *kept = call(
         functools.partial(inner_kernel, len(place)),
-        [(tall, F32, KEEP), (half, F32, KEEP), (half, F32, KEEP), (tall, F32, KEEP), (dw_shape, F32, KEEP),
-         (sums_shape, F32, KEEP), (spread, F32, KEEP), (proj_in.shape, BF16, KEEP), (proj_out.shape, BF16, KEEP),
-         ((8, hidden), F32, KEEP)],
-        (neighbours, tile_count, *place, Far(x), Far(dy), conv_kernel) + weights,
-        [pltpu.VMEM((edge * (edge - 2 * RIM) * slots, channels), F32)],
+        [(tall, F32, KEEP), (half, F32, KEEP), (half, F32, KEEP), (spread, F32, KEEP), (proj_in.shape, BF16, KEEP),
+         (proj_out.shape, BF16, KEEP), ((8, hidden), F32, KEEP)],
+        (neighbours, tile_count, *place.values(), Far(x), Far(dy), conv_kernel) + weights,
         smem=2 + len(place),
     )
-    west, east, full, g, send_l, send_r, held, sent, sums = call(
+    west, east, full, g, send_l, send_r, dw, sums = call(
         edge_kernel,
         [(side, F32, KEEP), (side, F32, KEEP), (half, F32, KEEP), (tall, F32, KEEP), (halo, BF16), (halo, BF16),
-         (travel, BF16), (travel, BF16), (sums_shape, F32, KEEP)],
-        (neighbours, place[0], from_west, from_east, center, dyt, dw, sums, full, g, *kept),
-        [pltpu.VMEM((edge * 2 * RIM * slots, channels), F32), pltpu.VMEM((2,) + travel, BF16)],
-        smem=2,
-        alias={8: 2, 9: 3},
+         (dw_shape, F32, KEEP), (sums_shape, F32, KEEP)],
+        (neighbours, from_west, from_east, center, dyt, *kept),
+        [pltpu.VMEM((edge * 2 * RIM * slots, channels), F32)],
+        smem=1,
+    )
+    grad_from_east = shifted(send_l, "space", -1)
+    grad_from_west = shifted(send_r, "space", 1)
+    full, g, held, sent, sums = call(
+        middle_kernel,
+        [(half, F32, KEEP), (tall, F32, KEEP), (travel, BF16), (travel, BF16), (sums_shape, F32, KEEP)],
+        (place[1, 2], center, dyt, conv, dw, sums, full, g, *kept[1:]),
+        [pltpu.VMEM((2,) + travel, BF16)],
+        smem=1,
+        alias={6: 0, 7: 1},
     )
     later = groups()[1:]
     arrived = [crossed(sent, 1)]
-    grad_from_east = shifted(send_l, "space", -1)
-    grad_from_west = shifted(send_r, "space", 1)
-
-    filler = ()
+
+    *sides, g, done = call(
+        sides_kernel, [(side, F32, KEEP), (side, F32, KEEP), (tall, F32, KEEP)],
+        (neighbours, grad_from_west, grad_from_east, g), smem=1, alias={3: 2}, token=True, work=WORK,
+    )
+    filler = (done,)
     taps = []
 
     def tap(h):
         v, done = call(
             functools.partial(tap_kernel, h), [((TAPS * TAPS, 8, LANES), F32, KEEP)], (center, west, east, g),
-            after=(begun,), token=True,
+            after=(begun,), token=True, work=WORK,
         )
         taps.append(v)
         return done
 
-    sides = None
+
     gx = ()
-    cuts = [0, 4, 9, edge]
+    cuts = [0, 6, 10, edge]
 
     def back():
         nonlocal gx
@@ -605,7 +628,7 @@
         held, *parts, begun = call(
             functools.partial(scatter_kernel, size),
             [((held.shape[0] // size, LANES), BF16)] * size,
-            (place[n + 1], held, *arrived),
+            (place[bit, size], held, *arrived),
             smem=1,
             after=filler,
             token=True,
@@ -615,10 +638,6 @@
         if n == 0:
             filler = (tap(0), tap(1))
         if n == 1:
-            *sides, g = call(
-                sides_kernel, [(side, F32, KEEP), (side, F32, KEEP), (tall, F32, KEEP)],
-                (neighbours, grad_from_west, grad_from_east, g), smem=1, alias={3: 2}, after=(begun,),
-            )
             filler = (back(),)
     held, begun = call(
         finish_kernel, [((held.shape[0] + LANES, LANES), BF16)], (*taps, sums, held, *arrived), after=filler, token=True
@@ -630,7 +649,7 @@
         rows = (held.shape[0] - LANES) * size + LANES
         held, begun = call(
             gather_kernel, [((rows, LANES), BF16)],
-            (place[len(later) - n], *parts), smem=1, after=filler, token=True,
+            (place[bit, size], *parts), smem=1, after=filler, token=True,
         )
     out_tiles, done = call(tiles_kernel, [(tiles, BF16)], (tile_count, full), smem=1, after=(begun,), token=True)
     factor = 1.0 / math.sqrt(lax.axis_size("dp") * lax.axis_size("space") * slots * edge * edge)
@@ -639,7 +658,7 @@
     grads = call(
         functools.partial(last_kernel, factor),
         [*small, ((channels, hidden), F32), ((1, hidden), F32), ((hidden, channels), F32), vec, vec],
-        (place[0], held, crossed(held, 1)),
+        (place[1, 2], held, crossed(held, 1)),
         smem=1,
         after=(done,),
     )

time: 80.6 us -> 78.7 us (0.976)
  Pallas kernels: 48.2 us -> 45.7 us
    pallas_call x15 -> x16, Pallas kernels: 48.2 us -> 45.7 us  [call(): pl.pallas_call(kernel, out_shape=tuple((pltpu.VMEM(o[0], o[1]) if len(o)...]
  transfers between devices with their start and end apart: 18 -> 18, of which waited for: 3 -> 4; matrix products, arithmetic and copies ran while one was open for 0% -> 0% of each run, Pallas kernels for 48% -> 46%
where the time goes in v4:
time: 78.7 us; the launch traced here: 78.3 us
  Pallas kernels  45.7 us (58%)
  starting transfers between devices  27 us (34%)
  waiting for transfers between devices  2.19 us (3%)
  local copies, waits for them, and re-layouts  1.75 us (2%)
  between operations  1.54 us (2%)
    pallas_call x16, Pallas kernels, call(): pl.pallas_call(kernel, out_shape=tuple((pltpu.VMEM(o[0], o[1]) if len(o)...  45.7 us
    ppermute x14, starting transfers between devices, crossed(): return lax.ppermute(v, AXES, [(i, i ^ mask) for i in range(n)])  16.1 us
    ppermute x4, starting transfers between devices, shifted(): lax.ppermute(block, axis, [((i - distance) % n, i) for i in range(n)])  10.9 us
    ppermute x14, waiting for transfers between devices, crossed(): return lax.ppermute(v, AXES, [(i, i ^ mask) for i in range(n)])  2.18 us
    transpose x3, local copies, waits for them, and re-layouts, columns(): x[:, :, lo:lo + RIM].transpose(1, 2, 0, 3)  1.75 us
  transfers between devices with their start and end apart: 18, of which 4 were waited for; matrix products, arithmetic and copies ran while one was open for 0% of the time, Pallas kernels for 46%

profile of v4, /device:TPU:0, one launch (start us, length us, event | category | flops | bytes accessed | tf_op | source)
XLA Modules:
  0.0 78.3 jit_solution(3651105120758477409)
XLA Ops:
  0.6 1.5 %slice_bitcast_fusion = (bf16[16,3,8,256]{3,1,0,2:T(4,128)(2,1)S(1)}, bf16[16,3,8,256]{3,1,0,2:T(4,128)(2,1)S(1)}) fusion(bf16[8,16,16,256]{3,2,1,0:T(8,128)(2,1)} %bitcast.25), kind=kLoop, calls=%fused_computation | loop fusion | bytes 786432 | tf_op jit(solution)/shard_map/transpose | solution.py:549
  2.1 0.1 copy.27
  2.3 3.0 %collective-permute-start = (bf16[384,256]{1,0:T(8,128)(2,1)S(1)}, bf16[384,256]{1,0:T(8,128)(2,1)S(1)}, u32[]{:S(2)}, u32[]{:S(2)}) collective-permute-start(bf16[384,256]{1,0:T(8,128)(2,1)S(1)} %bitcast.28), channel_id=1, source_target_pairs={{28,0},{0,4},{4,8},{8,12},{12,16},{16,20},{20,24},{24,28},{29,1},{... | collective-permute-start | bytes 589832 | tf_op jit(solution)/shard_map/ppermute | solution.py:511
  5.3 0.1 copy.28
  5.4 3.1 %collective-permute-start.1 = (bf16[384,256]{1,0:T(8,128)(2,1)S(1)}, bf16[384,256]{1,0:T(8,128)(2,1)S(1)}, u32[]{:S(2)}, u32[]{:S(2)}) collective-permute-start(bf16[384,256]{1,0:T(8,128)(2,1)S(1)} %bitcast.29), channel_id=1, source_target_pairs={{4,0},{8,4},{12,8},{16,12},{20,16},{24,20},{28,24},{0,28},{5,1},{9... | collective-permute-start | bytes 589832 | tf_op jit(solution)/shard_map/ppermute | solution.py:511
  9.2 8.6 %shard_map.212 = (f32[2,22,128,128]{3,2,1,0:T(8,128)S(1)}, f32[2,16,128,128]{3,2,1,0:T(8,128)S(1)}, f32[2,16,128,128]{3,2,1,0:T(8,128)S(1)}, f32[2,49,8,128]{3,2...) custom-call(s32[8,8]{1,0:T(8,128)} %refs_0_.9, ...), custom_call_target="tpu_custom_call" | custom-call | tf_op jit(solution)/shard_map/pallas_call | solution.py:45
  17.8 7.5 %shard_map.213 = (f32[2,22,24,128]{3,2,1,0:T(8,128)S(1)}, f32[2,22,24,128]{3,2,1,0:T(8,128)S(1)}, f32[2,16,128,128]{3,2,1,0:T(8,128)S(1)}, f32[2,22,128,128]{3,2...) custom-call(s32[8,8]{1,0:T(8,128)} %refs_0_.9, ...), custom_call_target="tpu_custom_call" | custom-call | tf_op jit(solution)/shard_map/pallas_call | solution.py:45
  25.4 4.7 %collective-permute-start.3 = (bf16[384,256]{1,0:T(8,128)(2,1)S(1)}, bf16[384,256]{1,0:T(8,128)(2,1)S(1)}, u32[]{:S(2)}, u32[]{:S(2)}) collective-permute-start(bf16[384,256]{1,0:T(8,128)(2,1)S(1)} %get-tuple-element.87), channel_id=1, source_target_pairs={{4,0},{8,4},{12,8},{16,12},{20,16},{24,20},{28,24},{0,28},{5,1},{9... | collective-permute-start | bytes 589832 | tf_op jit(solution)/shard_map/ppermute | solution.py:511
  30.1 6.8 %shard_map.214 = (f32[2,16,128,128]{3,2,1,0:T(8,128)S(1)}, f32[2,22,128,128]{3,2,1,0:T(8,128)S(1)}, bf16[2048,128]{1,0:T(8,128)(2,1)S(1)}, bf16[2048,128]{1,0:T(8,128)(2,1)S(1)}, f32[9,8,256]{2,1,0:T(8,128)S(1)}) custom-call(s32[1]{0:T(128)} %bitcast.refs_2_.refs_0_, ...), custom_call_target="tpu_custom_call", output_to_operand_aliasing={{0}: (6, {}), {1}: (7, {})} | custom-call | tf_op jit(solution)/shard_map/pallas_call | solution.py:45
  37.0 0.9 %shard_map.215 = (f32[2,22,24,128]{3,2,1,0:T(8,128)S(1)}, f32[2,22,24,128]{3,2,1,0:T(8,128)S(1)}, f32[2,22,128,128]{3,2,1,0:T(8,128)S(1)}, f32[8,128]{1,0:T(8,128)S(1)}) custom-call(s32[8,8]{1,0:T(8,128)} %refs_0_.9, bf16[384,256]{1,0:T(8,128)(2,1)S(1)} %collective-permute-done.2.refs_1_, ...), custom_call_target="tpu_custom_call", output_to_operand_aliasing={{2}: (3, {})} | custom-call | flops 8000000000 | bytes 31250000 | tf_op jit(solution)/shard_map/pallas_call | solution.py:45
  38.0 1.0 %collective-permute-done.4.refs_2_ = bf16[2048,128]{1,0:T(8,128)(2,1)S(1)} collective-permute-done((bf16[2048,128]{1,0:T(8,128)(2,1)S(1)}, bf16[2048,128]{1,0:T(8,128)(2,1)S(1)}, u32[]{:S(2)}, u32[]{:S(2)}) %collective-permute-start.4) | collective-permute-done | bytes 524320 | tf_op jit(solution)/shard_map/ppermute | solution.py:516
  38.9 0.3 shard_map.216
  39.2 1.7 %collective-permute-start.5 = (bf16[512,128]{1,0:T(8,128)(2,1)S(1)}, bf16[512,128]{1,0:T(8,128)(2,1)S(1)}, u32[]{:S(2)}, u32[]{:S(2)}) collective-permute-start(bf16[512,128]{1,0:T(8,128)(2,1)S(1)} %get-tuple-element.98), channel_id=1, source_target_pairs={{0,2},{1,3},{2,0},{3,1},{4,6},{5,7},{6,4},{7,5},{8,10},{9,11},{10,... | collective-permute-start | bytes 393224 | tf_op jit(solution)/shard_map/ppermute | solution.py:516
  41.0 1.8 %collective-permute-start.7 = (bf16[512,128]{1,0:T(8,128)(2,1)S(1)}, bf16[512,128]{1,0:T(8,128)(2,1)S(1)}, u32[]{:S(2)}, u32[]{:S(2)}) collective-permute-start(bf16[512,128]{1,0:T(8,128)(2,1)S(1)} %get-tuple-element.100), channel_id=1, source_target_pairs={{0,6},{1,7},{2,4},{3,5},{4,2},{5,3},{6,0},{7,1},{8,14},{9,15},{10,... | collective-permute-start | bytes 393224 | tf_op jit(solution)/shard_map/ppermute | solution.py:516
  42.8 3.7 %shard_map.218 = (f32[49,8,128]{2,1,0:T(8,128)S(1)}, f32[8,128]{1,0:T(8,128)S(1)}) custom-call(f32[2,22,128,128]{3,2,1,0:T(8,128)S(1)} %get-tuple-element.72.refs_3_.refs_1_.refs_0_, f32[2,22,24,128]{3,2,1,0:T(8,128)S(1)} %get-tuple-element.84.refs_1_, f32[2,22,24,128]{3,2,1,0:T(8,128)S(1)} %get-tuple-element.85.refs_2_, ...), custom_call_target="tpu_custom_call" | custom-call | flops 8000000000 | bytes 31250000 | tf_op jit(solution)/shard_map/pallas_call | solution.py:45
  46.5 3.7 %shard_map.217 = (f32[49,8,128]{2,1,0:T(8,128)S(1)}, f32[8,128]{1,0:T(8,128)S(1)}) custom-call(f32[2,22,128,128]{3,2,1,0:T(8,128)S(1)} %get-tuple-element.72.refs_3_.refs_1_.refs_0_, f32[2,22,24,128]{3,2,1,0:T(8,128)S(1)} %get-tuple-element.84.refs_1_, f32[2,22,24,128]{3,2,1,0:T(8,128)S(1)} %get-tuple-element.85.refs_2_, ...), custom_call_target="tpu_custom_call" | custom-call | flops 8000000000 | bytes 31250000 | tf_op jit(solution)/shard_map/pallas_call | solution.py:45
  50.3 0.2 shard_map.219
  50.5 1.2 %collective-permute-start.9 = (bf16[128,128]{1,0:T(8,128)(2,1)S(1)}, bf16[128,128]{1,0:T(8,128)(2,1)S(1)}, u32[]{:S(2)}, u32[]{:S(2)}) collective-permute-start(bf16[128,128]{1,0:T(8,128)(2,1)S(1)} %get-tuple-element.105), channel_id=1, source_target_pairs={{0,16},{1,17},{2,18},{3,19},{4,20},{5,21},{6,22},{7,23},{8,24},{9,... | collective-permute-start | bytes 98312 | tf_op jit(solution)/shard_map/ppermute | solution.py:516
  51.7 3.2 %collective-permute-start.10 = (bf16[128,128]{1,0:T(8,128)(2,1)S(1)}, bf16[128,128]{1,0:T(8,128)(2,1)S(1)}, u32[]{:S(2)}, u32[]{:S(2)}) collective-permute-start(bf16[128,128]{1,0:T(8,128)(2,1)S(1)} %get-tuple-element.106), channel_id=1, source_target_pairs={{0,24},{1,25},{2,26},{3,27},{4,28},{5,29},{6,30},{7,31},{8,16},{9,... | collective-permute-start | bytes 98312 | tf_op jit(solution)/shard_map/ppermute | solution.py:516
  54.9 3.5 %shard_map.220 = (bf16[8,6,16,256]{3,2,1,0:T(8,128)(2,1)S(1)}, f32[8,128]{1,0:T(8,128)S(1)}) custom-call(s32[1]{0:T(128)S(6)} %copy.32.refs_1_.refs_0_, f32[2,22,24,128]{3,2,1,0:T(8,128)S(1)} %get-tuple-element.107.refs_1_, f32[2,22,24,128]{3,2,1,0:T(8,128)S(1)} %get-tuple-element.108.refs_2_, f32[2,22,128,128]{3,2,1,0:T(8,128)S(1)} %get-tuple-element.89.refs_3_, ...), custom_call_target="tpu_custom_call" | custom-call | tf_op jit(solution)/shard_map/pallas_call | solution.py:45
  58.6 2.3 %collective-permute-start.13 = (bf16[256,128]{1,0:T(8,128)(2,1)S(1)}, bf16[256,128]{1,0:T(8,128)(2,1)S(1)}, u32[]{:S(2)}, u32[]{:S(2)}) collective-permute-start(bf16[256,128]{1,0:T(8,128)(2,1)S(1)} %get-tuple-element.111.refs_1_), channel_id=1, source_target_pairs={{0,24},{1,25},{2,26},{3,27},{4,28},{5,29},{6,30},{7,31},{8,16},{9,... | collective-permute-start | bytes 196616 | tf_op jit(solution)/shard_map/ppermute | solution.py:516
  60.9 2.1 %collective-permute-start.11 = (bf16[256,128]{1,0:T(8,128)(2,1)S(1)}, bf16[256,128]{1,0:T(8,128)(2,1)S(1)}, u32[]{:S(2)}, u32[]{:S(2)}) collective-permute-start(bf16[256,128]{1,0:T(8,128)(2,1)S(1)} %get-tuple-element.111.refs_1_), channel_id=1, source_target_pairs={{0,8},{1,9},{2,10},{3,11},{4,12},{5,13},{6,14},{7,15},{8,0},{9,1},... | collective-permute-start | bytes 196616 | tf_op jit(solution)/shard_map/ppermute | solution.py:516
  63.0 2.7 %shard_map.222 = (bf16[8,10,16,256]{3,2,1,0:T(8,128)(2,1)S(1)}, f32[8,128]{1,0:T(8,128)S(1)}) custom-call(s32[1]{0:T(128)S(6)} %copy.32.refs_1_.refs_0_, f32[2,22,24,128]{3,2,1,0:T(8,128)S(1)} %get-tuple-element.107.refs_1_, f32[2,22,24,128]{3,2,1,0:T(8,128)S(1)} %get-tuple-element.108.refs_2_, f32[2,22,128,128]{3,2,1,0:T(8,128)S(1)} %get-tuple-element.89.refs_3_, ...), custom_call_target="tpu_custom_call" | custom-call | tf_op jit(solution)/shard_map/pallas_call | solution.py:45
  65.7 0.4 collective-permute-done.12.refs_3_
  66.2 1.1 %collective-permute-start.16 = (bf16[640,128]{1,0:T(8,128)(2,1)S(1)}, bf16[640,128]{1,0:T(8,128)(2,1)S(1)}, u32[]{:S(2)}, u32[]{:S(2)}) collective-permute-start(bf16[640,128]{1,0:T(8,128)(2,1)S(1)} %get-tuple-element.115.refs_1_), channel_id=1, source_target_pairs={{0,6},{1,7},{2,4},{3,5},{4,2},{5,3},{6,0},{7,1},{8,14},{9,15},{10,... | collective-permute-start | bytes 491528 | tf_op jit(solution)/shard_map/ppermute | solution.py:516
  67.3 2.0 %collective-permute-start.15 = (bf16[640,128]{1,0:T(8,128)(2,1)S(1)}, bf16[640,128]{1,0:T(8,128)(2,1)S(1)}, u32[]{:S(2)}, u32[]{:S(2)}) collective-permute-start(bf16[640,128]{1,0:T(8,128)(2,1)S(1)} %get-tuple-element.115.refs_1_), channel_id=1, source_target_pairs={{0,4},{1,5},{2,6},{3,7},{4,0},{5,1},{6,2},{7,3},{8,12},{9,13},{10,... | collective-permute-start | bytes 491528 | tf_op jit(solution)/shard_map/ppermute | solution.py:516
  69.3 0.4 collective-permute-start.14
  69.7 4.5 %shard_map.224 = (bf16[8,16,16,256]{3,2,1,0:T(8,128)(2,1)}, f32[8,128]{1,0:T(8,128)S(1)}) custom-call(s32[1]{0:T(128)S(6)} %copy.32.refs_1_.refs_0_, f32[2,22,24,128]{3,2,1,0:T(8,128)S(1)} %get-tuple-element.107.refs_1_, f32[2,22,24,128]{3,2,1,0:T(8,128)S(1)} %get-tuple-element.108.refs_2_, f32[2,22,128,128]{3,2,1,0:T(8,128)S(1)} %get-tuple-element.89.refs_3_, ...), custom_call_target="tpu_custom_call" | custom-call | tf_op jit(solution)/shard_map/pallas_call | solution.py:45
  74.3 0.4 collective-permute-done.14.refs_2_
  74.8 1.5 %shard_map.226 = (bf16[8,16,16,256]{3,2,1,0:T(8,128)(2,1)}, f32[8,128]{1,0:T(8,128)S(1)}) custom-call(s32[1]{0:T(128)S(6)} %copy.32.refs_1_.refs_0_, f32[2,16,128,128]{3,2,1,0:T(8,128)S(1)} %get-tuple-element.83.refs_1_, f32[8,128]{1,0:T(8,128)S(1)} %get-tuple-element.119.refs_2_), custom_call_target="tpu_custom_call" | custom-call | tf_op jit(solution)/shard_map/pallas_call | solution.py:45
  76.3 0.4 collective-permute-done.17.refs_2_
  76.7 1.5 %shard_map.227 = (f32[7,7,256]{2,1,0:T(8,128)}, f32[1,256]{1,0:T(1,128)}, f32[1,256]{1,0:T(1,128)}, f32[1,256]{1,0:T(1,128)}, f32[256,1024]{1,0:T(8,128)}, /*ind...) custom-call(s32[1]{0:T(128)} %bitcast.refs_2_.refs_0_, ...), custom_call_target="tpu_custom_call" | custom-call | tf_op jit(solution)/shard_map/pallas_call | solution.py:45
  (23 shorter events, 0.5 us)
Async XLA Ops:
  2.3 15.6 %collective-permute-start = (bf16[384,256]{1,0:T(8,128)(2,1)S(1)}, bf16[384,256]{1,0:T(8,128)(2,1)S(1)}, u32[]{:S(2)}, u32[]{:S(2)}) collective-permute-start(bf16[384,256]{1,0:T(8,128)(2,1)S(1)} %bitcast.28), channel_id=1, source_target_pairs={{28,0},{0,4},{4,8},{8,12},{12,16},{16,20},{20,24},{24,28},{29,1},{... | collective-permute-start | bytes 589832 | tf_op jit(solution)/shard_map/ppermute | solution.py:511
  5.4 12.4 %collective-permute-start.1 = (bf16[384,256]{1,0:T(8,128)(2,1)S(1)}, bf16[384,256]{1,0:T(8,128)(2,1)S(1)}, u32[]{:S(2)}, u32[]{:S(2)}) collective-permute-start(bf16[384,256]{1,0:T(8,128)(2,1)S(1)} %bitcast.29), channel_id=1, source_target_pairs={{4,0},{8,4},{12,8},{16,12},{20,16},{24,20},{28,24},{0,28},{5,1},{9... | collective-permute-start | bytes 589832 | tf_op jit(solution)/shard_map/ppermute | solution.py:511
  25.3 11.7 %collective-permute-start.2 = (bf16[384,256]{1,0:T(8,128)(2,1)S(1)}, bf16[384,256]{1,0:T(8,128)(2,1)S(1)}, u32[]{:S(2)}, u32[]{:S(2)}) collective-permute-start(bf16[384,256]{1,0:T(8,128)(2,1)S(1)} %get-tuple-element.86), channel_id=1, source_target_pairs={{28,0},{0,4},{4,8},{8,12},{12,16},{16,20},{20,24},{24,28},{29,1},{... | collective-permute-start | bytes 589832 | tf_op jit(solution)/shard_map/ppermute | solution.py:511
  25.4 11.6 %collective-permute-start.3 = (bf16[384,256]{1,0:T(8,128)(2,1)S(1)}, bf16[384,256]{1,0:T(8,128)(2,1)S(1)}, u32[]{:S(2)}, u32[]{:S(2)}) collective-permute-start(bf16[384,256]{1,0:T(8,128)(2,1)S(1)} %get-tuple-element.87), channel_id=1, source_target_pairs={{4,0},{8,4},{12,8},{16,12},{20,16},{24,20},{28,24},{0,28},{5,1},{9... | collective-permute-start | bytes 589832 | tf_op jit(solution)/shard_map/ppermute | solution.py:511
  36.9 2.0 %collective-permute-start.4 = (bf16[2048,128]{1,0:T(8,128)(2,1)S(1)}, bf16[2048,128]{1,0:T(8,128)(2,1)S(1)}, u32[]{:S(2)}, u32[]{:S(2)}) collective-permute-start(bf16[2048,128]{1,0:T(8,128)(2,1)S(1)} %get-tuple-element.91), channel_id=1, source_target_pairs={{0,1},{1,0},{2,3},{3,2},{4,5},{5,4},{6,7},{7,6},{8,9},{9,8},{10,11... | collective-permute-start | bytes 1572872 | tf_op jit(solution)/shard_map/ppermute | solution.py:516
  39.2 11.0 %collective-permute-start.5 = (bf16[512,128]{1,0:T(8,128)(2,1)S(1)}, bf16[512,128]{1,0:T(8,128)(2,1)S(1)}, u32[]{:S(2)}, u32[]{:S(2)}) collective-permute-start(bf16[512,128]{1,0:T(8,128)(2,1)S(1)} %get-tuple-element.98), channel_id=1, source_target_pairs={{0,2},{1,3},{2,0},{3,1},{4,6},{5,7},{6,4},{7,5},{8,10},{9,11},{10,... | collective-permute-start | bytes 393224 | tf_op jit(solution)/shard_map/ppermute | solution.py:516
  41.0 9.3 %collective-permute-start.6 = (bf16[512,128]{1,0:T(8,128)(2,1)S(1)}, bf16[512,128]{1,0:T(8,128)(2,1)S(1)}, u32[]{:S(2)}, u32[]{:S(2)}) collective-permute-start(bf16[512,128]{1,0:T(8,128)(2,1)S(1)} %get-tuple-element.99), channel_id=1, source_target_pairs={{0,4},{1,5},{2,6},{3,7},{4,0},{5,1},{6,2},{7,3},{8,12},{9,13},{10,... | collective-permute-start | bytes 393224 | tf_op jit(solution)/shard_map/ppermute | solution.py:516
  41.0 9.3 %collective-permute-start.7 = (bf16[512,128]{1,0:T(8,128)(2,1)S(1)}, bf16[512,128]{1,0:T(8,128)(2,1)S(1)}, u32[]{:S(2)}, u32[]{:S(2)}) collective-permute-start(bf16[512,128]{1,0:T(8,128)(2,1)S(1)} %get-tuple-element.100), channel_id=1, source_target_pairs={{0,6},{1,7},{2,4},{3,5},{4,2},{5,3},{6,0},{7,1},{8,14},{9,15},{10,... | collective-permute-start | bytes 393224 | tf_op jit(solution)/shard_map/ppermute | solution.py:516
  50.4 8.0 %collective-permute-start.8 = (bf16[128,128]{1,0:T(8,128)(2,1)S(1)}, bf16[128,128]{1,0:T(8,128)(2,1)S(1)}, u32[]{:S(2)}, u32[]{:S(2)}) collective-permute-start(bf16[128,128]{1,0:T(8,128)(2,1)S(1)} %get-tuple-element.104), channel_id=1, source_target_pairs={{0,8},{1,9},{2,10},{3,11},{4,12},{5,13},{6,14},{7,15},{8,0},{9,1},... | collective-permute-start | bytes 98312 | tf_op jit(solution)/shard_map/ppermute | solution.py:516
  50.5 7.9 %collective-permute-start.9 = (bf16[128,128]{1,0:T(8,128)(2,1)S(1)}, bf16[128,128]{1,0:T(8,128)(2,1)S(1)}, u32[]{:S(2)}, u32[]{:S(2)}) collective-permute-start(bf16[128,128]{1,0:T(8,128)(2,1)S(1)} %get-tuple-element.105), channel_id=1, source_target_pairs={{0,16},{1,17},{2,18},{3,19},{4,20},{5,21},{6,22},{7,23},{8,24},{9,... | collective-permute-start | bytes 98312 | tf_op jit(solution)/shard_map/ppermute | solution.py:516
  51.7 6.8 %collective-permute-start.10 = (bf16[128,128]{1,0:T(8,128)(2,1)S(1)}, bf16[128,128]{1,0:T(8,128)(2,1)S(1)}, u32[]{:S(2)}, u32[]{:S(2)}) collective-permute-start(bf16[128,128]{1,0:T(8,128)(2,1)S(1)} %get-tuple-element.106), channel_id=1, source_target_pairs={{0,24},{1,25},{2,26},{3,27},{4,28},{5,29},{6,30},{7,31},{8,16},{9,... | collective-permute-start | bytes 98312 | tf_op jit(solution)/shard_map/ppermute | solution.py:516
  58.6 7.1 %collective-permute-start.13 = (bf16[256,128]{1,0:T(8,128)(2,1)S(1)}, bf16[256,128]{1,0:T(8,128)(2,1)S(1)}, u32[]{:S(2)}, u32[]{:S(2)}) collective-permute-start(bf16[256,128]{1,0:T(8,128)(2,1)S(1)} %get-tuple-element.111.refs_1_), channel_id=1, source_target_pairs={{0,24},{1,25},{2,26},{3,27},{4,28},{5,29},{6,30},{7,31},{8,16},{9,... | collective-permute-start | bytes 196616 | tf_op jit(solution)/shard_map/ppermute | solution.py:516
  60.9 5.2 %collective-permute-start.12 = (bf16[256,128]{1,0:T(8,128)(2,1)S(1)}, bf16[256,128]{1,0:T(8,128)(2,1)S(1)}, u32[]{:S(2)}, u32[]{:S(2)}) collective-permute-start(bf16[256,128]{1,0:T(8,128)(2,1)S(1)} %get-tuple-element.111.refs_1_), channel_id=1, source_target_pairs={{0,16},{1,17},{2,18},{3,19},{4,20},{5,21},{6,22},{7,23},{8,24},{9,... | collective-permute-start | bytes 196616 | tf_op jit(solution)/shard_map/ppermute | solution.py:516
  60.9 5.2 %collective-permute-start.11 = (bf16[256,128]{1,0:T(8,128)(2,1)S(1)}, bf16[256,128]{1,0:T(8,128)(2,1)S(1)}, u32[]{:S(2)}, u32[]{:S(2)}) collective-permute-start(bf16[256,128]{1,0:T(8,128)(2,1)S(1)} %get-tuple-element.111.refs_1_), channel_id=1, source_target_pairs={{0,8},{1,9},{2,10},{3,11},{4,12},{5,13},{6,14},{7,15},{8,0},{9,1},... | collective-permute-start | bytes 196616 | tf_op jit(solution)/shard_map/ppermute | solution.py:516
  66.2 8.1 %collective-permute-start.16 = (bf16[640,128]{1,0:T(8,128)(2,1)S(1)}, bf16[640,128]{1,0:T(8,128)(2,1)S(1)}, u32[]{:S(2)}, u32[]{:S(2)}) collective-permute-start(bf16[640,128]{1,0:T(8,128)(2,1)S(1)} %get-tuple-element.115.refs_1_), channel_id=1, source_target_pairs={{0,6},{1,7},{2,4},{3,5},{4,2},{5,3},{6,0},{7,1},{8,14},{9,15},{10,... | collective-permute-start | bytes 491528 | tf_op jit(solution)/shard_map/ppermute | solution.py:516
  67.3 7.0 %collective-permute-start.15 = (bf16[640,128]{1,0:T(8,128)(2,1)S(1)}, bf16[640,128]{1,0:T(8,128)(2,1)S(1)}, u32[]{:S(2)}, u32[]{:S(2)}) collective-permute-start(bf16[640,128]{1,0:T(8,128)(2,1)S(1)} %get-tuple-element.115.refs_1_), channel_id=1, source_target_pairs={{0,4},{1,5},{2,6},{3,7},{4,0},{5,1},{6,2},{7,3},{8,12},{9,13},{10,... | collective-permute-start | bytes 491528 | tf_op jit(solution)/shard_map/ppermute | solution.py:516
  69.3 5.3 %collective-permute-start.14 = (bf16[640,128]{1,0:T(8,128)(2,1)S(1)}, bf16[640,128]{1,0:T(8,128)(2,1)S(1)}, u32[]{:S(2)}, u32[]{:S(2)}) collective-permute-start(bf16[640,128]{1,0:T(8,128)(2,1)S(1)} %get-tuple-element.115.refs_1_), channel_id=1, source_target_pairs={{0,2},{1,3},{2,0},{3,1},{4,6},{5,7},{6,4},{7,5},{8,10},{9,11},{10,... | collective-permute-start | bytes 491528 | tf_op jit(solution)/shard_map/ppermute | solution.py:516
  74.7 2.0 %collective-permute-start.17 = (bf16[2176,128]{1,0:T(8,128)(2,1)S(1)}, bf16[2176,128]{1,0:T(8,128)(2,1)S(1)}, u32[]{:S(2)}, u32[]{:S(2)}) collective-permute-start(bf16[2176,128]{1,0:T(8,128)(2,1)S(1)} %get-tuple-element.122.refs_1_), channel_id=1, source_target_pairs={{0,1},{1,0},{2,3},{3,2},{4,5},{5,4},{6,7},{7,6},{8,9},{9,8},{10,11... | collective-permute-start | bytes 1671176 | tf_op jit(solution)/shard_map/ppermute | solution.py:516

commit v5 on v4

--- a/solution.py
+++ b/solution.py
@@ -372,13 +372,13 @@
     lax.fori_loop(0, 16, row, 0)
 
 
-def tap_kernel(h, center_ref, west_ref, east_ref, g_ref, acc_ref):
+def tap_kernel(h, first, center_ref, west_ref, east_ref, g_ref, acc_ref):
     pads = (west_ref, center_ref, east_ref)
 
     def row_tap(i, carry):
         def row(r, accs):
             g = [g_ref[h, 3 + r, c * 8 : c * 8 + 8, :] for c in range(16)]
-            xs = [pad_col(pads, h, r + i, c) for c in range(22)]
+            xs = [pad_col(pads, h, r + first + i, c) for c in range(22)]
             new = []
             for j in range(TAPS):
                 terms = [xs[c + j] * g[c] for c in range(16)]
@@ -392,7 +392,7 @@
             acc_ref[i * TAPS + j] = accs[j]
         return carry
 
-    lax.fori_loop(0, TAPS, row_tap, 0)
+    lax.fori_loop(0, acc_ref.shape[0] // TAPS, row_tap, 0)
 
 
 def sides_kernel(nbr_ref, hw_ref, he_ref, g_in, west_ref, east_ref, g_ref):
@@ -442,7 +442,7 @@
                 outs[k][...] = piece
 
 
-def finish_kernel(tap0, tap1, sums, *refs):
+def finish_kernel(tap0, tap1, tap2, sums, *refs):
     held, out = refs[:-1], refs[-1]
     ns = sums.shape[0]
     total = added(held)
@@ -450,8 +450,8 @@
     out[0:rows, :] = total
     dense = jnp.sum(sums[...], axis=1)
     rest = jnp.zeros((64 - ns - 49, LANES), F32)
-    for h, tap in enumerate((tap0, tap1)):
-        part = jnp.concatenate([dense[:, lanes(h)], jnp.sum(tap[...], axis=1), rest], axis=0)
+    for h, parts in enumerate(((tap0, tap1), (tap2,))):
+        part = jnp.concatenate([dense[:, lanes(h)], *(jnp.sum(p[...], axis=1) for p in parts), rest], axis=0)
         out[rows + 64 * h : rows + 64 * h + 64, :] = part.astype(BF16)
 
 
@@ -590,21 +590,22 @@
     later = groups()[1:]
     arrived = [crossed(sent, 1)]
 
-    *sides, g, done = call(
-        sides_kernel, [(side, F32, KEEP), (side, F32, KEEP), (tall, F32, KEEP)],
-        (neighbours, grad_from_west, grad_from_east, g), smem=1, alias={3: 2}, token=True, work=WORK,
-    )
-    filler = (done,)
     taps = []
 
-    def tap(h):
+    def tap(h, first, last, after):
         v, done = call(
-            functools.partial(tap_kernel, h), [((TAPS * TAPS, 8, LANES), F32, KEEP)], (center, west, east, g),
-            after=(begun,), token=True, work=WORK,
+            functools.partial(tap_kernel, h, first), [(((last - first) * TAPS, 8, LANES), F32, KEEP)],
+            (center, west, east, g), after=after, token=True, work=WORK,
         )
         taps.append(v)
         return done
 
+
+    *sides, g, done = call(
+        sides_kernel, [(side, F32, KEEP), (side, F32, KEEP), (tall, F32, KEEP)],
+        (neighbours, grad_from_west, grad_from_east, g), smem=1, alias={3: 2}, after=(tap(0, 0, 3, ()),), token=True, work=WORK,
+    )
+    filler = (done,)
 
     gx = ()
     cuts = [0, 6, 10, edge]
@@ -636,7 +637,7 @@
         arrived = [crossed(p, k * bit) for k, p in enumerate(parts, 1)]
         filler = ()
         if n == 0:
-            filler = (tap(0), tap(1))
+            filler = (tap(0, 3, TAPS, (begun,)), tap(1, 0, TAPS, (begun,)))
         if n == 1:
             filler = (back(),)
     held, begun = call(

time: 78.7 us -> 78.1 us (level)
    pallas_call x16 -> x17, Pallas kernels: 45.7 us -> 45.9 us  [call(): pl.pallas_call(kernel, out_shape=tuple((pltpu.VMEM(o[0], o[1]) if len(o)...]
  transfers between devices with their start and end apart: 18 -> 18, of which waited for: 4 -> 3; matrix products, arithmetic and copies ran while one was open for 0% -> 0% of each run, Pallas kernels for 46% -> 46%
where the time goes in v5:
time: 78.1 us; the launch traced here: 77.7 us
  Pallas kernels  45.9 us (59%)
  starting transfers between devices  27 us (35%)
  local copies, waits for them, and re-layouts  1.75 us (2%)
  between operations  1.54 us (2%)
  waiting for transfers between devices  1.49 us (2%)
    pallas_call x17, Pallas kernels, call(): pl.pallas_call(kernel, out_shape=tuple((pltpu.VMEM(o[0], o[1]) if len(o)...  45.9 us
    ppermute x14, starting transfers between devices, crossed(): return lax.ppermute(v, AXES, [(i, i ^ mask) for i in range(n)])  16.1 us
    ppermute x4, starting transfers between devices, shifted(): lax.ppermute(block, axis, [((i - distance) % n, i) for i in range(n)])  10.9 us
    transpose x3, local copies, waits for them, and re-layouts, columns(): x[:, :, lo:lo + RIM].transpose(1, 2, 0, 3)  1.75 us
  transfers between devices with their start and end apart: 18, of which 3 were waited for; matrix products, arithmetic and copies ran while one was open for 0% of the time, Pallas kernels for 46%

profile of v5, /device:TPU:0, one launch (start us, length us, event | category | flops | bytes accessed | tf_op | source)
XLA Modules:
  0.0 77.7 jit_solution(6313855506600822367)
XLA Ops:
  0.6 1.5 %slice_bitcast_fusion = (bf16[16,3,8,256]{3,1,0,2:T(4,128)(2,1)S(1)}, bf16[16,3,8,256]{3,1,0,2:T(4,128)(2,1)S(1)}) fusion(bf16[8,16,16,256]{3,2,1,0:T(8,128)(2,1)} %bitcast.25), kind=kLoop, calls=%fused_computation | loop fusion | bytes 786432 | tf_op jit(solution)/shard_map/transpose | solution.py:549
  2.1 0.1 copy.27
  2.3 3.0 %collective-permute-start = (bf16[384,256]{1,0:T(8,128)(2,1)S(1)}, bf16[384,256]{1,0:T(8,128)(2,1)S(1)}, u32[]{:S(2)}, u32[]{:S(2)}) collective-permute-start(bf16[384,256]{1,0:T(8,128)(2,1)S(1)} %bitcast.28), channel_id=1, source_target_pairs={{28,0},{0,4},{4,8},{8,12},{12,16},{16,20},{20,24},{24,28},{29,1},{... | collective-permute-start | bytes 589832 | tf_op jit(solution)/shard_map/ppermute | solution.py:511
  5.3 0.1 copy.28
  5.4 3.1 %collective-permute-start.1 = (bf16[384,256]{1,0:T(8,128)(2,1)S(1)}, bf16[384,256]{1,0:T(8,128)(2,1)S(1)}, u32[]{:S(2)}, u32[]{:S(2)}) collective-permute-start(bf16[384,256]{1,0:T(8,128)(2,1)S(1)} %bitcast.29), channel_id=1, source_target_pairs={{4,0},{8,4},{12,8},{16,12},{20,16},{24,20},{28,24},{0,28},{5,1},{9... | collective-permute-start | bytes 589832 | tf_op jit(solution)/shard_map/ppermute | solution.py:511
  9.2 8.6 %shard_map.212 = (f32[2,22,128,128]{3,2,1,0:T(8,128)S(1)}, f32[2,16,128,128]{3,2,1,0:T(8,128)S(1)}, f32[2,16,128,128]{3,2,1,0:T(8,128)S(1)}, f32[2,49,8,128]{3,2...) custom-call(s32[8,8]{1,0:T(8,128)} %refs_0_.9, ...), custom_call_target="tpu_custom_call" | custom-call | tf_op jit(solution)/shard_map/pallas_call | solution.py:45
  17.8 7.5 %shard_map.213 = (f32[2,22,24,128]{3,2,1,0:T(8,128)S(1)}, f32[2,22,24,128]{3,2,1,0:T(8,128)S(1)}, f32[2,16,128,128]{3,2,1,0:T(8,128)S(1)}, f32[2,22,128,128]{3,2...) custom-call(s32[8,8]{1,0:T(8,128)} %refs_0_.9, ...), custom_call_target="tpu_custom_call" | custom-call | tf_op jit(solution)/shard_map/pallas_call | solution.py:45
  25.4 4.7 %collective-permute-start.3 = (bf16[384,256]{1,0:T(8,128)(2,1)S(1)}, bf16[384,256]{1,0:T(8,128)(2,1)S(1)}, u32[]{:S(2)}, u32[]{:S(2)}) collective-permute-start(bf16[384,256]{1,0:T(8,128)(2,1)S(1)} %get-tuple-element.91), channel_id=1, source_target_pairs={{4,0},{8,4},{12,8},{16,12},{20,16},{24,20},{28,24},{0,28},{5,1},{9... | collective-permute-start | bytes 589832 | tf_op jit(solution)/shard_map/ppermute | solution.py:511
  30.1 6.8 %shard_map.214 = (f32[2,16,128,128]{3,2,1,0:T(8,128)S(1)}, f32[2,22,128,128]{3,2,1,0:T(8,128)S(1)}, bf16[2048,128]{1,0:T(8,128)(2,1)S(1)}, bf16[2048,128]{1,0:T(8,128)(2,1)S(1)}, f32[9,8,256]{2,1,0:T(8,128)S(1)}) custom-call(s32[1]{0:T(128)} %bitcast.refs_2_.refs_0_, ...), custom_call_target="tpu_custom_call", output_to_operand_aliasing={{0}: (6, {}), {1}: (7, {})} | custom-call | tf_op jit(solution)/shard_map/pallas_call | solution.py:45
  37.0 1.6 %shard_map.215 = (f32[21,8,128]{2,1,0:T(8,128)S(1)}, f32[8,128]{1,0:T(8,128)S(1)}) custom-call(f32[2,22,128,128]{3,2,1,0:T(8,128)S(1)} %get-tuple-element.74.refs_3_.refs_1_.refs_0_, f32[2,22,24,128]{3,2,1,0:T(8,128)S(1)} %get-tuple-element.86.refs_1_, f32[2,22,24,128]{3,2,1,0:T(8,128)S(1)} %get-tuple-element.87.refs_2_, ...), custom_call_target="tpu_custom_call" | custom-call | flops 8000000000 | bytes 31250000 | tf_op jit(solution)/shard_map/pallas_call | solution.py:45
  38.7 0.9 %shard_map.216 = (f32[2,22,24,128]{3,2,1,0:T(8,128)S(1)}, f32[2,22,24,128]{3,2,1,0:T(8,128)S(1)}, f32[2,22,128,128]{3,2,1,0:T(8,128)S(1)}, f32[8,128]{1,0:T(8,128)S(1)}) custom-call(s32[8,8]{1,0:T(8,128)} %refs_0_.9, bf16[384,256]{1,0:T(8,128)(2,1)S(1)} %collective-permute-done.2.refs_1_, ...), custom_call_target="tpu_custom_call", output_to_operand_aliasing={{2}: (3, {})} | custom-call | flops 8000000000 | bytes 31250000 | tf_op jit(solution)/shard_map/pallas_call | solution.py:45
  39.6 0.3 shard_map.217
  39.9 1.7 %collective-permute-start.5 = (bf16[512,128]{1,0:T(8,128)(2,1)S(1)}, bf16[512,128]{1,0:T(8,128)(2,1)S(1)}, u32[]{:S(2)}, u32[]{:S(2)}) collective-permute-start(bf16[512,128]{1,0:T(8,128)(2,1)S(1)} %get-tuple-element.102), channel_id=1, source_target_pairs={{0,2},{1,3},{2,0},{3,1},{4,6},{5,7},{6,4},{7,5},{8,10},{9,11},{10,... | collective-permute-start | bytes 393224 | tf_op jit(solution)/shard_map/ppermute | solution.py:516
  41.6 1.8 %collective-permute-start.7 = (bf16[512,128]{1,0:T(8,128)(2,1)S(1)}, bf16[512,128]{1,0:T(8,128)(2,1)S(1)}, u32[]{:S(2)}, u32[]{:S(2)}) collective-permute-start(bf16[512,128]{1,0:T(8,128)(2,1)S(1)} %get-tuple-element.104), channel_id=1, source_target_pairs={{0,6},{1,7},{2,4},{3,5},{4,2},{5,3},{6,0},{7,1},{8,14},{9,15},{10,... | collective-permute-start | bytes 393224 | tf_op jit(solution)/shard_map/ppermute | solution.py:516
  43.5 2.2 %shard_map.218 = (f32[28,8,128]{2,1,0:T(8,128)S(1)}, f32[8,128]{1,0:T(8,128)S(1)}) custom-call(f32[2,22,128,128]{3,2,1,0:T(8,128)S(1)} %get-tuple-element.74.refs_3_.refs_1_.refs_0_, f32[2,22,24,128]{3,2,1,0:T(8,128)S(1)} %get-tuple-element.86.refs_1_, f32[2,22,24,128]{3,2,1,0:T(8,128)S(1)} %get-tuple-element.87.refs_2_, ...), custom_call_target="tpu_custom_call" | custom-call | flops 8000000000 | bytes 31250000 | tf_op jit(solution)/shard_map/pallas_call | solution.py:45
  45.7 3.8 %shard_map.219 = (f32[49,8,128]{2,1,0:T(8,128)S(1)}, f32[8,128]{1,0:T(8,128)S(1)}) custom-call(f32[2,22,128,128]{3,2,1,0:T(8,128)S(1)} %get-tuple-element.74.refs_3_.refs_1_.refs_0_, f32[2,22,24,128]{3,2,1,0:T(8,128)S(1)} %get-tuple-element.86.refs_1_, f32[2,22,24,128]{3,2,1,0:T(8,128)S(1)} %get-tuple-element.87.refs_2_, ...), custom_call_target="tpu_custom_call" | custom-call | flops 8000000000 | bytes 31250000 | tf_op jit(solution)/shard_map/pallas_call | solution.py:45
  49.4 0.6 collective-permute-done.6.refs_3_
  50.1 0.2 shard_map.220
  50.3 0.6 collective-permute-start.9
  50.9 3.8 %collective-permute-start.10 = (bf16[128,128]{1,0:T(8,128)(2,1)S(1)}, bf16[128,128]{1,0:T(8,128)(2,1)S(1)}, u32[]{:S(2)}, u32[]{:S(2)}) collective-permute-start(bf16[128,128]{1,0:T(8,128)(2,1)S(1)} %get-tuple-element.110), channel_id=1, source_target_pairs={{0,24},{1,25},{2,26},{3,27},{4,28},{5,29},{6,30},{7,31},{8,16},{9,... | collective-permute-start | bytes 98312 | tf_op jit(solution)/shard_map/ppermute | solution.py:516
  54.7 3.5 %shard_map.221 = (bf16[8,6,16,256]{3,2,1,0:T(8,128)(2,1)S(1)}, f32[8,128]{1,0:T(8,128)S(1)}) custom-call(s32[1]{0:T(128)S(6)} %copy.32.refs_1_.refs_0_, f32[2,22,24,128]{3,2,1,0:T(8,128)S(1)} %get-tuple-element.111.refs_1_, f32[2,22,24,128]{3,2,1,0:T(8,128)S(1)} %get-tuple-element.112.refs_2_, f32[2,22,128,128]{3,2,1,0:T(8,128)S(1)} %get-tuple-element.93.refs_3_, ...), custom_call_target="tpu_custom_call" | custom-call | tf_op jit(solution)/shard_map/pallas_call | solution.py:45
  58.4 2.3 %collective-permute-start.13 = (bf16[256,128]{1,0:T(8,128)(2,1)S(1)}, bf16[256,128]{1,0:T(8,128)(2,1)S(1)}, u32[]{:S(2)}, u32[]{:S(2)}) collective-permute-start(bf16[256,128]{1,0:T(8,128)(2,1)S(1)} %get-tuple-element.115.refs_1_), channel_id=1, source_target_pairs={{0,24},{1,25},{2,26},{3,27},{4,28},{5,29},{6,30},{7,31},{8,16},{9,... | collective-permute-start | bytes 196616 | tf_op jit(solution)/shard_map/ppermute | solution.py:516
  60.7 2.1 %collective-permute-start.11 = (bf16[256,128]{1,0:T(8,128)(2,1)S(1)}, bf16[256,128]{1,0:T(8,128)(2,1)S(1)}, u32[]{:S(2)}, u32[]{:S(2)}) collective-permute-start(bf16[256,128]{1,0:T(8,128)(2,1)S(1)} %get-tuple-element.115.refs_1_), channel_id=1, source_target_pairs={{0,8},{1,9},{2,10},{3,11},{4,12},{5,13},{6,14},{7,15},{8,0},{9,1},... | collective-permute-start | bytes 196616 | tf_op jit(solution)/shard_map/ppermute | solution.py:516
  62.8 2.7 %shard_map.223 = (bf16[8,10,16,256]{3,2,1,0:T(8,128)(2,1)S(1)}, f32[8,128]{1,0:T(8,128)S(1)}) custom-call(s32[1]{0:T(128)S(6)} %copy.32.refs_1_.refs_0_, f32[2,22,24,128]{3,2,1,0:T(8,128)S(1)} %get-tuple-element.111.refs_1_, f32[2,22,24,128]{3,2,1,0:T(8,128)S(1)} %get-tuple-element.112.refs_2_, f32[2,22,128,128]{3,2,1,0:T(8,128)S(1)} %get-tuple-element.93.refs_3_, ...), custom_call_target="tpu_custom_call" | custom-call | tf_op jit(solution)/shard_map/pallas_call | solution.py:45
  65.5 0.4 collective-permute-done.12.refs_3_
  66.0 1.3 %collective-permute-start.16 = (bf16[640,128]{1,0:T(8,128)(2,1)S(1)}, bf16[640,128]{1,0:T(8,128)(2,1)S(1)}, u32[]{:S(2)}, u32[]{:S(2)}) collective-permute-start(bf16[640,128]{1,0:T(8,128)(2,1)S(1)} %get-tuple-element.119.refs_1_), channel_id=1, source_target_pairs={{0,6},{1,7},{2,4},{3,5},{4,2},{5,3},{6,0},{7,1},{8,14},{9,15},{10,... | collective-permute-start | bytes 491528 | tf_op jit(solution)/shard_map/ppermute | solution.py:516
  67.2 1.3 %collective-permute-start.15 = (bf16[640,128]{1,0:T(8,128)(2,1)S(1)}, bf16[640,128]{1,0:T(8,128)(2,1)S(1)}, u32[]{:S(2)}, u32[]{:S(2)}) collective-permute-start(bf16[640,128]{1,0:T(8,128)(2,1)S(1)} %get-tuple-element.119.refs_1_), channel_id=1, source_target_pairs={{0,4},{1,5},{2,6},{3,7},{4,0},{5,1},{6,2},{7,3},{8,12},{9,13},{10,... | collective-permute-start | bytes 491528 | tf_op jit(solution)/shard_map/ppermute | solution.py:516
  68.5 1.0 %collective-permute-start.14 = (bf16[640,128]{1,0:T(8,128)(2,1)S(1)}, bf16[640,128]{1,0:T(8,128)(2,1)S(1)}, u32[]{:S(2)}, u32[]{:S(2)}) collective-permute-start(bf16[640,128]{1,0:T(8,128)(2,1)S(1)} %get-tuple-element.119.refs_1_), channel_id=1, source_target_pairs={{0,2},{1,3},{2,0},{3,1},{4,6},{5,7},{6,4},{7,5},{8,10},{9,11},{10,... | collective-permute-start | bytes 491528 | tf_op jit(solution)/shard_map/ppermute | solution.py:516
  69.5 4.5 %shard_map.225 = (bf16[8,16,16,256]{3,2,1,0:T(8,128)(2,1)}, f32[8,128]{1,0:T(8,128)S(1)}) custom-call(s32[1]{0:T(128)S(6)} %copy.32.refs_1_.refs_0_, f32[2,22,24,128]{3,2,1,0:T(8,128)S(1)} %get-tuple-element.111.refs_1_, f32[2,22,24,128]{3,2,1,0:T(8,128)S(1)} %get-tuple-element.112.refs_2_, f32[2,22,128,128]{3,2,1,0:T(8,128)S(1)} %get-tuple-element.93.refs_3_, ...), custom_call_target="tpu_custom_call" | custom-call | tf_op jit(solution)/shard_map/pallas_call | solution.py:45
  74.2 1.5 %shard_map.227 = (bf16[8,16,16,256]{3,2,1,0:T(8,128)(2,1)}, f32[8,128]{1,0:T(8,128)S(1)}) custom-call(s32[1]{0:T(128)S(6)} %copy.32.refs_1_.refs_0_, f32[2,16,128,128]{3,2,1,0:T(8,128)S(1)} %get-tuple-element.85.refs_1_, f32[8,128]{1,0:T(8,128)S(1)} %get-tuple-element.123.refs_2_), custom_call_target="tpu_custom_call" | custom-call | tf_op jit(solution)/shard_map/pallas_call | solution.py:45
  75.7 0.4 collective-permute-done.17.refs_2_
  76.2 1.5 %shard_map.228 = (f32[7,7,256]{2,1,0:T(8,128)}, f32[1,256]{1,0:T(1,128)}, f32[1,256]{1,0:T(1,128)}, f32[1,256]{1,0:T(1,128)}, f32[256,1024]{1,0:T(8,128)}, /*ind...) custom-call(s32[1]{0:T(128)} %bitcast.refs_2_.refs_0_, ...), custom_call_target="tpu_custom_call" | custom-call | tf_op jit(solution)/shard_map/pallas_call | solution.py:45
  (24 shorter events, 0.5 us)
Async XLA Ops:
  2.3 15.6 %collective-permute-start = (bf16[384,256]{1,0:T(8,128)(2,1)S(1)}, bf16[384,256]{1,0:T(8,128)(2,1)S(1)}, u32[]{:S(2)}, u32[]{:S(2)}) collective-permute-start(bf16[384,256]{1,0:T(8,128)(2,1)S(1)} %bitcast.28), channel_id=1, source_target_pairs={{28,0},{0,4},{4,8},{8,12},{12,16},{16,20},{20,24},{24,28},{29,1},{... | collective-permute-start | bytes 589832 | tf_op jit(solution)/shard_map/ppermute | solution.py:511
  5.4 12.4 %collective-permute-start.1 = (bf16[384,256]{1,0:T(8,128)(2,1)S(1)}, bf16[384,256]{1,0:T(8,128)(2,1)S(1)}, u32[]{:S(2)}, u32[]{:S(2)}) collective-permute-start(bf16[384,256]{1,0:T(8,128)(2,1)S(1)} %bitcast.29), channel_id=1, source_target_pairs={{4,0},{8,4},{12,8},{16,12},{20,16},{24,20},{28,24},{0,28},{5,1},{9... | collective-permute-start | bytes 589832 | tf_op jit(solution)/shard_map/ppermute | solution.py:511
  25.3 13.3 %collective-permute-start.2 = (bf16[384,256]{1,0:T(8,128)(2,1)S(1)}, bf16[384,256]{1,0:T(8,128)(2,1)S(1)}, u32[]{:S(2)}, u32[]{:S(2)}) collective-permute-start(bf16[384,256]{1,0:T(8,128)(2,1)S(1)} %get-tuple-element.90), channel_id=1, source_target_pairs={{28,0},{0,4},{4,8},{8,12},{12,16},{16,20},{20,24},{24,28},{29,1},{... | collective-permute-start | bytes 589832 | tf_op jit(solution)/shard_map/ppermute | solution.py:511
  25.4 13.2 %collective-permute-start.3 = (bf16[384,256]{1,0:T(8,128)(2,1)S(1)}, bf16[384,256]{1,0:T(8,128)(2,1)S(1)}, u32[]{:S(2)}, u32[]{:S(2)}) collective-permute-start(bf16[384,256]{1,0:T(8,128)(2,1)S(1)} %get-tuple-element.91), channel_id=1, source_target_pairs={{4,0},{8,4},{12,8},{16,12},{20,16},{24,20},{28,24},{0,28},{5,1},{9... | collective-permute-start | bytes 589832 | tf_op jit(solution)/shard_map/ppermute | solution.py:511
  36.9 2.6 %collective-permute-start.4 = (bf16[2048,128]{1,0:T(8,128)(2,1)S(1)}, bf16[2048,128]{1,0:T(8,128)(2,1)S(1)}, u32[]{:S(2)}, u32[]{:S(2)}) collective-permute-start(bf16[2048,128]{1,0:T(8,128)(2,1)S(1)} %get-tuple-element.95), channel_id=1, source_target_pairs={{0,1},{1,0},{2,3},{3,2},{4,5},{5,4},{6,7},{7,6},{8,9},{9,8},{10,11... | collective-permute-start | bytes 1572872 | tf_op jit(solution)/shard_map/ppermute | solution.py:516
  39.9 9.5 %collective-permute-start.5 = (bf16[512,128]{1,0:T(8,128)(2,1)S(1)}, bf16[512,128]{1,0:T(8,128)(2,1)S(1)}, u32[]{:S(2)}, u32[]{:S(2)}) collective-permute-start(bf16[512,128]{1,0:T(8,128)(2,1)S(1)} %get-tuple-element.102), channel_id=1, source_target_pairs={{0,2},{1,3},{2,0},{3,1},{4,6},{5,7},{6,4},{7,5},{8,10},{9,11},{10,... | collective-permute-start | bytes 393224 | tf_op jit(solution)/shard_map/ppermute | solution.py:516
  41.6 8.4 %collective-permute-start.6 = (bf16[512,128]{1,0:T(8,128)(2,1)S(1)}, bf16[512,128]{1,0:T(8,128)(2,1)S(1)}, u32[]{:S(2)}, u32[]{:S(2)}) collective-permute-start(bf16[512,128]{1,0:T(8,128)(2,1)S(1)} %get-tuple-element.103), channel_id=1, source_target_pairs={{0,4},{1,5},{2,6},{3,7},{4,0},{5,1},{6,2},{7,3},{8,12},{9,13},{10,... | collective-permute-start | bytes 393224 | tf_op jit(solution)/shard_map/ppermute | solution.py:516
  41.6 8.4 %collective-permute-start.7 = (bf16[512,128]{1,0:T(8,128)(2,1)S(1)}, bf16[512,128]{1,0:T(8,128)(2,1)S(1)}, u32[]{:S(2)}, u32[]{:S(2)}) collective-permute-start(bf16[512,128]{1,0:T(8,128)(2,1)S(1)} %get-tuple-element.104), channel_id=1, source_target_pairs={{0,6},{1,7},{2,4},{3,5},{4,2},{5,3},{6,0},{7,1},{8,14},{9,15},{10,... | collective-permute-start | bytes 393224 | tf_op jit(solution)/shard_map/ppermute | solution.py:516
  50.2 8.0 %collective-permute-start.8 = (bf16[128,128]{1,0:T(8,128)(2,1)S(1)}, bf16[128,128]{1,0:T(8,128)(2,1)S(1)}, u32[]{:S(2)}, u32[]{:S(2)}) collective-permute-start(bf16[128,128]{1,0:T(8,128)(2,1)S(1)} %get-tuple-element.108), channel_id=1, source_target_pairs={{0,8},{1,9},{2,10},{3,11},{4,12},{5,13},{6,14},{7,15},{8,0},{9,1},... | collective-permute-start | bytes 98312 | tf_op jit(solution)/shard_map/ppermute | solution.py:516
  50.3 7.9 %collective-permute-start.9 = (bf16[128,128]{1,0:T(8,128)(2,1)S(1)}, bf16[128,128]{1,0:T(8,128)(2,1)S(1)}, u32[]{:S(2)}, u32[]{:S(2)}) collective-permute-start(bf16[128,128]{1,0:T(8,128)(2,1)S(1)} %get-tuple-element.109), channel_id=1, source_target_pairs={{0,16},{1,17},{2,18},{3,19},{4,20},{5,21},{6,22},{7,23},{8,24},{9,... | collective-permute-start | bytes 98312 | tf_op jit(solution)/shard_map/ppermute | solution.py:516
  50.9 7.4 %collective-permute-start.10 = (bf16[128,128]{1,0:T(8,128)(2,1)S(1)}, bf16[128,128]{1,0:T(8,128)(2,1)S(1)}, u32[]{:S(2)}, u32[]{:S(2)}) collective-permute-start(bf16[128,128]{1,0:T(8,128)(2,1)S(1)} %get-tuple-element.110), channel_id=1, source_target_pairs={{0,24},{1,25},{2,26},{3,27},{4,28},{5,29},{6,30},{7,31},{8,16},{9,... | collective-permute-start | bytes 98312 | tf_op jit(solution)/shard_map/ppermute | solution.py:516
  58.4 7.1 %collective-permute-start.13 = (bf16[256,128]{1,0:T(8,128)(2,1)S(1)}, bf16[256,128]{1,0:T(8,128)(2,1)S(1)}, u32[]{:S(2)}, u32[]{:S(2)}) collective-permute-start(bf16[256,128]{1,0:T(8,128)(2,1)S(1)} %get-tuple-element.115.refs_1_), channel_id=1, source_target_pairs={{0,24},{1,25},{2,26},{3,27},{4,28},{5,29},{6,30},{7,31},{8,16},{9,... | collective-permute-start | bytes 196616 | tf_op jit(solution)/shard_map/ppermute | solution.py:516
  60.7 5.2 %collective-permute-start.12 = (bf16[256,128]{1,0:T(8,128)(2,1)S(1)}, bf16[256,128]{1,0:T(8,128)(2,1)S(1)}, u32[]{:S(2)}, u32[]{:S(2)}) collective-permute-start(bf16[256,128]{1,0:T(8,128)(2,1)S(1)} %get-tuple-element.115.refs_1_), channel_id=1, source_target_pairs={{0,16},{1,17},{2,18},{3,19},{4,20},{5,21},{6,22},{7,23},{8,24},{9,... | collective-permute-start | bytes 196616 | tf_op jit(solution)/shard_map/ppermute | solution.py:516
  60.7 5.2 %collective-permute-start.11 = (bf16[256,128]{1,0:T(8,128)(2,1)S(1)}, bf16[256,128]{1,0:T(8,128)(2,1)S(1)}, u32[]{:S(2)}, u32[]{:S(2)}) collective-permute-start(bf16[256,128]{1,0:T(8,128)(2,1)S(1)} %get-tuple-element.115.refs_1_), channel_id=1, source_target_pairs={{0,8},{1,9},{2,10},{3,11},{4,12},{5,13},{6,14},{7,15},{8,0},{9,1},... | collective-permute-start | bytes 196616 | tf_op jit(solution)/shard_map/ppermute | solution.py:516
  66.0 8.1 %collective-permute-start.16 = (bf16[640,128]{1,0:T(8,128)(2,1)S(1)}, bf16[640,128]{1,0:T(8,128)(2,1)S(1)}, u32[]{:S(2)}, u32[]{:S(2)}) collective-permute-start(bf16[640,128]{1,0:T(8,128)(2,1)S(1)} %get-tuple-element.119.refs_1_), channel_id=1, source_target_pairs={{0,6},{1,7},{2,4},{3,5},{4,2},{5,3},{6,0},{7,1},{8,14},{9,15},{10,... | collective-permute-start | bytes 491528 | tf_op jit(solution)/shard_map/ppermute | solution.py:516
  67.2 6.9 %collective-permute-start.15 = (bf16[640,128]{1,0:T(8,128)(2,1)S(1)}, bf16[640,128]{1,0:T(8,128)(2,1)S(1)}, u32[]{:S(2)}, u32[]{:S(2)}) collective-permute-start(bf16[640,128]{1,0:T(8,128)(2,1)S(1)} %get-tuple-element.119.refs_1_), channel_id=1, source_target_pairs={{0,4},{1,5},{2,6},{3,7},{4,0},{5,1},{6,2},{7,3},{8,12},{9,13},{10,... | collective-permute-start | bytes 491528 | tf_op jit(solution)/shard_map/ppermute | solution.py:516
  68.5 5.6 %collective-permute-start.14 = (bf16[640,128]{1,0:T(8,128)(2,1)S(1)}, bf16[640,128]{1,0:T(8,128)(2,1)S(1)}, u32[]{:S(2)}, u32[]{:S(2)}) collective-permute-start(bf16[640,128]{1,0:T(8,128)(2,1)S(1)} %get-tuple-element.119.refs_1_), channel_id=1, source_target_pairs={{0,2},{1,3},{2,0},{3,1},{4,6},{5,7},{6,4},{7,5},{8,10},{9,11},{10,... | collective-permute-start | bytes 491528 | tf_op jit(solution)/shard_map/ppermute | solution.py:516
  74.1 2.0 %collective-permute-start.17 = (bf16[2176,128]{1,0:T(8,128)(2,1)S(1)}, bf16[2176,128]{1,0:T(8,128)(2,1)S(1)}, u32[]{:S(2)}, u32[]{:S(2)}) collective-permute-start(bf16[2176,128]{1,0:T(8,128)(2,1)S(1)} %get-tuple-element.126.refs_1_), channel_id=1, source_target_pairs={{0,1},{1,0},{2,3},{3,2},{4,5},{5,4},{6,7},{7,6},{8,9},{9,8},{10,11... | collective-permute-start | bytes 1671176 | tf_op jit(solution)/shard_map/ppermute | solution.py:516
